TPU v7x, 32 devices: a whole 2x2x4 slice. The times are simulated.
32 devices in a mesh: gx: 8 (over y, x, core), gy: 4 (over z).
Axes of the slice: x: 2, y: 2, z: 4, core: 2. Of those that a mesh axis runs over, the one named last changes fastest.
Arguments:
- right_side: float32 [4, 3, 8, 64, 512], P(None, None, None, 'gx', 'gy'), may hold values from -6 to 6
- material: int32 [8, 64, 512], P(None, 'gx', 'gy'), may hold values 0 or 1
Outputs:
- solution: float32 [4, 3, 8, 64, 512], P(None, None, None, 'gx', 'gy')
All inputs are finite; a program needn't handle non-finite values. No bound on the sum of `material` on one device may be relied on, other than what follows from the above.
Results may differ from a plain program's by a relative error of at most 0.00002.
Values sent between devices are 32-bit elements; how exact they have to be, the bound alone decides.
No kernel may reach another device: no remote copies, remote signals or barrier semaphores. Data moves between devices by JAX's collectives and lax.ppermute only.
A program may use at most 64 MiB of HBM per device.

v0:
```python
import jax
import jax.numpy as jnp
from jax import lax
from jax.sharding import PartitionSpec as P

LEVELS = 4
COARSE = 6


relax_weight = 0.6
mass_shift = 0.01
grad_div = 2.5
unit_moves = ((0, 1, 0), (0, 0, 1), (1, 0, 0))


def padded_2(value, sides, width):
    for axis, dim in sides:
        size, length = (lax.axis_size(axis), value.shape[dim])
        up = [(i, (i + 1) % size) for i in range(size - 1)]
        down = [(j, i) for i, j in up]
        last = lax.slice_in_dim(value, length - width, length, axis=dim)
        initial = lax.slice_in_dim(value, 0, width, axis=dim)
        before = lax.ppermute(last, axis, up)
        after = lax.ppermute(initial, axis, down)
        value = jnp.concatenate([before, value, after], axis=dim)
    return value


def offset_view(padded, move):
    depth_z = padded.shape[-3]
    width_x = padded.shape[-2]
    width_y = padded.shape[-1]
    return padded[
        ...,
        1 + move[0] : depth_z - 1 + move[0],
        1 + move[1] : width_x - 1 + move[1],
        1 + move[2] : width_y - 1 + move[2],
    ]


def signed_move(first, first_sign, second, second_sign):
    return tuple((first_sign * first[index] + second_sign * second[index] for index in range(3)))


def diagonal_of(coeff_pad, scale):
    coeff = offset_view(coeff_pad, (0, 0, 0))
    faces = jnp.zeros_like(coeff)
    for direction in range(3):
        for sign in (1, -1):
            move = tuple((sign * entry for entry in unit_moves[direction]))
            faces = faces + 0.5 * (coeff + offset_view(coeff_pad, move))
    return mass_shift + scale * (faces + 2.0 * grad_div * coeff)


def stencil(padded, coeff_pad, scale):
    center = offset_view(padded, (0, 0, 0))
    coeff = offset_view(coeff_pad, (0, 0, 0))
    laplace = jnp.zeros_like(center)
    for direction in range(3):
        for sign in (1, -1):
            move = tuple((sign * entry for entry in unit_moves[direction]))
            face = 0.5 * (coeff + offset_view(coeff_pad, move))
            laplace = laplace + face * (center - offset_view(padded, move))
    pieces = []
    for comp in range(3):
        total = jnp.zeros_like(center[:, 0])
        for other in range(3):
            field = padded[:, other]
            if comp == other:
                step_move = unit_moves[comp]
                back_move = tuple((-entry for entry in step_move))
                total = total + (
                    offset_view(field, step_move)
                    - 2.0 * offset_view(field, (0, 0, 0))
                    + offset_view(field, back_move)
                )
            else:
                first = unit_moves[comp]
                second = unit_moves[other]
                mixed = offset_view(field, signed_move(first, 1, second, 1)) - offset_view(
                    field, signed_move(first, 1, second, -1)
                )
                mixed = (
                    mixed
                    - offset_view(field, signed_move(first, -1, second, 1))
                    + offset_view(field, signed_move(first, -1, second, -1))
                )
                total = total + 0.25 * mixed
        pieces.append(total)
    graddiv = jnp.stack(pieces, axis=1)
    return mass_shift * center + scale * (laplace - grad_div * coeff * graddiv)


def coarsen(array):
    lead = array.shape[:-3]
    depth_z, width_x, width_y = array.shape[-3:]
    grouped = array.reshape(lead + (depth_z // 2, 2, width_x // 2, 2, width_y // 2, 2))
    return jnp.mean(grouped, axis=(-5, -3, -1))


def refine(array):
    return jnp.repeat(jnp.repeat(jnp.repeat(array, 2, axis=-3), 2, axis=-2), 2, axis=-1)


def pad_depth(array):
    widths = [(0, 0)] * (array.ndim - 3) + [(1, 1), (0, 0), (0, 0)]
    return jnp.pad(array, widths)


def rim_field(field):
    return pad_depth(padded_2(field, (("gx", 3), ("gy", 4)), 1))


def rim_coeff(coeff):
    return pad_depth(padded_2(coeff, (("gx", 1), ("gy", 2)), 1))


def relax_once(current, source, coeff_pad, diagonal, scale):
    image = stencil(rim_field(current), coeff_pad, scale)
    return current + relax_weight * (source - image) / diagonal


def cycle(source, coeff, level):
    scale = 0.25**level
    if level == LEVELS - 1:
        coeff_pad = rim_coeff(coeff)
        diagonal = diagonal_of(coeff_pad, scale)
        current = relax_weight * source / diagonal
        for sweep in range(COARSE - 1):
            current = relax_once(current, source, coeff_pad, diagonal, scale)
        return current
    coeff_pad = rim_coeff(coeff)
    diagonal = diagonal_of(coeff_pad, scale)
    current = relax_weight * source / diagonal
    current = relax_once(current, source, coeff_pad, diagonal, scale)
    remainder = source - stencil(rim_field(current), coeff_pad, scale)
    correction = cycle(coarsen(remainder), coarsen(coeff), level + 1)
    current = current + refine(correction)
    current = relax_once(current, source, coeff_pad, diagonal, scale)
    return relax_once(current, source, coeff_pad, diagonal, scale)


def per_device(right_side, material):
    coeff = jnp.where(material == 1, 1.0, 0.05).astype(jnp.float32)
    return cycle(right_side, coeff, 0)


def solution(mesh):
    in_specs = (P(None, None, None, "gx", "gy"), P(None, "gx", "gy"))
    out_specs = P(None, None, None, "gx", "gy")
    return jax.shard_map(
        per_device, mesh=mesh, in_specs=in_specs, out_specs=out_specs, check_vma=False
    )
```

profile of v0, /device:TPU:27, one launch (start us, length us, event | category | flops | bytes accessed | tf_op | source)
XLA Modules:
  0.0 420.9 jit_solution(4083331329022595380)
XLA Ops:
  3.4 3.9 collective-permute-start.1
  12.0 4.5 %collective-permute-start.25 = (f32[2,1,32]{2,1,0:T(1,128)S(1)}, f32[2,1,32]{2,1,0:T(1,128)S(1)}, u32[]{:S(2)}, u32[]{:S(2)}) collective-permute-start(f32[2,1,32]{2,1,0:T(1,128)S(1)} %get-tuple-element.205), channel_id=1, source_target_pairs={{0,4},{4,8},{8,12},{12,16},{16,20},{20,24},{24,28},{1,5},{5,9},{9,... | collective-permute-start | bytes 776 | tf_op jit(solution)/shard_map/ppermute | solution.py:23
  18.5 4.5 %collective-permute-start.13 = (f32[4,1,64]{2,1,0:T(1,128)S(1)}, f32[4,1,64]{2,1,0:T(1,128)S(1)}, u32[]{:S(2)}, u32[]{:S(2)}) collective-permute-start(f32[4,1,64]{2,1,0:T(1,128)S(1)} %get-tuple-element.187), channel_id=1, source_target_pairs={{0,4},{4,8},{8,12},{12,16},{16,20},{20,24},{24,28},{1,5},{5,9},{9,... | collective-permute-start | bytes 3080 | tf_op jit(solution)/shard_map/ppermute | solution.py:23
  27.2 4.6 %collective-permute-start.26 = (f32[2,4,1]{2,1,0:T(4,128)}, f32[2,4,1]{2,1,0:T(4,128)}, u32[]{:S(2)}, u32[]{:S(2)}) collective-permute-start(f32[2,4,1]{2,1,0:T(4,128)} %get-tuple-element.190), channel_id=1, source_target_pairs={{1,0},{2,1},{3,2},{5,4},{6,5},{7,6},{9,8},{10,9},{11,10},{13,12},{... | collective-permute-start | bytes 104 | tf_op jit(solution)/shard_map/ppermute | solution.py:24
  38.5 4.3 %collective-permute-done.4 = f32[4,3,8,1,128]{4,2,3,1,0:T(8,128)S(1)} collective-permute-done((f32[4,3,8,1,128]{4,2,3,1,0:T(8,128)S(1)}, f32[4,3,8,1,128]{4,2,3,1,0:T(8,128)S(1)}, u32[]{:S(2)}, u32[]{:S(2)}) %collective-permute-start.4) | collective-permute-done | bytes 49184 | tf_op jit(solution)/shard_map/ppermute | solution.py:24
  43.0 4.3 %collective-permute-start.6 = (f32[4,3,8,10,1]{4,2,3,1,0:T(8,128)S(1)}, f32[4,3,8,10,1]{4,2,3,1,0:T(8,128)S(1)}, u32[]{:S(2)}, u32[]{:S(2)}) collective-permute-start(f32[4,3,8,10,1]{4,2,3,1,0:T(8,128)S(1)} %get-tuple-element.55), channel_id=1, source_target_pairs={{1,0},{2,1},{3,2},{5,4},{6,5},{7,6},{9,8},{10,9},{11,10},{13,12},{... | collective-permute-start | bytes 11528 | tf_op jit(solution)/shard_map/ppermute | solution.py:24
  48.6 4.0 collective-permute-start.14
  67.9 4.3 %collective-permute-done.8 = f32[4,3,8,1,128]{4,2,3,1,0:T(8,128)S(1)} collective-permute-done((f32[4,3,8,1,128]{4,2,3,1,0:T(8,128)S(1)}, f32[4,3,8,1,128]{4,2,3,1,0:T(8,128)S(1)}, u32[]{:S(2)}, u32[]{:S(2)}) %collective-permute-start.8) | collective-permute-done | bytes 49184 | tf_op jit(solution)/shard_map/ppermute | solution.py:24
  76.5 6.2 %collective-permute-done.10 = f32[4,3,8,10,1]{4,2,3,1,0:T(8,128)S(1)} collective-permute-done((f32[4,3,8,10,1]{4,2,3,1,0:T(8,128)S(1)}, f32[4,3,8,10,1]{4,2,3,1,0:T(8,128)S(1)}, u32[]{:S(2)}, u32[]{:S(2)}) %collective-permute-start.10) | collective-permute-done | bytes 3872 | tf_op jit(solution)/shard_map/ppermute | solution.py:24
  82.7 4.1 collective-permute-done.11
  90.2 6.8 %copy.1445 = f32[4,3,8,8,128]{0,4,3,2,1:T(8,128)} copy(f32[4,3,8,8,128]{4,3,2,1,0:T(8,128)S(1)} %fusion.68) | data formatting | bytes 786432 | tf_op jit(solution)/shard_map/sub | solution.py:136
  96.9 12.3 %reduce_sum.68 = f32[4,3,4,4,64]{0,4,3,2,1:T(8,128)S(1)} reduce(f32[4,3,4,2,4,2,64,2]{0,7,6,5,4,3,2,1:T(2,128)} %bitcast.324, f32[]{:T(128)} %constant.23.clone.1), dimensions={3,5,7}, to_apply=%region_0.1 | reduce | flops 86016 | bytes 442372 | tf_op jit(solution)/shard_map/reduce_sum | solution.py:98
  115.1 3.6 collective-permute-done.16
  135.1 4.5 %collective-permute-start.37 = (f32[1,1,16]{2,1,0:T(1,128)S(1)}, f32[1,1,16]{2,1,0:T(1,128)S(1)}, u32[]{:S(2)}, u32[]{:S(2)}) collective-permute-start(f32[1,1,16]{2,1,0:T(1,128)S(1)} %get-tuple-element.213), channel_id=1, source_target_pairs={{0,4},{4,8},{8,12},{12,16},{16,20},{20,24},{24,28},{1,5},{5,9},{9,... | collective-permute-start | bytes 200 | tf_op jit(solution)/shard_map/ppermute | solution.py:23
  141.7 4.0 collective-permute-done.20
  149.9 3.8 collective-permute-done.23
  158.8 4.5 %collective-permute-start.29 = (f32[4,3,2,1,32]{4,0,3,2,1:T(4,128)S(1)}, f32[4,3,2,1,32]{4,0,3,2,1:T(4,128)S(1)}, u32[]{:S(2)}, u32[]{:S(2)}) collective-permute-start(f32[4,3,2,1,32]{4,0,3,2,1:T(4,128)S(1)} %get-tuple-element.170), channel_id=1, source_target_pairs={{0,4},{4,8},{8,12},{12,16},{16,20},{20,24},{24,28},{1,5},{5,9},{9,... | collective-permute-start | bytes 9224 | tf_op jit(solution)/shard_map/ppermute | solution.py:23
  168.9 4.6 %collective-permute-start.38 = (f32[1,3,1]{2,1,0:T(4,128)S(1)}, f32[1,3,1]{2,1,0:T(4,128)S(1)}, u32[]{:S(2)}, u32[]{:S(2)}) collective-permute-start(f32[1,3,1]{2,1,0:T(4,128)S(1)} %get-tuple-element.195), channel_id=1, source_target_pairs={{1,0},{2,1},{3,2},{5,4},{6,5},{7,6},{9,8},{10,9},{11,10},{13,12},{... | collective-permute-start | bytes 44 | tf_op jit(solution)/shard_map/ppermute | solution.py:24
  176.4 5.9 %collective-permute-start.33 = (f32[4,3,2,1,32]{4,0,3,2,1:T(4,128)S(1)}, f32[4,3,2,1,32]{4,0,3,2,1:T(4,128)S(1)}, u32[]{:S(2)}, u32[]{:S(2)}) collective-permute-start(f32[4,3,2,1,32]{4,0,3,2,1:T(4,128)S(1)} %get-tuple-element.168), channel_id=1, source_target_pairs={{0,4},{4,8},{8,12},{12,16},{16,20},{20,24},{24,28},{1,5},{5,9},{9,... | collective-permute-start | bytes 9224 | tf_op jit(solution)/shard_map/ppermute | solution.py:23
  183.3 3.6 collective-permute-start.34
  194.9 6.5 %collective-permute-start.41 = (f32[4,3,1,1,16]{4,0,3,2,1:T(4,128)S(1)}, f32[4,3,1,1,16]{4,0,3,2,1:T(4,128)S(1)}, u32[]{:S(2)}, u32[]{:S(2)}) collective-permute-start(f32[4,3,1,1,16]{4,0,3,2,1:T(4,128)S(1)} %bitcast_divide_fusion), channel_id=1, source_target_pairs={{0,4},{4,8},{8,12},{12,16},{16,20},{20,24},{24,28},{1,5},{5,9},{9,... | collective-permute-start | bytes 2312 | tf_op jit(solution)/shard_map/ppermute | solution.py:23
  203.6 4.0 collective-permute-start.42
  210.8 6.2 %collective-permute-start.45 = (f32[4,3,1,1,16]{4,0,3,2,1:T(4,128)S(1)}, f32[4,3,1,1,16]{4,0,3,2,1:T(4,128)S(1)}, u32[]{:S(2)}, u32[]{:S(2)}) collective-permute-start(f32[4,3,1,1,16]{4,0,3,2,1:T(4,128)S(1)} %divide_add_fusion.9), channel_id=1, source_target_pairs={{0,4},{4,8},{8,12},{12,16},{16,20},{20,24},{24,28},{1,5},{5,9},{9,... | collective-permute-start | bytes 2312 | tf_op jit(solution)/shard_map/ppermute | solution.py:23
  219.2 4.6 %collective-permute-start.46 = (f32[4,3,1,3,1]{4,0,3,2,1:T(4,128)S(1)}, f32[4,3,1,3,1]{4,0,3,2,1:T(4,128)S(1)}, u32[]{:S(2)}, u32[]{:S(2)}) collective-permute-start(f32[4,3,1,3,1]{4,0,3,2,1:T(4,128)S(1)} %get-tuple-element.178), channel_id=1, source_target_pairs={{1,0},{2,1},{3,2},{5,4},{6,5},{7,6},{9,8},{10,9},{11,10},{13,12},{... | collective-permute-start | bytes 440 | tf_op jit(solution)/shard_map/ppermute | solution.py:24
  227.0 5.9 %collective-permute-start.49 = (f32[4,3,1,1,16]{4,0,3,2,1:T(4,128)S(1)}, f32[4,3,1,1,16]{4,0,3,2,1:T(4,128)S(1)}, u32[]{:S(2)}, u32[]{:S(2)}) collective-permute-start(f32[4,3,1,1,16]{4,0,3,2,1:T(4,128)S(1)} %divide_add_fusion.8), channel_id=1, source_target_pairs={{0,4},{4,8},{8,12},{12,16},{16,20},{20,24},{24,28},{1,5},{5,9},{9,... | collective-permute-start | bytes 2312 | tf_op jit(solution)/shard_map/ppermute | solution.py:23
  235.1 4.6 %collective-permute-start.50 = (f32[4,3,1,3,1]{4,0,3,2,1:T(4,128)S(1)}, f32[4,3,1,3,1]{4,0,3,2,1:T(4,128)S(1)}, u32[]{:S(2)}, u32[]{:S(2)}) collective-permute-start(f32[4,3,1,3,1]{4,0,3,2,1:T(4,128)S(1)} %get-tuple-element.176), channel_id=1, source_target_pairs={{1,0},{2,1},{3,2},{5,4},{6,5},{7,6},{9,8},{10,9},{11,10},{13,12},{... | collective-permute-start | bytes 440 | tf_op jit(solution)/shard_map/ppermute | solution.py:24
  242.9 5.9 %collective-permute-start.53 = (f32[4,3,1,1,16]{4,0,3,2,1:T(4,128)S(1)}, f32[4,3,1,1,16]{4,0,3,2,1:T(4,128)S(1)}, u32[]{:S(2)}, u32[]{:S(2)}) collective-permute-start(f32[4,3,1,1,16]{4,0,3,2,1:T(4,128)S(1)} %divide_add_fusion.7), channel_id=1, source_target_pairs={{0,4},{4,8},{8,12},{12,16},{16,20},{20,24},{24,28},{1,5},{5,9},{9,... | collective-permute-start | bytes 2312 | tf_op jit(solution)/shard_map/ppermute | solution.py:23
  251.0 4.6 %collective-permute-start.54 = (f32[4,3,1,3,1]{4,0,3,2,1:T(4,128)S(1)}, f32[4,3,1,3,1]{4,0,3,2,1:T(4,128)S(1)}, u32[]{:S(2)}, u32[]{:S(2)}) collective-permute-start(f32[4,3,1,3,1]{4,0,3,2,1:T(4,128)S(1)} %get-tuple-element.174), channel_id=1, source_target_pairs={{1,0},{2,1},{3,2},{5,4},{6,5},{7,6},{9,8},{10,9},{11,10},{13,12},{... | collective-permute-start | bytes 440 | tf_op jit(solution)/shard_map/ppermute | solution.py:24
  258.8 5.9 %collective-permute-start.57 = (f32[4,3,1,1,16]{4,0,3,2,1:T(4,128)S(1)}, f32[4,3,1,1,16]{4,0,3,2,1:T(4,128)S(1)}, u32[]{:S(2)}, u32[]{:S(2)}) collective-permute-start(f32[4,3,1,1,16]{4,0,3,2,1:T(4,128)S(1)} %divide_add_fusion.6), channel_id=1, source_target_pairs={{0,4},{4,8},{8,12},{12,16},{16,20},{20,24},{24,28},{1,5},{5,9},{9,... | collective-permute-start | bytes 2312 | tf_op jit(solution)/shard_map/ppermute | solution.py:23
  265.6 3.9 collective-permute-start.58
  276.9 6.2 %collective-permute-start.61 = (f32[4,3,2,1,32]{4,0,3,2,1:T(4,128)S(1)}, f32[4,3,2,1,32]{4,0,3,2,1:T(4,128)S(1)}, u32[]{:S(2)}, u32[]{:S(2)}) collective-permute-start(f32[4,3,2,1,32]{4,0,3,2,1:T(4,128)S(1)} %get-tuple-element.166), channel_id=1, source_target_pairs={{0,4},{4,8},{8,12},{12,16},{16,20},{20,24},{24,28},{1,5},{5,9},{9,... | collective-permute-start | bytes 9224 | tf_op jit(solution)/shard_map/ppermute | solution.py:23
  284.1 3.6 collective-permute-start.62
  289.1 3.8 collective-permute-done.63
  295.7 6.2 %collective-permute-start.65 = (f32[4,3,2,1,32]{4,0,3,2,1:T(4,128)S(1)}, f32[4,3,2,1,32]{4,0,3,2,1:T(4,128)S(1)}, u32[]{:S(2)}, u32[]{:S(2)}) collective-permute-start(f32[4,3,2,1,32]{4,0,3,2,1:T(4,128)S(1)} %get-tuple-element.164), channel_id=1, source_target_pairs={{0,4},{4,8},{8,12},{12,16},{16,20},{20,24},{24,28},{1,5},{5,9},{9,... | collective-permute-start | bytes 9224 | tf_op jit(solution)/shard_map/ppermute | solution.py:23
  302.9 3.6 collective-permute-start.66
  307.9 3.5 collective-permute-done.67
  314.0 6.5 %collective-permute-start.69 = (f32[4,3,4,1,64]{4,2,3,1,0:T(4,128)S(1)}, f32[4,3,4,1,64]{4,2,3,1,0:T(4,128)S(1)}, u32[]{:S(2)}, u32[]{:S(2)}) collective-permute-start(f32[4,3,4,1,64]{4,2,3,1,0:T(4,128)S(1)} %bitcast.356), channel_id=1, source_target_pairs={{0,4},{4,8},{8,12},{12,16},{16,20},{20,24},{24,28},{1,5},{5,9},{9,... | collective-permute-start | bytes 36872 | tf_op jit(solution)/shard_map/ppermute | solution.py:23
  322.5 4.0 collective-permute-done.68
  330.6 3.8 collective-permute-done.71
  341.4 4.0 collective-permute-done.72
  349.3 3.8 collective-permute-done.75
  360.7 4.3 %copy.1576 = f32[4,3,8,8,128]{4,3,2,1,0:T(8,128)S(1)} copy(f32[4,3,8,8,128]{3,2,4,1,0:T(8,128)} %bitcast.325) | data formatting | bytes 786432 | tf_op jit(solution)/shard_map/reshape | solution.py:102
  370.8 4.0 collective-permute-done.76
  378.0 7.0 %collective-permute-done.78 = f32[4,3,8,10,1]{4,2,3,1,0:T(8,128)S(1)} collective-permute-done((f32[4,3,8,10,1]{4,2,3,1,0:T(8,128)S(1)}, f32[4,3,8,10,1]{4,2,3,1,0:T(8,128)S(1)}, u32[]{:S(2)}, u32[]{:S(2)}) %collective-permute-start.78) | collective-permute-done | bytes 3872 | tf_op jit(solution)/shard_map/ppermute | solution.py:24
  385.0 4.1 collective-permute-done.79
  397.3 3.8 collective-permute-done.80
  404.3 8.0 %collective-permute-done.82 = f32[4,3,8,10,1]{4,2,3,1,0:T(8,128)S(1)} collective-permute-done((f32[4,3,8,10,1]{4,2,3,1,0:T(8,128)S(1)}, f32[4,3,8,10,1]{4,2,3,1,0:T(8,128)S(1)}, u32[]{:S(2)}, u32[]{:S(2)}) %collective-permute-start.82) | collective-permute-done | bytes 3872 | tf_op jit(solution)/shard_map/ppermute | solution.py:24
  412.3 4.1 collective-permute-done.83
  (472 shorter events, 182.3 us)
Async XLA Ops:
  0.8 22.3 %collective-permute-start = (f32[8,1,128]{2,1,0:T(1,128)S(1)}, f32[8,1,128]{2,1,0:T(1,128)S(1)}, u32[]{:S(2)}, u32[]{:S(2)}) collective-permute-start(f32[8,1,128]{2,1,0:T(1,128)S(1)} %get-tuple-element.163), channel_id=1, source_target_pairs={{4,0},{8,4},{12,8},{16,12},{20,16},{24,20},{28,24},{5,1},{9,5},{13... | collective-permute-start | bytes 12296 | tf_op jit(solution)/shard_map/ppermute | solution.py:24
  3.4 19.7 %collective-permute-start.1 = (f32[8,1,128]{2,1,0:T(1,128)S(1)}, f32[8,1,128]{2,1,0:T(1,128)S(1)}, u32[]{:S(2)}, u32[]{:S(2)}) collective-permute-start(f32[8,1,128]{2,1,0:T(1,128)S(1)} %get-tuple-element.162), channel_id=1, source_target_pairs={{0,4},{4,8},{8,12},{12,16},{16,20},{20,24},{24,28},{1,5},{5,9},{9,... | collective-permute-start | bytes 12296 | tf_op jit(solution)/shard_map/ppermute | solution.py:23
  10.0 8.4 %collective-permute-start.24 = (f32[2,1,32]{2,1,0:T(1,128)S(1)}, f32[2,1,32]{2,1,0:T(1,128)S(1)}, u32[]{:S(2)}, u32[]{:S(2)}) collective-permute-start(f32[2,1,32]{2,1,0:T(1,128)S(1)} %get-tuple-element.206), channel_id=1, source_target_pairs={{4,0},{8,4},{12,8},{16,12},{20,16},{24,20},{28,24},{5,1},{9,5},{13... | collective-permute-start | bytes 776 | tf_op jit(solution)/shard_map/ppermute | solution.py:24
  12.0 11.1 %collective-permute-start.25 = (f32[2,1,32]{2,1,0:T(1,128)S(1)}, f32[2,1,32]{2,1,0:T(1,128)S(1)}, u32[]{:S(2)}, u32[]{:S(2)}) collective-permute-start(f32[2,1,32]{2,1,0:T(1,128)S(1)} %get-tuple-element.205), channel_id=1, source_target_pairs={{0,4},{4,8},{8,12},{12,16},{16,20},{20,24},{24,28},{1,5},{5,9},{9,... | collective-permute-start | bytes 776 | tf_op jit(solution)/shard_map/ppermute | solution.py:23
  16.5 19.9 %collective-permute-start.12 = (f32[4,1,64]{2,1,0:T(1,128)S(1)}, f32[4,1,64]{2,1,0:T(1,128)S(1)}, u32[]{:S(2)}, u32[]{:S(2)}) collective-permute-start(f32[4,1,64]{2,1,0:T(1,128)S(1)} %get-tuple-element.188), channel_id=1, source_target_pairs={{4,0},{8,4},{12,8},{16,12},{20,16},{24,20},{28,24},{5,1},{9,5},{13... | collective-permute-start | bytes 3080 | tf_op jit(solution)/shard_map/ppermute | solution.py:24
  18.5 17.9 %collective-permute-start.13 = (f32[4,1,64]{2,1,0:T(1,128)S(1)}, f32[4,1,64]{2,1,0:T(1,128)S(1)}, u32[]{:S(2)}, u32[]{:S(2)}) collective-permute-start(f32[4,1,64]{2,1,0:T(1,128)S(1)} %get-tuple-element.187), channel_id=1, source_target_pairs={{0,4},{4,8},{8,12},{12,16},{16,20},{20,24},{24,28},{1,5},{5,9},{9,... | collective-permute-start | bytes 3080 | tf_op jit(solution)/shard_map/ppermute | solution.py:23
  23.2 8.6 %collective-permute-start.2 = (f32[8,10,1]{2,1,0:T(8,128)S(1)}, f32[8,10,1]{2,1,0:T(8,128)S(1)}, u32[]{:S(2)}, u32[]{:S(2)}) collective-permute-start(f32[8,10,1]{2,1,0:T(8,128)S(1)} %get-tuple-element.116), channel_id=1, source_target_pairs={{1,0},{2,1},{3,2},{5,4},{6,5},{7,6},{9,8},{10,9},{11,10},{13,12},{... | collective-permute-start | bytes 968 | tf_op jit(solution)/shard_map/ppermute | solution.py:24
  25.3 7.8 %collective-permute-start.3 = (f32[8,10,1]{2,1,0:T(8,128)S(1)}, f32[8,10,1]{2,1,0:T(8,128)S(1)}, u32[]{:S(2)}, u32[]{:S(2)}) collective-permute-start(f32[8,10,1]{2,1,0:T(8,128)S(1)} %get-tuple-element.115), channel_id=1, source_target_pairs={{0,1},{1,2},{2,3},{4,5},{5,6},{6,7},{8,9},{9,10},{10,11},{12,13},{... | collective-permute-start | bytes 968 | tf_op jit(solution)/shard_map/ppermute | solution.py:23
  27.2 84.5 %collective-permute-start.26 = (f32[2,4,1]{2,1,0:T(4,128)}, f32[2,4,1]{2,1,0:T(4,128)}, u32[]{:S(2)}, u32[]{:S(2)}) collective-permute-start(f32[2,4,1]{2,1,0:T(4,128)} %get-tuple-element.190), channel_id=1, source_target_pairs={{1,0},{2,1},{3,2},{5,4},{6,5},{7,6},{9,8},{10,9},{11,10},{13,12},{... | collective-permute-start | bytes 104 | tf_op jit(solution)/shard_map/ppermute | solution.py:24
  31.8 80.0 %collective-permute-start.27 = (f32[2,4,1]{2,1,0:T(4,128)}, f32[2,4,1]{2,1,0:T(4,128)}, u32[]{:S(2)}, u32[]{:S(2)}) collective-permute-start(f32[2,4,1]{2,1,0:T(4,128)} %get-tuple-element.189), channel_id=1, source_target_pairs={{0,1},{1,2},{2,3},{4,5},{5,6},{6,7},{8,9},{9,10},{10,11},{12,13},{... | collective-permute-start | bytes 104 | tf_op jit(solution)/shard_map/ppermute | solution.py:23
  36.4 6.3 %collective-permute-start.4 = (f32[4,3,8,1,128]{4,2,3,1,0:T(8,128)S(1)}, f32[4,3,8,1,128]{4,2,3,1,0:T(8,128)S(1)}, u32[]{:S(2)}, u32[]{:S(2)}) collective-permute-start(f32[4,3,8,1,128]{4,2,3,1,0:T(8,128)S(1)} %bitcast.342), channel_id=1, source_target_pairs={{4,0},{8,4},{12,8},{16,12},{20,16},{24,20},{28,24},{5,1},{9,5},{13... | collective-permute-start | bytes 147464 | tf_op jit(solution)/shard_map/ppermute | solution.py:24
  43.0 12.9 %collective-permute-start.6 = (f32[4,3,8,10,1]{4,2,3,1,0:T(8,128)S(1)}, f32[4,3,8,10,1]{4,2,3,1,0:T(8,128)S(1)}, u32[]{:S(2)}, u32[]{:S(2)}) collective-permute-start(f32[4,3,8,10,1]{4,2,3,1,0:T(8,128)S(1)} %get-tuple-element.55), channel_id=1, source_target_pairs={{1,0},{2,1},{3,2},{5,4},{6,5},{7,6},{9,8},{10,9},{11,10},{13,12},{... | collective-permute-start | bytes 11528 | tf_op jit(solution)/shard_map/ppermute | solution.py:24
  47.3 12.7 %collective-permute-start.7 = (f32[4,3,8,10,1]{4,2,3,1,0:T(8,128)S(1)}, f32[4,3,8,10,1]{4,2,3,1,0:T(8,128)S(1)}, u32[]{:S(2)}, u32[]{:S(2)}) collective-permute-start(f32[4,3,8,10,1]{4,2,3,1,0:T(8,128)S(1)} %get-tuple-element.54), channel_id=1, source_target_pairs={{0,1},{1,2},{2,3},{4,5},{5,6},{6,7},{8,9},{9,10},{10,11},{12,13},{... | collective-permute-start | bytes 11528 | tf_op jit(solution)/shard_map/ppermute | solution.py:23
  48.6 17.1 %collective-permute-start.14 = (f32[4,6,1]{2,1,0:T(8,128)S(1)}, f32[4,6,1]{2,1,0:T(8,128)S(1)}, u32[]{:S(2)}, u32[]{:S(2)}) collective-permute-start(f32[4,6,1]{2,1,0:T(8,128)S(1)} %get-tuple-element.183), channel_id=1, source_target_pairs={{1,0},{2,1},{3,2},{5,4},{6,5},{7,6},{9,8},{10,9},{11,10},{13,12},{... | collective-permute-start | bytes 296 | tf_op jit(solution)/shard_map/ppermute | solution.py:24
  55.8 9.9 %collective-permute-start.15 = (f32[4,6,1]{2,1,0:T(8,128)S(1)}, f32[4,6,1]{2,1,0:T(8,128)S(1)}, u32[]{:S(2)}, u32[]{:S(2)}) collective-permute-start(f32[4,6,1]{2,1,0:T(8,128)S(1)} %get-tuple-element.182), channel_id=1, source_target_pairs={{0,1},{1,2},{2,3},{4,5},{5,6},{6,7},{8,9},{9,10},{10,11},{12,13},{... | collective-permute-start | bytes 296 | tf_op jit(solution)/shard_map/ppermute | solution.py:23
  72.4 10.3 %collective-permute-start.10 = (f32[4,3,8,10,1]{4,2,3,1,0:T(8,128)S(1)}, f32[4,3,8,10,1]{4,2,3,1,0:T(8,128)S(1)}, u32[]{:S(2)}, u32[]{:S(2)}) collective-permute-start(f32[4,3,8,10,1]{4,2,3,1,0:T(8,128)S(1)} %get-tuple-element.51), channel_id=1, source_target_pairs={{1,0},{2,1},{3,2},{5,4},{6,5},{7,6},{9,8},{10,9},{11,10},{13,12},{... | collective-permute-start | bytes 11528 | tf_op jit(solution)/shard_map/ppermute | solution.py:24
  74.3 12.5 %collective-permute-start.11 = (f32[4,3,8,10,1]{4,2,3,1,0:T(8,128)S(1)}, f32[4,3,8,10,1]{4,2,3,1,0:T(8,128)S(1)}, u32[]{:S(2)}, u32[]{:S(2)}) collective-permute-start(f32[4,3,8,10,1]{4,2,3,1,0:T(8,128)S(1)} %get-tuple-element.50), channel_id=1, source_target_pairs={{0,1},{1,2},{2,3},{4,5},{5,6},{6,7},{8,9},{9,10},{10,11},{12,13},{... | collective-permute-start | bytes 11528 | tf_op jit(solution)/shard_map/ppermute | solution.py:23
  130.0 11.6 %collective-permute-start.21 = (f32[4,3,4,1,64]{4,2,3,1,0:T(4,128)S(1)}, f32[4,3,4,1,64]{4,2,3,1,0:T(4,128)S(1)}, u32[]{:S(2)}, u32[]{:S(2)}) collective-permute-start(f32[4,3,4,1,64]{4,2,3,1,0:T(4,128)S(1)} %bitcast.352), channel_id=1, source_target_pairs={{0,4},{4,8},{8,12},{12,16},{16,20},{20,24},{24,28},{1,5},{5,9},{9,... | collective-permute-start | bytes 36872 | tf_op jit(solution)/shard_map/ppermute | solution.py:23
  133.2 30.2 %collective-permute-start.36 = (f32[1,1,16]{2,1,0:T(1,128)S(1)}, f32[1,1,16]{2,1,0:T(1,128)S(1)}, u32[]{:S(2)}, u32[]{:S(2)}) collective-permute-start(f32[1,1,16]{2,1,0:T(1,128)S(1)} %get-tuple-element.213), channel_id=1, source_target_pairs={{4,0},{8,4},{12,8},{16,12},{20,16},{24,20},{28,24},{5,1},{9,5},{13... | collective-permute-start | bytes 200 | tf_op jit(solution)/shard_map/ppermute | solution.py:24
  135.1 28.2 %collective-permute-start.37 = (f32[1,1,16]{2,1,0:T(1,128)S(1)}, f32[1,1,16]{2,1,0:T(1,128)S(1)}, u32[]{:S(2)}, u32[]{:S(2)}) collective-permute-start(f32[1,1,16]{2,1,0:T(1,128)S(1)} %get-tuple-element.213), channel_id=1, source_target_pairs={{0,4},{4,8},{8,12},{12,16},{16,20},{20,24},{24,28},{1,5},{5,9},{9,... | collective-permute-start | bytes 200 | tf_op jit(solution)/shard_map/ppermute | solution.py:23
  156.9 6.5 %collective-permute-start.28 = (f32[4,3,2,1,32]{4,0,3,2,1:T(4,128)S(1)}, f32[4,3,2,1,32]{4,0,3,2,1:T(4,128)S(1)}, u32[]{:S(2)}, u32[]{:S(2)}) collective-permute-start(f32[4,3,2,1,32]{4,0,3,2,1:T(4,128)S(1)} %get-tuple-element.171), channel_id=1, source_target_pairs={{4,0},{8,4},{12,8},{16,12},{20,16},{24,20},{28,24},{5,1},{9,5},{13... | collective-permute-start | bytes 9224 | tf_op jit(solution)/shard_map/ppermute | solution.py:24
  164.3 9.2 %collective-permute-start.30 = (f32[4,3,2,4,1]{4,3,2,1,0:T(4,128)S(1)}, f32[4,3,2,4,1]{4,3,2,1,0:T(4,128)S(1)}, u32[]{:S(2)}, u32[]{:S(2)}) collective-permute-start(f32[4,3,2,4,1]{4,3,2,1,0:T(4,128)S(1)} %get-tuple-element.159), channel_id=1, source_target_pairs={{1,0},{2,1},{3,2},{5,4},{6,5},{7,6},{9,8},{10,9},{11,10},{13,12},{... | collective-permute-start | bytes 1160 | tf_op jit(solution)/shard_map/ppermute | solution.py:24
  166.3 7.3 %collective-permute-start.31 = (f32[4,3,2,4,1]{4,3,2,1,0:T(4,128)S(1)}, f32[4,3,2,4,1]{4,3,2,1,0:T(4,128)S(1)}, u32[]{:S(2)}, u32[]{:S(2)}) collective-permute-start(f32[4,3,2,4,1]{4,3,2,1,0:T(4,128)S(1)} %get-tuple-element.158), channel_id=1, source_target_pairs={{0,1},{1,2},{2,3},{4,5},{5,6},{6,7},{8,9},{9,10},{10,11},{12,13},{... | collective-permute-start | bytes 1160 | tf_op jit(solution)/shard_map/ppermute | solution.py:23
  167.6 14.7 %collective-permute-start.39 = (f32[1,3,1]{2,1,0:T(4,128)S(1)}, f32[1,3,1]{2,1,0:T(4,128)S(1)}, u32[]{:S(2)}, u32[]{:S(2)}) collective-permute-start(f32[1,3,1]{2,1,0:T(4,128)S(1)} %get-tuple-element.194), channel_id=1, source_target_pairs={{0,1},{1,2},{2,3},{4,5},{5,6},{6,7},{8,9},{9,10},{10,11},{12,13},{... | collective-permute-start | bytes 44 | tf_op jit(solution)/shard_map/ppermute | solution.py:23
  168.9 13.4 %collective-permute-start.38 = (f32[1,3,1]{2,1,0:T(4,128)S(1)}, f32[1,3,1]{2,1,0:T(4,128)S(1)}, u32[]{:S(2)}, u32[]{:S(2)}) collective-permute-start(f32[1,3,1]{2,1,0:T(4,128)S(1)} %get-tuple-element.195), channel_id=1, source_target_pairs={{1,0},{2,1},{3,2},{5,4},{6,5},{7,6},{9,8},{10,9},{11,10},{13,12},{... | collective-permute-start | bytes 44 | tf_op jit(solution)/shard_map/ppermute | solution.py:24
  174.5 8.0 %collective-permute-start.32 = (f32[4,3,2,1,32]{4,0,3,2,1:T(4,128)S(1)}, f32[4,3,2,1,32]{4,0,3,2,1:T(4,128)S(1)}, u32[]{:S(2)}, u32[]{:S(2)}) collective-permute-start(f32[4,3,2,1,32]{4,0,3,2,1:T(4,128)S(1)} %get-tuple-element.169), channel_id=1, source_target_pairs={{4,0},{8,4},{12,8},{16,12},{20,16},{24,20},{28,24},{5,1},{9,5},{13... | collective-permute-start | bytes 9224 | tf_op jit(solution)/shard_map/ppermute | solution.py:24
  176.4 6.8 %collective-permute-start.33 = (f32[4,3,2,1,32]{4,0,3,2,1:T(4,128)S(1)}, f32[4,3,2,1,32]{4,0,3,2,1:T(4,128)S(1)}, u32[]{:S(2)}, u32[]{:S(2)}) collective-permute-start(f32[4,3,2,1,32]{4,0,3,2,1:T(4,128)S(1)} %get-tuple-element.168), channel_id=1, source_target_pairs={{0,4},{4,8},{8,12},{12,16},{16,20},{20,24},{24,28},{1,5},{5,9},{9,... | collective-permute-start | bytes 9224 | tf_op jit(solution)/shard_map/ppermute | solution.py:23
  193.0 8.5 %collective-permute-start.40 = (f32[4,3,1,1,16]{4,0,3,2,1:T(4,128)S(1)}, f32[4,3,1,1,16]{4,0,3,2,1:T(4,128)S(1)}, u32[]{:S(2)}, u32[]{:S(2)}) collective-permute-start(f32[4,3,1,1,16]{4,0,3,2,1:T(4,128)S(1)} %bitcast_divide_fusion), channel_id=1, source_target_pairs={{4,0},{8,4},{12,8},{16,12},{20,16},{24,20},{28,24},{5,1},{9,5},{13... | collective-permute-start | bytes 2312 | tf_op jit(solution)/shard_map/ppermute | solution.py:24
  194.9 7.3 %collective-permute-start.41 = (f32[4,3,1,1,16]{4,0,3,2,1:T(4,128)S(1)}, f32[4,3,1,1,16]{4,0,3,2,1:T(4,128)S(1)}, u32[]{:S(2)}, u32[]{:S(2)}) collective-permute-start(f32[4,3,1,1,16]{4,0,3,2,1:T(4,128)S(1)} %bitcast_divide_fusion), channel_id=1, source_target_pairs={{0,4},{4,8},{8,12},{12,16},{16,20},{20,24},{24,28},{1,5},{5,9},{9,... | collective-permute-start | bytes 2312 | tf_op jit(solution)/shard_map/ppermute | solution.py:23
  208.9 8.2 %collective-permute-start.44 = (f32[4,3,1,1,16]{4,0,3,2,1:T(4,128)S(1)}, f32[4,3,1,1,16]{4,0,3,2,1:T(4,128)S(1)}, u32[]{:S(2)}, u32[]{:S(2)}) collective-permute-start(f32[4,3,1,1,16]{4,0,3,2,1:T(4,128)S(1)} %divide_add_fusion.9), channel_id=1, source_target_pairs={{4,0},{8,4},{12,8},{16,12},{20,16},{24,20},{28,24},{5,1},{9,5},{13... | collective-permute-start | bytes 2312 | tf_op jit(solution)/shard_map/ppermute | solution.py:24
  210.8 7.0 %collective-permute-start.45 = (f32[4,3,1,1,16]{4,0,3,2,1:T(4,128)S(1)}, f32[4,3,1,1,16]{4,0,3,2,1:T(4,128)S(1)}, u32[]{:S(2)}, u32[]{:S(2)}) collective-permute-start(f32[4,3,1,1,16]{4,0,3,2,1:T(4,128)S(1)} %divide_add_fusion.9), channel_id=1, source_target_pairs={{0,4},{4,8},{8,12},{12,16},{16,20},{20,24},{24,28},{1,5},{5,9},{9,... | collective-permute-start | bytes 2312 | tf_op jit(solution)/shard_map/ppermute | solution.py:23
  225.1 7.9 %collective-permute-start.48 = (f32[4,3,1,1,16]{4,0,3,2,1:T(4,128)S(1)}, f32[4,3,1,1,16]{4,0,3,2,1:T(4,128)S(1)}, u32[]{:S(2)}, u32[]{:S(2)}) collective-permute-start(f32[4,3,1,1,16]{4,0,3,2,1:T(4,128)S(1)} %divide_add_fusion.8), channel_id=1, source_target_pairs={{4,0},{8,4},{12,8},{16,12},{20,16},{24,20},{28,24},{5,1},{9,5},{13... | collective-permute-start | bytes 2312 | tf_op jit(solution)/shard_map/ppermute | solution.py:24
  227.0 6.7 %collective-permute-start.49 = (f32[4,3,1,1,16]{4,0,3,2,1:T(4,128)S(1)}, f32[4,3,1,1,16]{4,0,3,2,1:T(4,128)S(1)}, u32[]{:S(2)}, u32[]{:S(2)}) collective-permute-start(f32[4,3,1,1,16]{4,0,3,2,1:T(4,128)S(1)} %divide_add_fusion.8), channel_id=1, source_target_pairs={{0,4},{4,8},{8,12},{12,16},{16,20},{20,24},{24,28},{1,5},{5,9},{9,... | collective-permute-start | bytes 2312 | tf_op jit(solution)/shard_map/ppermute | solution.py:23
  240.9 7.9 %collective-permute-start.52 = (f32[4,3,1,1,16]{4,0,3,2,1:T(4,128)S(1)}, f32[4,3,1,1,16]{4,0,3,2,1:T(4,128)S(1)}, u32[]{:S(2)}, u32[]{:S(2)}) collective-permute-start(f32[4,3,1,1,16]{4,0,3,2,1:T(4,128)S(1)} %divide_add_fusion.7), channel_id=1, source_target_pairs={{4,0},{8,4},{12,8},{16,12},{20,16},{24,20},{28,24},{5,1},{9,5},{13... | collective-permute-start | bytes 2312 | tf_op jit(solution)/shard_map/ppermute | solution.py:24
  242.9 6.7 %collective-permute-start.53 = (f32[4,3,1,1,16]{4,0,3,2,1:T(4,128)S(1)}, f32[4,3,1,1,16]{4,0,3,2,1:T(4,128)S(1)}, u32[]{:S(2)}, u32[]{:S(2)}) collective-permute-start(f32[4,3,1,1,16]{4,0,3,2,1:T(4,128)S(1)} %divide_add_fusion.7), channel_id=1, source_target_pairs={{0,4},{4,8},{8,12},{12,16},{16,20},{20,24},{24,28},{1,5},{5,9},{9,... | collective-permute-start | bytes 2312 | tf_op jit(solution)/shard_map/ppermute | solution.py:23
  256.8 7.9 %collective-permute-start.56 = (f32[4,3,1,1,16]{4,0,3,2,1:T(4,128)S(1)}, f32[4,3,1,1,16]{4,0,3,2,1:T(4,128)S(1)}, u32[]{:S(2)}, u32[]{:S(2)}) collective-permute-start(f32[4,3,1,1,16]{4,0,3,2,1:T(4,128)S(1)} %divide_add_fusion.6), channel_id=1, source_target_pairs={{4,0},{8,4},{12,8},{16,12},{20,16},{24,20},{28,24},{5,1},{9,5},{13... | collective-permute-start | bytes 2312 | tf_op jit(solution)/shard_map/ppermute | solution.py:24
  258.8 6.7 %collective-permute-start.57 = (f32[4,3,1,1,16]{4,0,3,2,1:T(4,128)S(1)}, f32[4,3,1,1,16]{4,0,3,2,1:T(4,128)S(1)}, u32[]{:S(2)}, u32[]{:S(2)}) collective-permute-start(f32[4,3,1,1,16]{4,0,3,2,1:T(4,128)S(1)} %divide_add_fusion.6), channel_id=1, source_target_pairs={{0,4},{4,8},{8,12},{12,16},{16,20},{20,24},{24,28},{1,5},{5,9},{9,... | collective-permute-start | bytes 2312 | tf_op jit(solution)/shard_map/ppermute | solution.py:23
  274.9 8.2 %collective-permute-start.60 = (f32[4,3,2,1,32]{4,0,3,2,1:T(4,128)S(1)}, f32[4,3,2,1,32]{4,0,3,2,1:T(4,128)S(1)}, u32[]{:S(2)}, u32[]{:S(2)}) collective-permute-start(f32[4,3,2,1,32]{4,0,3,2,1:T(4,128)S(1)} %get-tuple-element.167), channel_id=1, source_target_pairs={{4,0},{8,4},{12,8},{16,12},{20,16},{24,20},{28,24},{5,1},{9,5},{13... | collective-permute-start | bytes 9224 | tf_op jit(solution)/shard_map/ppermute | solution.py:24
  276.9 7.1 %collective-permute-start.61 = (f32[4,3,2,1,32]{4,0,3,2,1:T(4,128)S(1)}, f32[4,3,2,1,32]{4,0,3,2,1:T(4,128)S(1)}, u32[]{:S(2)}, u32[]{:S(2)}) collective-permute-start(f32[4,3,2,1,32]{4,0,3,2,1:T(4,128)S(1)} %get-tuple-element.166), channel_id=1, source_target_pairs={{0,4},{4,8},{8,12},{12,16},{16,20},{20,24},{24,28},{1,5},{5,9},{9,... | collective-permute-start | bytes 9224 | tf_op jit(solution)/shard_map/ppermute | solution.py:23
  293.8 8.2 %collective-permute-start.64 = (f32[4,3,2,1,32]{4,0,3,2,1:T(4,128)S(1)}, f32[4,3,2,1,32]{4,0,3,2,1:T(4,128)S(1)}, u32[]{:S(2)}, u32[]{:S(2)}) collective-permute-start(f32[4,3,2,1,32]{4,0,3,2,1:T(4,128)S(1)} %get-tuple-element.165), channel_id=1, source_target_pairs={{4,0},{8,4},{12,8},{16,12},{20,16},{24,20},{28,24},{5,1},{9,5},{13... | collective-permute-start | bytes 9224 | tf_op jit(solution)/shard_map/ppermute | solution.py:24
  295.7 7.1 %collective-permute-start.65 = (f32[4,3,2,1,32]{4,0,3,2,1:T(4,128)S(1)}, f32[4,3,2,1,32]{4,0,3,2,1:T(4,128)S(1)}, u32[]{:S(2)}, u32[]{:S(2)}) collective-permute-start(f32[4,3,2,1,32]{4,0,3,2,1:T(4,128)S(1)} %get-tuple-element.164), channel_id=1, source_target_pairs={{0,4},{4,8},{8,12},{12,16},{16,20},{20,24},{24,28},{1,5},{5,9},{9,... | collective-permute-start | bytes 9224 | tf_op jit(solution)/shard_map/ppermute | solution.py:23
  314.0 8.5 %collective-permute-start.69 = (f32[4,3,4,1,64]{4,2,3,1,0:T(4,128)S(1)}, f32[4,3,4,1,64]{4,2,3,1,0:T(4,128)S(1)}, u32[]{:S(2)}, u32[]{:S(2)}) collective-permute-start(f32[4,3,4,1,64]{4,2,3,1,0:T(4,128)S(1)} %bitcast.356), channel_id=1, source_target_pairs={{0,4},{4,8},{8,12},{12,16},{16,20},{20,24},{24,28},{1,5},{5,9},{9,... | collective-permute-start | bytes 36872 | tf_op jit(solution)/shard_map/ppermute | solution.py:23
  368.5 6.3 %collective-permute-start.76 = (f32[4,3,8,1,128]{4,2,3,1,0:T(8,128)S(1)}, f32[4,3,8,1,128]{4,2,3,1,0:T(8,128)S(1)}, u32[]{:S(2)}, u32[]{:S(2)}) collective-permute-start(f32[4,3,8,1,128]{4,2,3,1,0:T(8,128)S(1)} %bitcast.346), channel_id=1, source_target_pairs={{4,0},{8,4},{12,8},{16,12},{20,16},{24,20},{28,24},{5,1},{9,5},{13... | collective-permute-start | bytes 147464 | tf_op jit(solution)/shard_map/ppermute | solution.py:24
  375.0 10.0 %collective-permute-start.78 = (f32[4,3,8,10,1]{4,2,3,1,0:T(8,128)S(1)}, f32[4,3,8,10,1]{4,2,3,1,0:T(8,128)S(1)}, u32[]{:S(2)}, u32[]{:S(2)}) collective-permute-start(f32[4,3,8,10,1]{4,2,3,1,0:T(8,128)S(1)} %get-tuple-element.47), channel_id=1, source_target_pairs={{1,0},{2,1},{3,2},{5,4},{6,5},{7,6},{9,8},{10,9},{11,10},{13,12},{... | collective-permute-start | bytes 11528 | tf_op jit(solution)/shard_map/ppermute | solution.py:24
  376.7 12.4 %collective-permute-start.79 = (f32[4,3,8,10,1]{4,2,3,1,0:T(8,128)S(1)}, f32[4,3,8,10,1]{4,2,3,1,0:T(8,128)S(1)}, u32[]{:S(2)}, u32[]{:S(2)}) collective-permute-start(f32[4,3,8,10,1]{4,2,3,1,0:T(8,128)S(1)} %get-tuple-element.46), channel_id=1, source_target_pairs={{0,1},{1,2},{2,3},{4,5},{5,6},{6,7},{8,9},{9,10},{10,11},{12,13},{... | collective-permute-start | bytes 11528 | tf_op jit(solution)/shard_map/ppermute | solution.py:23
  394.8 6.3 %collective-permute-start.80 = (f32[4,3,8,1,128]{4,2,3,1,0:T(8,128)S(1)}, f32[4,3,8,1,128]{4,2,3,1,0:T(8,128)S(1)}, u32[]{:S(2)}, u32[]{:S(2)}) collective-permute-start(f32[4,3,8,1,128]{4,2,3,1,0:T(8,128)S(1)} %bitcast.347), channel_id=1, source_target_pairs={{4,0},{8,4},{12,8},{16,12},{20,16},{24,20},{28,24},{5,1},{9,5},{13... | collective-permute-start | bytes 147464 | tf_op jit(solution)/shard_map/ppermute | solution.py:24
  401.3 10.9 %collective-permute-start.82 = (f32[4,3,8,10,1]{4,2,3,1,0:T(8,128)S(1)}, f32[4,3,8,10,1]{4,2,3,1,0:T(8,128)S(1)}, u32[]{:S(2)}, u32[]{:S(2)}) collective-permute-start(f32[4,3,8,10,1]{4,2,3,1,0:T(8,128)S(1)} %get-tuple-element.43), channel_id=1, source_target_pairs={{1,0},{2,1},{3,2},{5,4},{6,5},{7,6},{9,8},{10,9},{11,10},{13,12},{... | collective-permute-start | bytes 11528 | tf_op jit(solution)/shard_map/ppermute | solution.py:24
  403.0 13.4 %collective-permute-start.83 = (f32[4,3,8,10,1]{4,2,3,1,0:T(8,128)S(1)}, f32[4,3,8,10,1]{4,2,3,1,0:T(8,128)S(1)}, u32[]{:S(2)}, u32[]{:S(2)}) collective-permute-start(f32[4,3,8,10,1]{4,2,3,1,0:T(8,128)S(1)} %get-tuple-element.42), channel_id=1, source_target_pairs={{0,1},{1,2},{2,3},{4,5},{5,6},{6,7},{8,9},{9,10},{10,11},{12,13},{... | collective-permute-start | bytes 11528 | tf_op jit(solution)/shard_map/ppermute | solution.py:23
  (74 other events, 1009.2 us)
where the time goes:
time: 429 us; the launch traced here: 421 us
  starting transfers between devices  234 us (55%)
  waiting for transfers between devices  113 us (26%)
  other arithmetic  40.2 us (9%)
  local copies, waits for them, and re-layouts  30.3 us (7%)
    ppermute x42, starting transfers between devices, padded_2(): before = lax.ppermute(last, axis, up)  124 us
    ppermute x42, starting transfers between devices, padded_2(): after = lax.ppermute(initial, axis, down)  110 us
    ppermute x42, waiting for transfers between devices, padded_2(): after = lax.ppermute(initial, axis, down)  62 us
    ppermute x42, waiting for transfers between devices, padded_2(): before = lax.ppermute(last, axis, up)  50.9 us
    reduce_sum x8, other arithmetic, coarsen(): return jnp.mean(grouped, axis=(-5, -3, -1))  14.8 us
    another operation x51, other arithmetic, stencil(): graddiv = jnp.stack(pieces, axis=1)  8.93 us
  transfers between devices with their start and end apart: 84, of which 40 were waited for; matrix products, arithmetic and copies ran while one was open for 9% of the time, Pallas kernels for 0%

commit v1 on v0

v1 whole, which is shorter than its diff:
```python
import functools

import jax
import jax.numpy as jnp
from jax import lax
from jax.experimental import pallas as pl
from jax.experimental.pallas import tpu as pltpu
from jax.sharding import PartitionSpec as P

RELAX = 0.6
MASS = 0.01
GRAD_DIV = 2.5
VEC, COMP, NZ, BX, BY = 4, 3, 8, 8, 128
COARSE = 6
RIM = 16
SEG = BY + 2 * RIM
L0 = VEC * SEG
L1 = 256
FX = 6
CX = 7
F32 = jnp.float32


def iota(shape, dim):
    return lax.broadcasted_iota(jnp.int32, shape, dim)


def exact_dot(value, selector):
    high = value.astype(jnp.bfloat16)
    rest = value - high.astype(F32)
    mid = rest.astype(jnp.bfloat16)
    low = (rest - mid.astype(F32)).astype(jnp.bfloat16)
    dot = functools.partial(jnp.dot, preferred_element_type=F32)
    return dot(high, selector) + dot(mid, selector) + dot(low, selector)


class Level:
    def __init__(self, index, rows, lanes, length=None):
        self.scale = 0.25**index
        self.rows = rows
        self.lanes = lanes
        row = iota((8, lanes), 0)
        self.has_zp, self.has_zm = row < 8 - rows, row >= rows
        self.has_yp = self.has_ym = None
        if length is not None:
            lane = iota((8, lanes), 1)
            self.has_yp, self.has_ym = lane < length - 1, lane > 0

    def yp(self, a):
        return pltpu.roll(a, self.lanes - 1, 1)

    def ym(self, a):
        return pltpu.roll(a, 1, 1)

    def zp(self, a):
        return pltpu.roll(a, 8 - self.rows, 0)

    def zm(self, a):
        return pltpu.roll(a, self.rows, 0)

    @staticmethod
    def keep(mask, a):
        return a if mask is None else jnp.where(mask, a, 0.0)

    def dy_of(self, up, down):
        return self.keep(self.has_yp, up) - self.keep(self.has_ym, down)

    def dz_of(self, up, down):
        return self.keep(self.has_zp, up) - self.keep(self.has_zm, down)

    @property
    def layered(self):
        return self.rows < 8

    def weights(self, coeff, at, k_ref, kat):
        c = coeff[at]
        near = [coeff[at + 1], coeff[at - 1], self.keep(self.has_yp, self.yp(c)), self.keep(self.has_ym, self.ym(c))]
        if self.layered:
            near += [self.keep(self.has_zp, self.zp(c)), self.keep(self.has_zm, self.zm(c))]
        total = near[0]
        for n in near[1:]:
            total = total + n
        diag = MASS + self.scale * (8.0 * c + 0.5 * total)
        gain = jnp.where(c > 0.0, RELAX / diag, 0.0)
        half = (0.5 * self.scale) * gain
        own = (GRAD_DIV * self.scale) * gain * c
        masks = [None, None, self.has_yp, self.has_ym, self.has_zp, self.has_zm]
        for i, n in enumerate(near):
            face = half * (c + n)
            k_ref[i, kat] = self.keep(masks[i], face)
            k_ref[6 + i, kat] = self.keep(masks[i], face + own)
        k_ref[12, kat] = 0.25 * own
        return gain, diag * (1.0 / RELAX)

    def cross(self, u, at, t_ref, tat):
        uy = u[1, at]
        t = self.dy_of(self.yp(uy), self.ym(uy))
        if self.layered:
            uz = u[2, at]
            t = t + self.dz_of(self.zp(uz), self.zm(uz))
        t_ref[tat] = t

    def change(self, u, at, t_ref, tat, k_ref, kat, x1, xat):
        k = lambda i: k_ref[i, kat]
        ux, uy, uz = (u[c, at] for c in range(3))
        fore = [u[c, at + 1] for c in range(3)]
        back = [u[c, at - 1] for c in range(3)]
        y_up = [self.yp(a) for a in (ux, uy, uz)]
        y_dn = [self.ym(a) for a in (ux, uy, uz)]
        dxx = fore[0] - back[0]
        dyy = self.dy_of(y_up[1], y_dn[1])
        side = dxx
        if self.layered:
            z_up = [self.zp(a) for a in (ux, uy, uz)]
            z_dn = [self.zm(a) for a in (ux, uy, uz)]
            side = dxx + self.dz_of(z_up[2], z_dn[2])
        mixed = [t_ref[tat + 1] - t_ref[tat - 1], self.dy_of(self.yp(side), self.ym(side)), None]
        if self.layered:
            below = dxx + dyy
            mixed[2] = self.dz_of(self.zp(below), self.zm(below))
        out = []
        for c, own in enumerate((ux, uy, uz)):
            total = x1[c, xat] - RELAX * own
            total = total + k(6 if c == 0 else 0) * fore[c] + k(7 if c == 0 else 1) * back[c]
            total = total + k(8 if c == 1 else 2) * y_up[c] + k(9 if c == 1 else 3) * y_dn[c]
            if self.layered:
                total = total + k(10 if c == 2 else 4) * z_up[c] + k(11 if c == 2 else 5) * z_dn[c]
            if mixed[c] is not None:
                total = total + k(12) * mixed[c]
            out.append(total)
        return out

    def apply(self, u, uo, t_ref, k_ref, ko, x1, xo, low, high, unroll, write):
        def ahead(p):
            self.cross(u, p + uo, t_ref, p - low + 1)

        def one(p):
            d = self.change(u, p + uo, t_ref, p - low + 1, k_ref, p + ko, x1, p + xo)
            write(p, d)

        each(low - 1, high + 1, unroll, ahead)
        each(low, high, unroll, one)


def each(low, high, unroll, body):
    count = high - low
    while count % unroll:
        unroll -= 1
    if count == unroll:
        for p in range(low, high):
            body(p)
        return

    def step(i, carry):
        for b in range(unroll):
            body(low + i * unroll + b)
        return carry

    lax.fori_loop(0, count // unroll, step, 0)


def segment_lane(shape, dim):
    lane = iota(shape, dim)
    vec = (lane >= SEG).astype(jnp.int32) + (lane >= 2 * SEG).astype(jnp.int32) + (lane >= 3 * SEG).astype(jnp.int32)
    return vec * 128 + (32 - RIM // 2) + ((lane - vec * SEG) >> 1)


def bf16(mask, value):
    return jnp.where(mask, value, 0.0).astype(jnp.bfloat16)


def rows_of(ref, group, x):
    return ref[pl.ds(group * 64 + x, 8, stride=8), :]


def coeff_rows(m_ref, x):
    return jnp.where(rows_of(m_ref, 0, x) == 1, 1.0, 0.05).astype(F32)


def edge_kernel(f_ref, m_ref, left_ref, right_ref):
    for x in range(BX):
        for v in range(VEC):
            for c in range(COMP):
                val = rows_of(f_ref, v * COMP + c, x)
                lanes = pl.ds((x // 4) * 64 + 16 * v, 16)
                left_ref[c * 4 + x % 4, :, lanes] = val[:, :RIM]
                right_ref[c * 4 + x % 4, :, lanes] = val[:, BY - RIM :]
        val = coeff_rows(m_ref, x)
        left_ref[12, :, pl.ds(16 * x, 16)] = val[:, :RIM]
        right_ref[12, :, pl.ds(16 * x, 16)] = val[:, BY - RIM :]


def join_kernel(gy, f_ref, m_ref, l_ref, r_ref, own_ref, coeff_ref, left_ref, right_ref):
    place = lax.axis_index("gy")
    from_left = (place > 0).astype(F32)
    from_right = (place < gy - 1).astype(F32)
    for x in range(BX):
        for c in range(COMP):
            left = l_ref[c * 4 + x % 4] * from_left
            right = r_ref[c * 4 + x % 4] * from_right
            for v in range(VEC):
                start = SEG * v
                at = (x // 4) * 64 + 16 * v
                own_ref[c, x, :, pl.ds(start, RIM)] = left[:, at : at + RIM]
                own_ref[c, x, :, pl.ds(start + RIM, BY)] = rows_of(f_ref, v * COMP + c, x)
                own_ref[c, x, :, pl.ds(start + RIM + BY, RIM)] = right[:, at : at + RIM]
        start = SEG * (x % 4)
        coeff_ref[x // 4, :, pl.ds(start, RIM)] = l_ref[12, :, pl.ds(16 * x, 16)] * from_left
        coeff_ref[x // 4, :, pl.ds(start + RIM, BY)] = coeff_rows(m_ref, x)
        coeff_ref[x // 4, :, pl.ds(start + RIM + BY, RIM)] = r_ref[12, :, pl.ds(16 * x, 16)] * from_right
    for c in range(COMP):
        for x in range(FX):
            left_ref[c * FX + x] = own_ref[c, x]
            right_ref[c * FX + x] = own_ref[c, x + BX - FX]
    for i in range(2):
        left_ref[COMP * FX + i] = coeff_ref[i]
        right_ref[COMP * FX + i] = coeff_ref[i]


def down_kernel(
    gx, own_ref, coeff_ref, l_ref, r_ref,
    pay_ref, send_l, send_r, x2b_ref, x1b_ref, c1_ref, x2a_ref, x1a_ref, c0_ref,
    cx, k0, dr0, x1, x2, t0, rest, stack, k1, dr1, f1, y1, y2, t1, r1, stack1, pay,
):
    place = lax.axis_index("gx")
    from_left = (place > 0).astype(F32)
    from_right = (place < gx - 1).astype(F32)
    a = Level(0, 1, L0)

    def spread(plane, packed, sub, factor):
        val = packed[:, SEG * sub : SEG * sub + SEG]
        if factor is not None:
            val = val * factor
        for v in range(VEC):
            cx[plane + CX, :, pl.ds(SEG * v, SEG)] = val

    for x in range(BX):
        spread(x, coeff_ref[x // 4], x % 4, None)
    for x in range(CX):
        spread(x - CX, l_ref[COMP * FX + (x + BX - CX) // 4], (x + BX - CX) % 4, from_left)
        spread(x + BX, r_ref[COMP * FX + x // 4], x % 4, from_right)

    def start(low, high, load):
        def body(p):
            gain, back = a.weights(cx, p + CX, k0, p + FX)
            dr0[p + FX] = back
            for c in range(COMP):
                x1[c, p + FX] = gain * load(c, p)

        each(low, high, 1, body)

    start(-FX, 0, lambda c, p: l_ref[c * FX + p + FX])
    start(0, BX, lambda c, p: own_ref[c, p])
    start(BX, BX + FX, lambda c, p: r_ref[c * FX + p - BX])

    def to_x2(p, change):
        for c in range(COMP):
            x2[c, p + FX] = x1[c, p + FX] + change[c]

    a.apply(x1, FX, t0, k0, FX, x1, FX, 1 - FX, BX + FX - 1, 2, to_x2)

    def to_rest(p, change):
        for c in range(COMP):
            rest[c, p + 4] = change[c] * dr0[p + FX]

    a.apply(x2, FX, t0, k0, FX, x1, FX, -4, BX + 4, 2, to_rest)

    def gather_rows(i, plane):
        stack[pl.ds(8 * i, 8), :] = plane + a.zp(plane)

    for c in range(COMP):
        for i in range(8):
            gather_rows(8 * c + i, rest[c, 2 * i] + rest[c, 2 * i + 1])
    for i in range(10):
        gather_rows(24 + i, cx[2 * i + 1] + cx[2 * i + 2])
    selector = bf16(segment_lane((L0, 2 * L1), 0) == iota((L0, 2 * L1), 1), 0.125)
    coarse = exact_dot(stack[...], selector)
    even = (iota((8, L1), 0) & 1) == 0

    def merged(i):
        block = coarse[8 * i : 8 * i + 8]
        return jnp.where(even, block[:, :L1], pltpu.roll(block[:, L1:], 1, 0))

    for c in range(COMP):
        for i in range(8):
            f1[c, i] = merged(8 * c + i)
    for i in range(10):
        c1_ref[i] = merged(24 + i)

    b = Level(1, 2, L1)
    for p in range(-2, 6):
        gain, back = b.weights(c1_ref, p + 3, k1, p + 2)
        dr1[p + 2] = back
        for c in range(COMP):
            y1[c, p + 2] = gain * f1[c, p + 2]

    def to_y2(p, change):
        for c in range(COMP):
            y2[c, p + 1] = y1[c, p + 2] + change[c]

    b.apply(y1, 2, t1, k1, 2, y1, 2, -1, 5, 2, to_y2)

    def to_r1(p, change):
        for c in range(COMP):
            r1[c, p] = change[c] * dr1[p + 2]

    b.apply(y2, 1, t1, k1, 2, y1, 2, 0, 4, 2, to_r1)

    def gather_rows1(i, plane):
        plane = plane + b.zp(plane)
        stack1[pl.ds(8 * i, 8), :] = plane[:, :128]
        stack1[pl.ds(64 + 8 * i, 8), :] = plane[:, 128:]

    for c in range(COMP):
        for i in range(2):
            gather_rows1(2 * c + i, r1[c, 2 * i] + r1[c, 2 * i + 1])
    for i in range(2):
        gather_rows1(6 + i, c1_ref[2 * i + 3] + c1_ref[2 * i + 4])
    lane = iota((128, 128), 0) - 32
    selector1 = bf16((lane >> 1 == iota((128, 128), 1)) & (lane >= 0) & (lane < 64), 0.125)
    coarse1 = exact_dot(stack1[...], selector1)
    first = (iota((8, 32), 0) & 2) == 0
    for g in range(8):
        low = coarse1[8 * g : 8 * g + 8]
        high = pltpu.roll(coarse1[64 + 8 * g : 72 + 8 * g], 2, 0)
        pay[pl.ds(8 * (g // 4), 8), pl.ds(32 * (g % 4), 32)] = jnp.where(first, low[:, :32], high[:, :32])
    packed = pay[...]

    def copy(i, carry):
        pay_ref[i] = packed
        return carry

    lax.fori_loop(0, pay_ref.shape[0], copy, 0)

    for c in range(COMP):
        for i in range(3):
            send_l[3 * c + i] = y2[c, 1 + i]
            send_r[3 * c + i] = y2[c, 2 + i]
        for i in range(4):
            x2b_ref[c, i] = y2[c, 1 + i]
        for i in range(8):
            x1b_ref[c, i] = y1[c, i]
        for i in range(12):
            x2a_ref[c, i] = x2[c, i + 4]
        for i in range(10):
            x1a_ref[c, i] = x1[c, i + 5]
    for i in range(12):
        c0_ref[i] = cx[i + 5]


def up_kernel(
    gx, gy, got_ref, l_ref, r_ref, x2b_ref, x1b_ref, c1_ref, x2a_ref, x1a_ref, c0_ref, out_ref,
    c2, f2, k2, dr2, x1c, ua, ub, rc, t2, s2, c3, k3, x1d, va, vb, t3, s3, sw, w0, w1, k1, t1, sp, k0, u0, u1, t0,
):
    nx2, nx3 = 2 * gx, gx
    y2, l3 = 32 * gy, c3.shape[-1]
    place_x = lax.axis_index("gx")
    place_y = lax.axis_index("gy")
    from_left = (place_x > 0).astype(F32)
    from_right = (place_x < gx - 1).astype(F32)

    zero2 = jnp.zeros((8, y2), F32)
    for ref in (ua, ub):
        for c in range(COMP):
            for i in (0, 1, nx2 + 2, nx2 + 3):
                ref[c, i] = zero2
    c2[0] = zero2
    c2[nx2 + 1] = zero2

    def unpack(i):
        for j in range(gy):
            for g in range(8):
                block = got_ref[i * gy + j, pl.ds(8 * (g // 4), 8), pl.ds(32 * (g % 4), 32)]
                if g < 6:
                    f2[g // 2, 2 * i + g % 2, :, pl.ds(32 * j, 32)] = block
                else:
                    c2[2 * i + g - 5, :, pl.ds(32 * j, 32)] = block

    each(0, gx, 8, unpack)
    m = Level(2, 4, y2, y2)

    def start2(p):
        gain, back = m.weights(c2, p + 1, k2, p)
        dr2[p] = back
        for c in range(COMP):
            val = gain * f2[c, p]
            x1c[c, p] = val
            ua[c, p + 2] = val

    each(0, nx2, 4, start2)

    def sweep2(src, dst):
        def write(p, change):
            for c in range(COMP):
                dst[c, p + 2] = src[c, p + 2] + change[c]

        m.apply(src, 2, t2, k2, 0, x1c, 0, 0, nx2, 4, write)

    sweep2(ua, ub)

    def to_rc(p, change):
        for c in range(COMP):
            rc[c, p] = change[c] * dr2[p]

    m.apply(ub, 2, t2, k2, 0, x1c, 0, 0, nx2, 4, to_rc)

    def gather2(i):
        for c in range(COMP):
            plane = rc[c, 2 * i] + rc[c, 2 * i + 1]
            s2[pl.ds(8 * (c * nx3 + i), 8), :] = plane + pltpu.roll(plane, 4, 0)
        plane = c2[2 * i + 1] + c2[2 * i + 2]
        s2[pl.ds(8 * (COMP * nx3 + i), 8), :] = plane + pltpu.roll(plane, 4, 0)

    for i in range(nx3):
        gather2(i)
    selector = bf16((iota((y2, l3), 0) >> 1) == iota((y2, l3), 1), 0.125)
    coarse = exact_dot(s2[...], selector)
    zero3 = jnp.zeros((8, l3), F32)
    for ref in (va, vb):
        for c in range(COMP):
            ref[c, 0] = zero3
            ref[c, nx3 + 1] = zero3
    c3[0] = zero3
    c3[nx3 + 1] = zero3
    for i in range(nx3):
        c3[i + 1] = coarse[8 * (COMP * nx3 + i) : 8 * (COMP * nx3 + i) + 8]
    n = Level(3, 8, l3, 16 * gy)
    for p in range(nx3):
        gain, _ = n.weights(c3, p + 1, k3, p)
        for c in range(COMP):
            val = gain * coarse[8 * (c * nx3 + p) : 8 * (c * nx3 + p) + 8]
            x1d[c, p] = val
            va[c, p + 1] = val
    src, dst = va, vb
    for _ in range(COARSE - 1):

        def write3(p, change, src=src, dst=dst):
            for c in range(COMP):
                dst[c, p + 1] = src[c, p + 1] + change[c]

        n.apply(src, 1, t3, k3, 0, x1d, 0, 0, nx3, 8, write3)
        src, dst = dst, src
    for c in range(COMP):
        for i in range(nx3):
            s3[pl.ds(8 * (c * nx3 + i), 8), :] = src[c, i + 1]
    selector = bf16((iota((l3, y2), 1) >> 1) == iota((l3, y2), 0), 1.0)
    fine = exact_dot(s3[...], selector)
    for c in range(COMP):
        for i in range(nx3):
            block = fine[8 * (c * nx3 + i) : 8 * (c * nx3 + i) + 8]
            for j in range(2):
                ub[c, 2 * i + j + 2] = ub[c, 2 * i + j + 2] + block
    sweep2(ub, ua)
    sweep2(ua, ub)

    row = iota((8, y2), 0)
    for c in range(COMP):
        for i in range(6):
            e = ub[c, 2 * place_x + i]
            at = 16 * (6 * c + i)
            sw[pl.ds(at, 8), :] = jnp.where((row & 2) == 0, e, pltpu.roll(e, 2, 0))
            sw[pl.ds(at + 8, 8), :] = jnp.where((row & 2) != 0, e, pltpu.roll(e, 6, 0))
    y1g = place_y * 64 + iota((y2, 128), 1) - 32
    fine = exact_dot(sw[...], bf16((y1g >> 1) == iota((y2, 128), 0), 1.0))
    for c in range(COMP):
        for p in range(-3, 7):
            if p < 0:
                val = l_ref[3 * c + p + 3] * from_left
            elif p < 4:
                val = x2b_ref[c, p]
            else:
                val = r_ref[3 * c + p - 4] * from_right
            at = 16 * (6 * c + (p + 4) // 2)
            w0[c, p + 3] = val + jnp.concatenate([fine[at : at + 8], fine[at + 8 : at + 16]], axis=1)
    b = Level(1, 2, L1)
    for p in range(-2, 6):
        b.weights(c1_ref, p + 3, k1, p + 2)

    def write1(p, change):
        for c in range(COMP):
            w1[c, p + 3] = w0[c, p + 3] + change[c]

    b.apply(w0, 3, t1, k1, 2, x1b_ref, 2, -2, 6, 2, write1)

    odd = (iota((8, L1), 0) & 1) != 0

    def write1b(p, change):
        for c in range(COMP):
            e = w1[c, p + 3] + change[c]
            at = 8 * (6 * c + p + 1)
            sp[pl.ds(at, 8), pl.ds(0, L1)] = jnp.where(odd, pltpu.roll(e, 1, 0), e)
            sp[pl.ds(at, 8), pl.ds(L1, L1)] = jnp.where(odd, e, pltpu.roll(e, 7, 0))

    for p in range(-2, 6):
        b.cross(w1, p + 3, t1, p + 2)
    for p in range(-1, 5):
        write1b(p, b.change(w1, p + 3, t1, p + 2, k1, p + 2, x1b_ref, p + 2))

    selector = bf16(segment_lane((2 * L1, L0), 1) == iota((2 * L1, L0), 0), 1.0)
    fine = exact_dot(sp[...], selector)
    for c in range(COMP):
        for i in range(6):
            block = fine[8 * (6 * c + i) : 8 * (6 * c + i) + 8]
            for j in range(2):
                u0[c, 2 * i + j] = x2a_ref[c, 2 * i + j] + block
    a = Level(0, 1, L0)

    def start0(p):
        a.weights(c0_ref, p + 2, k0, p + 1)

    each(-1, 9, 1, start0)

    def write0(p, change):
        for c in range(COMP):
            u1[c, p + 2] = u0[c, p + 2] + change[c]

    a.apply(u0, 2, t0, k0, 1, x1a_ref, 1, -1, 9, 2, write0)

    def write_out(p, change):
        for c in range(COMP):
            val = u1[c, p + 2] + change[c]
            for v in range(VEC):
                at = SEG * v + RIM
                out_ref[pl.ds((v * COMP + c) * 64 + p, 8, stride=8), :] = val[:, at : at + BY]

    a.apply(u1, 2, t0, k0, 1, x1a_ref, 1, 0, BX, 2, write_out)


def call(kernel, outs, scratch, *args):
    vmem = pl.BlockSpec(memory_space=pltpu.VMEM)
    shapes = [jax.ShapeDtypeStruct(s, F32) for s in outs]
    return pl.pallas_call(
        kernel,
        out_shape=shapes,
        in_specs=[vmem] * len(args),
        out_specs=[vmem] * len(outs),
        scratch_shapes=[pltpu.VMEM(s, F32) for s in scratch],
        compiler_params=pltpu.CompilerParams(vmem_limit_bytes=48 * 1024 * 1024),
    )(*args)


def per_device(gx, gy, right_side, material):
    def ring(value, axis, size, step):
        return lax.ppermute(value, axis, [(i, (i + step) % size) for i in range(size)])

    f = right_side.reshape(VEC * COMP * NZ * BX, BY)
    m = material.reshape(NZ * BX, BY)
    edge = (13, 8, 128)
    to_left, to_right = call(edge_kernel, [edge, edge], [], f, m)
    right = ring(to_left, "gy", gy, -1)
    left = ring(to_right, "gy", gy, 1)
    side = (COMP * FX + 2, 8, L0)
    own, coeff, to_left, to_right = call(
        functools.partial(join_kernel, gy), [(COMP, BX, 8, L0), (2, 8, L0), side, side], [], f, m, left, right
    )
    right = ring(to_left, "gx", gx, -1)
    left = ring(to_right, "gx", gx, 1)
    n = gx * gy
    plane = lambda *lead: (*lead, 8, L0)
    plane1 = lambda *lead: (*lead, 8, L1)
    pay, to_left, to_right, *kept = call(
        functools.partial(down_kernel, gx),
        [(n, 16, 128), plane1(9), plane1(9), plane1(3, 4), plane1(3, 8), plane1(10), plane(3, 12), plane(3, 10), plane(12)],
        [
            plane(22), plane(13, 20), plane(20), plane(3, 20), plane(3, 20), plane(20), plane(3, 16), (272, L0),
            plane1(13, 8), plane1(8), plane1(3, 8), plane1(3, 8), plane1(3, 6), plane1(8), plane1(3, 4), (128, 128), (16, 128),
        ],
        own, coeff, left, right,
    )
    right = ring(to_left, "gx", gx, -1)
    left = ring(to_right, "gx", gx, 1)
    got = lax.all_to_all(pay, ("gx", "gy"), 0, 0)
    nx2, nx3, y2, l3 = 2 * gx, gx, 32 * gy, max(128, 16 * gy)
    plane2 = lambda *lead: (*lead, 8, y2)
    plane3 = lambda *lead: (*lead, 8, l3)
    (out,) = call(
        functools.partial(up_kernel, gx, gy),
        [(VEC * COMP * NZ * BX, BY)],
        [
            plane2(nx2 + 2), plane2(3, nx2), plane2(13, nx2), plane2(nx2), plane2(3, nx2), plane2(3, nx2 + 4), plane2(3, nx2 + 4),
            plane2(3, nx2), plane2(nx2 + 2), (32 * nx3, y2),
            plane3(nx3 + 2), plane3(13, nx3), plane3(3, nx3), plane3(3, nx3 + 2), plane3(3, nx3 + 2), plane3(nx3 + 2), (24 * nx3, l3),
            (288, y2), plane1(3, 10), plane1(3, 10), plane1(13, 8), plane1(10), (144, 2 * L1),
            plane(13, 10), plane(3, 12), plane(3, 12), plane(12),
        ],
        got, left, right, *kept,
    )
    return out.reshape(right_side.shape)


def solution(mesh):
    gx, gy = mesh.shape["gx"], mesh.shape["gy"]
    spec = P(None, None, None, "gx", "gy")
    return jax.shard_map(
        functools.partial(per_device, gx, gy), mesh=mesh, in_specs=(spec, P(None, "gx", "gy")), out_specs=spec, check_vma=False
    )
```

time: 429 us -> 61 us (0.14)
  the two profiles are of different devices: /device:TPU:27 before, /device:TPU:0 now
where the time goes in v1:
time: 61 us; the launch traced here: 60.7 us
  Pallas kernels  24 us (39%)
  waiting for transfers between devices  18.2 us (30%)
  starting transfers between devices  16.7 us (27%)
  local copies, waits for them, and re-layouts  1.75 us (3%)
    pallas_call x4, Pallas kernels, call(): pl.pallas_call(kernel, out_shape=shapes, in_specs=[vmem] * len(args), out...  24 us
    ppermute x6, waiting for transfers between devices, ring(): lax.ppermute(value, axis, [(i, (i + step) % size) for i in range(size)])  14.1 us
    ppermute x6, starting transfers between devices, ring(): lax.ppermute(value, axis, [(i, (i + step) % size) for i in range(size)])  10.6 us
    all_to_all x1, starting transfers between devices, per_device(): got = lax.all_to_all(pay, ('gx', 'gy'), 0, 0)  6.14 us
    all_to_all x1, waiting for transfers between devices, per_device(): got = lax.all_to_all(pay, ('gx', 'gy'), 0, 0)  4.19 us
    unnamed x4, local copies, waits for them, and re-layouts  1.75 us
  transfers between devices with their start and end apart: 7, of which 5 were waited for; matrix products, arithmetic and copies ran while one was open for 0% of the time, Pallas kernels for 0%

profile of v1, /device:TPU:0, one launch (start us, length us, event | category | flops | bytes accessed | tf_op | source)
XLA Modules:
  0.0 60.7 jit_solution(14846835804587208828)
XLA Ops:
  0.0 0.0 copy-start
  0.0 1.0 %copy-done = f32[4,3,8,8,128]{4,3,2,1,0:T(8,128)S(1)} copy-done((f32[4,3,8,8,128]{4,3,2,1,0:T(8,128)S(1)}, f32[4,3,8,8,128]{4,3,2,1,0:T(8,128)}, u32[]{:S(2)}) %copy-start) | copy-done | bytes 393240
  1.0 0.0 copy-start.1
  1.0 0.8 %copy-done.1 = s32[8,8,128]{2,1,0:T(8,128)S(1)} copy-done((s32[8,8,128]{2,1,0:T(8,128)S(1)}, s32[8,8,128]{2,1,0:T(8,128)}, u32[]{:S(2)}) %copy-start.1) | copy-done | bytes 32792
  1.8 0.3 shard_map.28
  2.0 3.1 %collective-permute-start = (f32[13,8,128]{2,1,0:T(8,128)S(1)}, f32[13,8,128]{2,1,0:T(8,128)S(1)}, u32[]{:S(2)}, u32[]{:S(2)}) collective-permute-start(f32[13,8,128]{2,1,0:T(8,128)S(1)} %get-tuple-element.20), channel_id=1, source_target_pairs={{0,1},{1,2},{2,3},{3,0},{4,5},{5,6},{6,7},{7,4},{8,9},{9,10},{10,1... | collective-permute-start | bytes 159752 | tf_op jit(solution)/shard_map/ppermute | solution.py:544
  5.1 2.1 %collective-permute-start.1 = (f32[13,8,128]{2,1,0:T(8,128)S(1)}, f32[13,8,128]{2,1,0:T(8,128)S(1)}, u32[]{:S(2)}, u32[]{:S(2)}) collective-permute-start(f32[13,8,128]{2,1,0:T(8,128)S(1)} %get-tuple-element.21), channel_id=1, source_target_pairs={{0,3},{1,0},{2,1},{3,2},{4,7},{5,4},{6,5},{7,6},{8,11},{9,8},{10,9... | collective-permute-start | bytes 159752 | tf_op jit(solution)/shard_map/ppermute | solution.py:544
  7.2 2.1 %collective-permute-done.l_ref = f32[13,8,128]{2,1,0:T(8,128)S(1)} collective-permute-done((f32[13,8,128]{2,1,0:T(8,128)S(1)}, f32[13,8,128]{2,1,0:T(8,128)S(1)}, u32[]{:S(2)}, u32[]{:S(2)}) %collective-permute-start) | collective-permute-done | bytes 53280 | tf_op jit(solution)/shard_map/ppermute | solution.py:544
  9.3 0.5 collective-permute-done.1.r_ref
  9.8 0.5 shard_map.29
  10.3 0.1 collective-permute-start.2
  10.3 2.6 %collective-permute-start.3 = (f32[20,8,640]{2,1,0:T(8,128)S(1)}, f32[20,8,640]{2,1,0:T(8,128)S(1)}, u32[]{:S(2)}, u32[]{:S(2)}) collective-permute-start(f32[20,8,640]{2,1,0:T(8,128)S(1)} %get-tuple-element.25), channel_id=1, source_target_pairs={{0,28},{4,0},{8,4},{12,8},{16,12},{20,16},{24,20},{28,24},{1,29},{... | collective-permute-start | bytes 1228808 | tf_op jit(solution)/shard_map/ppermute | solution.py:544
  13.0 8.1 %collective-permute-done.2.l_ref = f32[20,8,640]{2,1,0:T(8,128)S(1)} collective-permute-done((f32[20,8,640]{2,1,0:T(8,128)S(1)}, f32[20,8,640]{2,1,0:T(8,128)S(1)}, u32[]{:S(2)}, u32[]{:S(2)}) %collective-permute-start.2) | collective-permute-done | bytes 409632 | tf_op jit(solution)/shard_map/ppermute | solution.py:544
  21.1 0.0 collective-permute-done.3.r_ref
  21.1 10.4 %shard_map.30 = (f32[32,16,128]{2,1,0:T(8,128)}, f32[9,8,256]{2,1,0:T(8,128)S(1)}, f32[9,8,256]{2,1,0:T(8,128)S(1)}, f32[3,4,8,256]{3,2,1,0:T(8,128)S(1)}, f32[3...) custom-call(f32[3,8,8,640]{3,2,1,0:T(8,128)S(1)} %get-tuple-element., ...), custom_call_target="tpu_custom_call" | custom-call | tf_op jit(solution)/shard_map/pallas_call | solution.py:532
  31.5 6.1 %all-to-all-start = ((f32[32,16,128]{2,1,0:T(8,128)}), f32[32,16,128]{2,1,0:T(8,128)S(1)}, u32[]{:S(2)}, u32[]{:S(2)}) async-start(f32[32,16,128]{2,1,0:T(8,128)} %get-tuple-element.26), calls=%async_computation | async-start | bytes 524288 | tf_op jit(solution)/shard_map/all_to_all | solution.py:572
  37.6 0.3 collective-permute-start.4
  37.9 2.4 %collective-permute-start.5 = (f32[9,8,256]{2,1,0:T(8,128)S(1)}, f32[9,8,256]{2,1,0:T(8,128)S(1)}, u32[]{:S(2)}, u32[]{:S(2)}) collective-permute-start(f32[9,8,256]{2,1,0:T(8,128)S(1)} %get-tuple-element.28), channel_id=1, source_target_pairs={{0,28},{4,0},{8,4},{12,8},{16,12},{20,16},{24,20},{28,24},{1,29},{... | collective-permute-start | bytes 221192 | tf_op jit(solution)/shard_map/ppermute | solution.py:544
  40.3 3.3 %collective-permute-done.4.l_ref = f32[9,8,256]{2,1,0:T(8,128)S(1)} collective-permute-done((f32[9,8,256]{2,1,0:T(8,128)S(1)}, f32[9,8,256]{2,1,0:T(8,128)S(1)}, u32[]{:S(2)}, u32[]{:S(2)}) %collective-permute-start.4) | collective-permute-done | bytes 73760 | tf_op jit(solution)/shard_map/ppermute | solution.py:544
  43.6 0.0 collective-permute-done.5.r_ref
  43.6 4.2 %all-to-all-done.got_ref = f32[32,16,128]{2,1,0:T(8,128)S(1)} async-done(((f32[32,16,128]{2,1,0:T(8,128)}), f32[32,16,128]{2,1,0:T(8,128)S(1)}, u32[]{:S(2)}, u32[]{:S(2)}) %all-to-all-start) | async-done | bytes 262176 | tf_op jit(solution)/shard_map/all_to_all | solution.py:572
  47.8 12.9 %shard_map.31 = f32[768,128]{1,0:T(8,128)} custom-call(f32[32,16,128]{2,1,0:T(8,128)S(1)} %all-to-all-done.got_ref, f32[9,8,256]{2,1,0:T(8,128)S(1)} %collective-permute-done.4.l_ref, f32[9,8,256]{2,1,0:T(8,128)S(1)} %collective-permute-done.5.r_ref, f32[3,4,8,256]{3,2,1,0:T(8,128)S(1)} %get-tuple-element.29.x2b_ref, ...), custom_call_target="tpu_custom_call" | custom-call | tf_op jit(solution)/shard_map/pallas_call | solution.py:532
Async XLA Ops:
  0.0 1.0 %copy-start = (f32[4,3,8,8,128]{4,3,2,1,0:T(8,128)S(1)}, f32[4,3,8,8,128]{4,3,2,1,0:T(8,128)}, u32[]{:S(2)}) copy-start(f32[4,3,8,8,128]{4,3,2,1,0:T(8,128)} %param.2) | copy-start | bytes 1179652
  1.0 0.8 %copy-start.1 = (s32[8,8,128]{2,1,0:T(8,128)S(1)}, s32[8,8,128]{2,1,0:T(8,128)}, u32[]{:S(2)}) copy-start(s32[8,8,128]{2,1,0:T(8,128)} %param.3) | copy-start | bytes 98308
  2.0 7.3 %collective-permute-start = (f32[13,8,128]{2,1,0:T(8,128)S(1)}, f32[13,8,128]{2,1,0:T(8,128)S(1)}, u32[]{:S(2)}, u32[]{:S(2)}) collective-permute-start(f32[13,8,128]{2,1,0:T(8,128)S(1)} %get-tuple-element.20), channel_id=1, source_target_pairs={{0,1},{1,2},{2,3},{3,0},{4,5},{5,6},{6,7},{7,4},{8,9},{9,10},{10,1... | collective-permute-start | bytes 159752 | tf_op jit(solution)/shard_map/ppermute | solution.py:544
  5.1 4.7 %collective-permute-start.1 = (f32[13,8,128]{2,1,0:T(8,128)S(1)}, f32[13,8,128]{2,1,0:T(8,128)S(1)}, u32[]{:S(2)}, u32[]{:S(2)}) collective-permute-start(f32[13,8,128]{2,1,0:T(8,128)S(1)} %get-tuple-element.21), channel_id=1, source_target_pairs={{0,3},{1,0},{2,1},{3,2},{4,7},{5,4},{6,5},{7,6},{8,11},{9,8},{10,9... | collective-permute-start | bytes 159752 | tf_op jit(solution)/shard_map/ppermute | solution.py:544
  10.3 10.8 %collective-permute-start.2 = (f32[20,8,640]{2,1,0:T(8,128)S(1)}, f32[20,8,640]{2,1,0:T(8,128)S(1)}, u32[]{:S(2)}, u32[]{:S(2)}) collective-permute-start(f32[20,8,640]{2,1,0:T(8,128)S(1)} %get-tuple-element.24), channel_id=1, source_target_pairs={{0,4},{4,8},{8,12},{12,16},{16,20},{20,24},{24,28},{28,0},{1,5},{5... | collective-permute-start | bytes 1228808 | tf_op jit(solution)/shard_map/ppermute | solution.py:544
  10.3 10.8 %collective-permute-start.3 = (f32[20,8,640]{2,1,0:T(8,128)S(1)}, f32[20,8,640]{2,1,0:T(8,128)S(1)}, u32[]{:S(2)}, u32[]{:S(2)}) collective-permute-start(f32[20,8,640]{2,1,0:T(8,128)S(1)} %get-tuple-element.25), channel_id=1, source_target_pairs={{0,28},{4,0},{8,4},{12,8},{16,12},{20,16},{24,20},{28,24},{1,29},{... | collective-permute-start | bytes 1228808 | tf_op jit(solution)/shard_map/ppermute | solution.py:544
  31.5 16.3 %all-to-all-start = ((f32[32,16,128]{2,1,0:T(8,128)}), f32[32,16,128]{2,1,0:T(8,128)S(1)}, u32[]{:S(2)}, u32[]{:S(2)}) async-start(f32[32,16,128]{2,1,0:T(8,128)} %get-tuple-element.26), calls=%async_computation | async-start | bytes 524288 | tf_op jit(solution)/shard_map/all_to_all | solution.py:572
  37.6 6.0 %collective-permute-start.4 = (f32[9,8,256]{2,1,0:T(8,128)S(1)}, f32[9,8,256]{2,1,0:T(8,128)S(1)}, u32[]{:S(2)}, u32[]{:S(2)}) collective-permute-start(f32[9,8,256]{2,1,0:T(8,128)S(1)} %get-tuple-element.27), channel_id=1, source_target_pairs={{0,4},{4,8},{8,12},{12,16},{16,20},{20,24},{24,28},{28,0},{1,5},{5... | collective-permute-start | bytes 221192 | tf_op jit(solution)/shard_map/ppermute | solution.py:544
  37.9 5.7 %collective-permute-start.5 = (f32[9,8,256]{2,1,0:T(8,128)S(1)}, f32[9,8,256]{2,1,0:T(8,128)S(1)}, u32[]{:S(2)}, u32[]{:S(2)}) collective-permute-start(f32[9,8,256]{2,1,0:T(8,128)S(1)} %get-tuple-element.28), channel_id=1, source_target_pairs={{0,28},{4,0},{8,4},{12,8},{16,12},{20,16},{24,20},{28,24},{1,29},{... | collective-permute-start | bytes 221192 | tf_op jit(solution)/shard_map/ppermute | solution.py:544

commit v2 on v1

v2 whole, which is shorter than its diff:
```python
import functools

import jax
import jax.numpy as jnp
from jax import lax
from jax.experimental import pallas as pl
from jax.experimental.pallas import tpu as pltpu
from jax.sharding import PartitionSpec as P

RELAX = 0.6
MASS = 0.01
GRAD_DIV = 2.5
VEC, COMP, NZ, BX, BY = 4, 3, 8, 8, 128
COARSE = 6
UNROLL0, UNROLL1, UNROLL2 = 1, 2, 8
RIM = 16
LEFT = 11
PIECE = 108
SPLIT = 112
L0 = 5 * 128
K0 = 2 * 128
L1 = 2 * 128
FX = 6
CX = 7
F32 = jnp.float32


def iota(shape, dim):
    return lax.broadcasted_iota(jnp.int32, shape, dim)


def parts_of(value):
    high = value.astype(jnp.bfloat16)
    rest = value - high.astype(F32)
    mid = rest.astype(jnp.bfloat16)
    return high, mid, (rest - mid.astype(F32)).astype(jnp.bfloat16)


def exact_dot(parts, selector):
    out = [jnp.dot(p, selector, preferred_element_type=F32) for p in parts]
    return out[0] + out[1] + out[2]


class Level:
    def __init__(self, index, rows, width, kinds, length=None):
        self.scale = 0.25**index
        self.rows = rows
        self.width = width
        self.kinds = kinds
        row = iota((8, width), 0)
        self.has_zp, self.has_zm = row < 8 - rows, row >= rows
        self.has_yp = self.has_ym = None
        if length is not None:
            lane = iota((8, width), 1)
            self.has_yp, self.has_ym = lane < length - 1, lane > 0

    def lanes(self, tile):
        return pl.ds(tile * self.width, self.width)

    def yp(self, a):
        return pltpu.roll(a, self.width - 1, 1)

    def ym(self, a):
        return pltpu.roll(a, 1, 1)

    def zp(self, a):
        return pltpu.roll(a, 8 - self.rows, 0)

    def zm(self, a):
        return pltpu.roll(a, self.rows, 0)

    @staticmethod
    def keep(mask, a):
        return a if mask is None else jnp.where(mask, a, 0.0)

    def dy_of(self, up, down):
        return self.keep(self.has_yp, up) - self.keep(self.has_ym, down)

    def dz_of(self, up, down):
        return self.keep(self.has_zp, up) - self.keep(self.has_zm, down)

    @property
    def layered(self):
        return self.rows < 8

    def weights(self, coeff, at, k_ref, kat):
        gains, backs = [], []
        for kind in range(max(self.kinds) + 1):
            lanes = self.lanes(kind)
            c = coeff[at, :, lanes]
            near = [coeff[at + 1, :, lanes], coeff[at - 1, :, lanes]]
            near += [self.keep(self.has_yp, self.yp(c)), self.keep(self.has_ym, self.ym(c))]
            if self.layered:
                near += [self.keep(self.has_zp, self.zp(c)), self.keep(self.has_zm, self.zm(c))]
            total = near[0]
            for n in near[1:]:
                total = total + n
            diag = MASS + self.scale * (8.0 * c + 0.5 * total)
            gain = jnp.where(c > 0.0, RELAX / diag, 0.0)
            half = (0.5 * self.scale) * gain
            own = (GRAD_DIV * self.scale) * gain * c
            masks = [None, None, self.has_yp, self.has_ym, self.has_zp, self.has_zm]
            for i, n in enumerate(near):
                face = half * (c + n)
                k_ref[i, kat, :, lanes] = self.keep(masks[i], face)
                k_ref[6 + i, kat, :, lanes] = self.keep(masks[i], face + own)
            k_ref[12, kat, :, lanes] = 0.25 * own
            gains.append(gain)
            backs.append(diag * (1.0 / RELAX))
        return gains, backs

    def cross(self, u, at, t_ref, tat):
        for tile in range(len(self.kinds)):
            lanes = self.lanes(tile)
            uy = u[1, at, :, lanes]
            t = self.dy_of(self.yp(uy), self.ym(uy))
            if self.layered:
                uz = u[2, at, :, lanes]
                t = t + self.dz_of(self.zp(uz), self.zm(uz))
            t_ref[tat, :, lanes] = t

    def change(self, u, at, t_ref, px_ref, tat, k_ref, kat, x1, xat, write):
        for tile, kind in enumerate(self.kinds):
            lanes = self.lanes(tile)
            k = lambda i: k_ref[i, kat, :, self.lanes(kind)]
            mine = [u[c, at, :, lanes] for c in range(3)]
            fore = [u[c, at + 1, :, lanes] for c in range(3)]
            back = [u[c, at - 1, :, lanes] for c in range(3)]
            y_up = [self.yp(a) for a in mine]
            y_dn = [self.ym(a) for a in mine]
            dxx = fore[0] - back[0]
            dyy = self.dy_of(y_up[1], y_dn[1])
            side = dxx
            cross = dyy
            if self.layered:
                z_up = [self.zp(a) for a in mine]
                z_dn = [self.zm(a) for a in mine]
                dzz = self.dz_of(z_up[2], z_dn[2])
                side = dxx + dzz
                cross = dyy + dzz
            t_ref[tat, :, lanes] = cross
            mixed = [None, self.dy_of(self.yp(side), self.ym(side)), None]
            if self.layered:
                below = dxx + dyy
                mixed[2] = self.dz_of(self.zp(below), self.zm(below))
            for c in range(3):
                total = x1[c, xat, :, lanes] - RELAX * mine[c]
                total = total + (k(6 if c == 0 else 0) * fore[c] + k(7 if c == 0 else 1) * back[c])
                sides = k(8 if c == 1 else 2) * y_up[c] + k(9 if c == 1 else 3) * y_dn[c]
                if self.layered:
                    sides = sides + (k(10 if c == 2 else 4) * z_up[c] + k(11 if c == 2 else 5) * z_dn[c])
                if mixed[c] is not None:
                    sides = sides + k(12) * mixed[c]
                if c == 0:
                    px_ref[tat, :, lanes] = total + sides
                else:
                    write(c, tile, lanes, total + sides)

    def apply(self, u, uo, t_ref, px_ref, k_ref, ko, x1, xo, low, high, unroll, write):
        self.cross(u, low - 1 + uo, t_ref, 0)
        self.cross(u, high + uo, t_ref, high - low + 1)

        def one(p):
            def put(c, tile, lanes, d):
                write(c, p, tile, lanes, d)

            self.change(u, p + uo, t_ref, px_ref, p - low + 1, k_ref, p + ko, x1, p + xo, put)

        def mixed(p):
            at = p - low + 1
            for tile, kind in enumerate(self.kinds):
                lanes = self.lanes(tile)
                t = t_ref[at + 1, :, lanes] - t_ref[at - 1, :, lanes]
                write(0, p, tile, lanes, px_ref[at, :, lanes] + k_ref[12, p + ko, :, self.lanes(kind)] * t)

        each(low, high, unroll, one)
        each(low, high, 2 * unroll, mixed)


def each(low, high, unroll, body):
    count = high - low
    while count % unroll:
        unroll -= 1
    if count == unroll:
        for p in range(low, high):
            body(p)
        return

    def step(i, carry):
        for b in range(unroll):
            body(low + i * unroll + b)
        return carry

    lax.fori_loop(0, count // unroll, step, 0)


def tile_y(lane):
    return (lane & 127) - LEFT, PIECE + (lane & 31), (lane & 127) >> 5


def bf16(mask, value):
    return jnp.where(mask, value, 0.0).astype(jnp.bfloat16)


def rows_of(ref, group, x):
    return ref[pl.ds(group * 64 + x, 8, stride=8), :]


def coeff_rows(m_ref, x):
    return jnp.where(rows_of(m_ref, 0, x) == 1, 1.0, 0.05).astype(F32)


def edge_kernel(f_ref, m_ref, left_ref, right_ref):
    for x in range(BX):
        for v in range(VEC):
            for c in range(COMP):
                val = rows_of(f_ref, v * COMP + c, x)
                lanes = pl.ds((x // 4) * 64 + 16 * v, 16)
                left_ref[c * 4 + x % 4, :, lanes] = val[:, :RIM]
                right_ref[c * 4 + x % 4, :, lanes] = val[:, BY - RIM :]
        val = coeff_rows(m_ref, x)
        left_ref[12, :, pl.ds(16 * x, 16)] = val[:, :RIM]
        right_ref[12, :, pl.ds(16 * x, 16)] = val[:, BY - RIM :]


def join_kernel(gy, f_ref, m_ref, l_ref, r_ref, own_ref, left_ref, right_ref):
    place = lax.axis_index("gy")
    from_left = (place > 0).astype(F32)
    from_right = (place < gy - 1).astype(F32)
    kept = BY - PIECE

    def put(ref, at, start, piece_at, piece_start, val, left, right):
        ref[*at, :, pl.ds(start, LEFT)] = left[:, RIM - LEFT :]
        ref[*at, :, pl.ds(start + LEFT, 128 - LEFT)] = val[:, : 128 - LEFT]
        ref[*piece_at, :, pl.ds(piece_start, kept)] = val[:, PIECE:]
        ref[*piece_at, :, pl.ds(piece_start + kept, 32 - kept)] = right[:, : 32 - kept]

    for x in range(BX):
        for c in range(COMP):
            left = l_ref[c * 4 + x % 4] * from_left
            right = r_ref[c * 4 + x % 4] * from_right
            for v in range(VEC):
                at = (x // 4) * 64 + 16 * v
                val = rows_of(f_ref, v * COMP + c, x)
                place = (BX * c + x,)
                put(own_ref, place, 128 * v, place, 512 + 32 * v, val, left[:, at : at + RIM], right[:, at : at + RIM])
        left = l_ref[12, :, pl.ds(16 * x, 16)] * from_left
        right = r_ref[12, :, pl.ds(16 * x, 16)] * from_right
        base = COMP * BX
        at, piece = x, 8 + x // 4
        put(
            own_ref, (base + at // 5,), 128 * (at % 5), (base + piece // 5,), 128 * (piece % 5) + 32 * (x % 4),
            coeff_rows(m_ref, x), left, right,
        )
    for c in range(COMP):
        for x in range(FX):
            left_ref[c * FX + x] = own_ref[BX * c + x]
            right_ref[c * FX + x] = own_ref[BX * c + x + BX - FX]
    for i in range(2):
        left_ref[COMP * FX + i] = own_ref[COMP * BX + i]
        right_ref[COMP * FX + i] = own_ref[COMP * BX + i]


def down_kernel(
    gx, own_ref, l_ref, r_ref,
    pay_ref, send_l, send_r, x1, x2, k0, y1, y2, k1,
    cx, dr0, t0, p0, rest, stack, cstack, c1, dr1, f1, t1, p1, r1, stack1, pay,
):
    place = lax.axis_index("gx")
    from_left = (place > 0).astype(F32)
    from_right = (place < gx - 1).astype(F32)
    a = Level(0, 1, 128, (0, 0, 0, 0, 1))

    def spread(plane, ref, base, x, factor):
        at, piece = x, 8 + x // 4
        val = ref[base + at // 5, :, pl.ds(128 * (at % 5), 128)]
        end = ref[base + piece // 5, :, pl.ds(128 * (piece % 5) + 32 * (x % 4), 32)]
        if factor is not None:
            val, end = val * factor, end * factor
        cx[plane + CX, :, pl.ds(0, 128)] = val
        for v in range(VEC):
            cx[plane + CX, :, pl.ds(128 + 32 * v, 32)] = end

    for x in range(BX):
        spread(x, own_ref, COMP * BX, x, None)
    for x in range(CX):
        spread(x - CX, l_ref, COMP * FX, x + BX - CX, from_left)
        spread(x + BX, r_ref, COMP * FX, x, from_right)

    def start(low, high, load):
        def body(p):
            gain, back = a.weights(cx, p + CX, k0, p + FX)
            for kind in range(2):
                dr0[p + FX, :, a.lanes(kind)] = back[kind]
            for c in range(COMP):
                plane = load(c, p)
                for tile, kind in enumerate(a.kinds):
                    x1[c, p + FX, :, a.lanes(tile)] = gain[kind] * plane[:, 128 * tile : 128 * tile + 128]

        each(low, high, 2, body)

    start(-FX, 0, lambda c, p: l_ref[c * FX + p + FX])
    start(0, BX, lambda c, p: own_ref[BX * c + p])
    start(BX, BX + FX, lambda c, p: r_ref[c * FX + p - BX])

    def to_x2(c, p, tile, lanes, d):
        x2[c, p + FX, :, lanes] = x1[c, p + FX, :, lanes] + d

    a.apply(x1, FX, t0, p0, k0, FX, x1, FX, 1 - FX, BX + FX - 1, UNROLL0, to_x2)

    def to_rest(c, p, tile, lanes, d):
        rest[c, p + 4, :, lanes] = d * dr0[p + FX, :, a.lanes(a.kinds[tile])]

    a.apply(x2, FX, t0, p0, k0, FX, x1, FX, -4, BX + 4, UNROLL0, to_rest)

    for c in range(COMP):
        for i in range(8):
            plane = rest[c, 2 * i] + rest[c, 2 * i + 1]
            stack[pl.ds(64 * c + 8 * i, 8), :] = plane + a.zp(plane)
    for i in range(10):
        plane = cx[2 * i + 1] + cx[2 * i + 2]
        cstack[pl.ds(8 * i, 8), :] = plane + a.zp(plane)
    selectors = []
    row, col = iota((K0, 128), 0), iota((K0, 128), 1)
    y, y_piece, vec = tile_y(row)
    for v in range(VEC):
        own_tile = (row < 128) & (y >= -8) & (y < SPLIT) & ((y >> 1) + 32 == col)
        piece = (row >= 128) & (vec == v) & (y_piece >= SPLIT) & (y_piece < BY + 8) & ((y_piece >> 1) + 32 == col)
        selectors.append(bf16(own_tile | piece, 0.125))
    parts = parts_of(stack[...])
    coarse = [
        exact_dot([jnp.concatenate([p[:, 128 * v : 128 * v + 128], p[:, 512:]], axis=1) for p in parts], selectors[v])
        for v in range(VEC)
    ]
    coarse_c = exact_dot(parts_of(cstack[...]), selectors[0])
    even = (iota((8, 128), 0) & 1) == 0
    for c in range(COMP):
        for i in range(8):
            at = 64 * c + 8 * i
            for low in range(2):
                odd = pltpu.roll(coarse[2 + low][at : at + 8], 1, 0)
                f1[c, i, :, pl.ds(128 * low, 128)] = jnp.where(even, coarse[low][at : at + 8], odd)
    for i in range(10):
        block = coarse_c[8 * i : 8 * i + 8]
        c1[i] = jnp.where(even, block, pltpu.roll(block, 1, 0))

    b = Level(1, 2, 128, (0, 0))
    for p in range(-2, 6):
        gain, back = b.weights(c1, p + 3, k1, p + 2)
        dr1[p + 2] = back[0]
        for c in range(COMP):
            for tile in range(2):
                y1[c, p + 2, :, b.lanes(tile)] = gain[0] * f1[c, p + 2, :, b.lanes(tile)]

    def to_y2(c, p, tile, lanes, d):
        y2[c, p + 1, :, lanes] = y1[c, p + 2, :, lanes] + d

    b.apply(y1, 2, t1, p1, k1, 2, y1, 2, -1, 5, UNROLL1, to_y2)
    for c in range(COMP):
        for i in range(3):
            send_l[3 * c + i] = y2[c, 1 + i]
            send_r[3 * c + i] = y2[c, 2 + i]

    def to_r1(c, p, tile, lanes, d):
        r1[c, p, :, lanes] = d * dr1[p + 2]

    b.apply(y2, 1, t1, p1, k1, 2, y1, 2, 0, 4, UNROLL1, to_r1)

    for c in range(COMP):
        for i in range(2):
            plane = r1[c, 2 * i] + r1[c, 2 * i + 1]
            plane = plane + pltpu.roll(plane, 6, 0)
            stack1[pl.ds(8 * (2 * c + i), 8), :] = plane[:, :128]
            stack1[pl.ds(64 + 8 * (2 * c + i), 8), :] = plane[:, 128:]
    for i in range(2):
        plane = c1[2 * i + 3] + c1[2 * i + 4]
        plane = plane + b.zp(plane)
        stack1[pl.ds(8 * (6 + i), 8), :] = plane
        stack1[pl.ds(64 + 8 * (6 + i), 8), :] = plane
    lane = iota((128, 128), 0) - 32
    selector1 = bf16((lane >> 1 == iota((128, 128), 1)) & (lane >= 0) & (lane < 64), 0.125)
    coarse1 = exact_dot(parts_of(stack1[...]), selector1)
    first = (iota((8, 32), 0) & 2) == 0
    for g in range(8):
        low = coarse1[8 * g : 8 * g + 8]
        high = pltpu.roll(coarse1[64 + 8 * g : 72 + 8 * g], 2, 0)
        pay[pl.ds(8 * (g // 4), 8), pl.ds(32 * (g % 4), 32)] = jnp.where(first, low[:, :32], high[:, :32])
    packed = pay[...]

    def copy(i):
        pay_ref[i] = packed

    each(0, pay_ref.shape[0], 8, copy)


def up_kernel(
    gx, gy, got_ref, l_ref, r_ref, x1, x2, k0, y1, y2, k1, out_ref,
    c2, f2, k2, dr2, x1c, ua, ub, rc, t2, p2, s2, c3, k3, x1d, va, vb, t3, p3, s3, sw, w0, w1, t1, p1, sp, u0, u1, t0, p0,
):
    nx2, nx3 = 2 * gx, gx
    yy2, l3 = 32 * gy, c3.shape[-1]
    place_x = lax.axis_index("gx")
    place_y = lax.axis_index("gy")
    from_left = (place_x > 0).astype(F32)
    from_right = (place_x < gx - 1).astype(F32)

    zero2 = jnp.zeros((8, yy2), F32)
    for ref in (ua, ub):
        for c in range(COMP):
            for i in (0, 1, nx2 + 2, nx2 + 3):
                ref[c, i] = zero2
    c2[0] = zero2
    c2[nx2 + 1] = zero2

    def unpack(i):
        for j in range(gy):
            for g in range(8):
                block = got_ref[i * gy + j, pl.ds(8 * (g // 4), 8), pl.ds(32 * (g % 4), 32)]
                if g < 6:
                    f2[g // 2, 2 * i + g % 2, :, pl.ds(32 * j, 32)] = block
                else:
                    c2[2 * i + g - 5, :, pl.ds(32 * j, 32)] = block

    each(0, gx, 8, unpack)
    m = Level(2, 4, yy2, (0,), yy2)

    def start2(p):
        gain, back = m.weights(c2, p + 1, k2, p)
        dr2[p] = back[0]
        for c in range(COMP):
            val = gain[0] * f2[c, p]
            x1c[c, p] = val
            ua[c, p + 2] = val

    each(0, nx2, 8, start2)

    def sweep2(src, dst):
        def write(c, p, tile, lanes, d):
            dst[c, p + 2] = src[c, p + 2] + d

        m.apply(src, 2, t2, p2, k2, 0, x1c, 0, 0, nx2, UNROLL2, write)

    sweep2(ua, ub)

    def to_rc(c, p, tile, lanes, d):
        rc[c, p] = d * dr2[p]

    m.apply(ub, 2, t2, p2, k2, 0, x1c, 0, 0, nx2, UNROLL2, to_rc)

    for i in range(nx3):
        for c in range(COMP):
            plane = rc[c, 2 * i] + rc[c, 2 * i + 1]
            s2[pl.ds(8 * (c * nx3 + i), 8), :] = plane + pltpu.roll(plane, 4, 0)
        plane = c2[2 * i + 1] + c2[2 * i + 2]
        s2[pl.ds(8 * (COMP * nx3 + i), 8), :] = plane + pltpu.roll(plane, 4, 0)
    selector = bf16((iota((yy2, l3), 0) >> 1) == iota((yy2, l3), 1), 0.125)
    coarse = exact_dot(parts_of(s2[...]), selector)
    zero3 = jnp.zeros((8, l3), F32)
    for ref in (va, vb):
        for c in range(COMP):
            ref[c, 0] = zero3
            ref[c, nx3 + 1] = zero3
    c3[0] = zero3
    c3[nx3 + 1] = zero3
    for i in range(nx3):
        c3[i + 1] = coarse[8 * (COMP * nx3 + i) : 8 * (COMP * nx3 + i) + 8]
    n = Level(3, 8, l3, (0,), 16 * gy)
    for p in range(nx3):
        gain, _ = n.weights(c3, p + 1, k3, p)
        for c in range(COMP):
            val = gain[0] * coarse[8 * (c * nx3 + p) : 8 * (c * nx3 + p) + 8]
            x1d[c, p] = val
            va[c, p + 1] = val
    src, dst = va, vb
    for _ in range(COARSE - 1):

        def write3(c, p, tile, lanes, d, src=src, dst=dst):
            dst[c, p + 1] = src[c, p + 1] + d

        n.apply(src, 1, t3, p3, k3, 0, x1d, 0, 0, nx3, UNROLL2, write3)
        src, dst = dst, src
    for c in range(COMP):
        for i in range(nx3):
            s3[pl.ds(8 * (c * nx3 + i), 8), :] = src[c, i + 1]
    selector = bf16((iota((l3, yy2), 1) >> 1) == iota((l3, yy2), 0), 1.0)
    fine = exact_dot(parts_of(s3[...]), selector)
    for c in range(COMP):
        for i in range(nx3):
            block = fine[8 * (c * nx3 + i) : 8 * (c * nx3 + i) + 8]
            for j in range(2):
                ub[c, 2 * i + j + 2] = ub[c, 2 * i + j + 2] + block
    sweep2(ub, ua)
    sweep2(ua, ub)

    row = iota((8, yy2), 0)
    for c in range(COMP):
        for i in range(6):
            e = ub[c, 2 * place_x + i]
            at = 16 * (6 * c + i)
            sw[pl.ds(at, 8), :] = jnp.where((row & 2) == 0, e, pltpu.roll(e, 2, 0))
            sw[pl.ds(at + 8, 8), :] = jnp.where((row & 2) != 0, e, pltpu.roll(e, 6, 0))
    y1g = place_y * 64 + iota((yy2, 128), 1) - 32
    fine = exact_dot(parts_of(sw[...]), bf16((y1g >> 1) == iota((yy2, 128), 0), 1.0))
    for c in range(COMP):
        for p in range(-3, 7):
            if p < 0:
                val = l_ref[3 * c + p + 3] * from_left
            elif p < 4:
                val = y2[c, p + 1]
            else:
                val = r_ref[3 * c + p - 4] * from_right
            at = 16 * (6 * c + (p + 4) // 2)
            w0[c, p + 3] = val + jnp.concatenate([fine[at : at + 8], fine[at + 8 : at + 16]], axis=1)
    b = Level(1, 2, 128, (0, 0))

    def write1(c, p, tile, lanes, d):
        w1[c, p + 3, :, lanes] = w0[c, p + 3, :, lanes] + d

    b.apply(w0, 3, t1, p1, k1, 2, y1, 2, -2, 6, UNROLL1, write1)
    odd = (iota((8, 128), 0) & 1) != 0

    def write1b(c, p, tile, lanes, d):
        e = w1[c, p + 3, :, lanes] + d
        rows = pl.ds(8 * (6 * c + p + 1), 8)
        sp[tile, rows, :] = jnp.where(odd, pltpu.roll(e, 1, 0), e)
        sp[2 + tile, rows, :] = jnp.where(odd, e, pltpu.roll(e, 7, 0))

    b.apply(w1, 3, t1, p1, k1, 2, y1, 2, -1, 5, 6, write1b)

    col = iota((128, K0), 1)
    y, y_piece, vec = tile_y(col)
    piece = None
    for v in range(VEC):
        parent = jnp.where(col < 128, y >> 1, y_piece >> 1) + 32
        selector = bf16((parent == iota((128, K0), 0)) & ((col < 128) | (vec == v)), 1.0)
        fine = exact_dot(parts_of(sp[v]), selector)
        piece = fine[:, 128:] if v == 0 else piece + fine[:, 128:]
        for c in range(COMP):
            for i in range(6):
                at = 8 * (6 * c + i)
                for j in range(2):
                    u0[c, 2 * i + j, :, pl.ds(128 * v, 128)] = x2[c, 2 * i + j + 4, :, pl.ds(128 * v, 128)] + fine[at : at + 8, :128]
    for c in range(COMP):
        for i in range(6):
            at = 8 * (6 * c + i)
            for j in range(2):
                u0[c, 2 * i + j, :, pl.ds(512, 128)] = x2[c, 2 * i + j + 4, :, pl.ds(512, 128)] + piece[at : at + 8]
    a = Level(0, 1, 128, (0, 0, 0, 0, 1))

    def write0(c, p, tile, lanes, d):
        u1[c, p + 2, :, lanes] = u0[c, p + 2, :, lanes] + d

    a.apply(u0, 2, t0, p0, k0, FX, x1, FX, -1, 9, UNROLL0, write0)

    def write_last(c, p, tile, lanes, d):
        u0[c, p + 2, :, lanes] = u1[c, p + 2, :, lanes] + d

    a.apply(u1, 2, t0, p0, k0, FX, x1, FX, 0, BX, UNROLL0, write_last)
    near = iota((8, 128), 1) < SPLIT
    for x in range(BX):
        for c in range(COMP):
            last = u0[c, x + 2, :, pl.ds(512, 128)]
            for v in range(VEC):
                main = pltpu.roll(u0[c, x + 2, :, pl.ds(128 * v, 128)], 128 - LEFT, 1)
                ends = pltpu.roll(last, (PIECE - 32 * v) % 128, 1)
                out_ref[pl.ds((v * COMP + c) * 64 + x, 8, stride=8), :] = jnp.where(near, main, ends)


def call(kernel, outs, scratch, *args):
    vmem = pl.BlockSpec(memory_space=pltpu.VMEM)
    shapes = [jax.ShapeDtypeStruct(s, F32) for s in outs]
    return pl.pallas_call(
        kernel,
        out_shape=shapes,
        in_specs=[vmem] * len(args),
        out_specs=[vmem] * len(outs),
        scratch_shapes=[pltpu.VMEM(s, F32) for s in scratch],
        compiler_params=pltpu.CompilerParams(vmem_limit_bytes=32 * 1024 * 1024),
    )(*args)


def per_device(gx, gy, right_side, material):
    def ring(value, axis, size, step):
        return lax.ppermute(value, axis, [(i, (i + step) % size) for i in range(size)])

    f = right_side.reshape(VEC * COMP * NZ * BX, BY)
    m = material.reshape(NZ * BX, BY)
    edge = (13, 8, 128)
    to_left, to_right = call(edge_kernel, [edge, edge], [], f, m)
    right = ring(to_left, "gy", gy, -1)
    left = ring(to_right, "gy", gy, 1)
    side = (COMP * FX + 2, 8, L0)
    own, to_left, to_right = call(
        functools.partial(join_kernel, gy), [(COMP * BX + 2, 8, L0), side, side], [], f, m, left, right
    )
    right = ring(to_left, "gx", gx, -1)
    left = ring(to_right, "gx", gx, 1)
    n = gx * gy
    plane = lambda *lead: (*lead, 8, L0)
    plane1 = lambda *lead: (*lead, 8, L1)
    nf, nc = BX + 2 * FX, BX + 2 * CX
    pay, to_left, to_right, *kept = call(
        functools.partial(down_kernel, gx),
        [
            (n, 16, 128), plane1(9), plane1(9), plane(3, nf), plane(3, nf), (13, nf, 8, K0), plane1(3, 8), plane1(3, 6), (13, 8, 8, 128),
        ],
        [
            (nc, 8, K0), (nf, 8, K0), plane(nf), plane(nf), plane(3, 16), (192, L0), (80, K0), (10, 8, 128),
            (8, 8, 128), plane1(3, 8), plane1(10), plane1(10), plane1(3, 4), (128, 128), (16, 128),
        ],
        own, left, right,
    )
    right = ring(to_left, "gx", gx, -1)
    left = ring(to_right, "gx", gx, 1)
    got = lax.all_to_all(pay, ("gx", "gy"), 0, 0)
    nx2, nx3, y2, l3 = 2 * gx, gx, 32 * gy, max(128, 16 * gy)
    plane2 = lambda *lead: (*lead, 8, y2)
    plane3 = lambda *lead: (*lead, 8, l3)
    (out,) = call(
        functools.partial(up_kernel, gx, gy),
        [(VEC * COMP * NZ * BX, BY)],
        [
            plane2(nx2 + 2), plane2(3, nx2), plane2(13, nx2), plane2(nx2), plane2(3, nx2), plane2(3, nx2 + 4), plane2(3, nx2 + 4),
            plane2(3, nx2), plane2(nx2 + 2), plane2(nx2 + 2), (32 * nx3, y2),
            plane3(nx3 + 2), plane3(13, nx3), plane3(3, nx3), plane3(3, nx3 + 2), plane3(3, nx3 + 2), plane3(nx3 + 2), plane3(nx3 + 2),
            (24 * nx3, l3), (288, y2), plane1(3, 10), plane1(3, 10), plane1(10), plane1(10), (4, 144, 128),
            plane(3, 12), plane(3, 12), plane(12), plane(12),
        ],
        got, left, right, *kept,
    )
    return out.reshape(right_side.shape)


def solution(mesh):
    gx, gy = mesh.shape["gx"], mesh.shape["gy"]
    spec = P(None, None, None, "gx", "gy")
    return jax.shard_map(
        functools.partial(per_device, gx, gy), mesh=mesh, in_specs=(spec, P(None, "gx", "gy")), out_specs=spec, check_vma=False
    )
```

time: 61 us -> 64.2 us (1.052)
  local copies, waits for them, and re-layouts: 1.75 us -> 13.2 us
  Pallas kernels: 24 us -> 16.7 us
  waiting for transfers between devices: 18.2 us -> 17 us
    unnamed x4 -> x32, local copies, waits for them, and re-layouts: 1.75 us -> 13.2 us
    pallas_call x4, Pallas kernels: 24 us -> 16.7 us  [call(): pl.pallas_call(kernel, out_shape=shapes, in_specs=[vmem] * len(args), out...]
    all_to_all x1, waiting for transfers between devices: 4.19 us -> 2.7 us  [per_device(): got = lax.all_to_all(pay, ('gx', 'gy'), 0, 0)]
where the time goes in v2:
time: 64.2 us; the launch traced here: 63.7 us
  waiting for transfers between devices  17 us (26%)
  starting transfers between devices  16.8 us (26%)
  Pallas kernels  16.7 us (26%)
  local copies, waits for them, and re-layouts  13.2 us (21%)
    pallas_call x4, Pallas kernels, call(): pl.pallas_call(kernel, out_shape=shapes, in_specs=[vmem] * len(args), out...  16.7 us
    ppermute x6, waiting for transfers between devices, ring(): lax.ppermute(value, axis, [(i, (i + step) % size) for i in range(size)])  14.3 us
    unnamed x32, local copies, waits for them, and re-layouts  13.2 us
    ppermute x6, starting transfers between devices, ring(): lax.ppermute(value, axis, [(i, (i + step) % size) for i in range(size)])  10.6 us
    all_to_all x1, starting transfers between devices, per_device(): got = lax.all_to_all(pay, ('gx', 'gy'), 0, 0)  6.27 us
    all_to_all x1, waiting for transfers between devices, per_device(): got = lax.all_to_all(pay, ('gx', 'gy'), 0, 0)  2.7 us
  transfers between devices with their start and end apart: 7, of which 5 were waited for; matrix products, arithmetic and copies ran while one was open for 0% of the time, Pallas kernels for 0%

profile of v2, /device:TPU:0, one launch (start us, length us, event | category | flops | bytes accessed | tf_op | source)
XLA Modules:
  0.0 63.7 jit_solution(11669142772548108400)
XLA Ops:
  0.0 0.0 copy-start
  0.0 1.0 %copy-done = f32[4,3,8,8,128]{4,3,2,1,0:T(8,128)S(1)} copy-done((f32[4,3,8,8,128]{4,3,2,1,0:T(8,128)S(1)}, f32[4,3,8,8,128]{4,3,2,1,0:T(8,128)}, u32[]{:S(2)}) %copy-start) | copy-done | bytes 393240
  1.0 0.0 copy-start.8
  1.0 0.8 %copy-done.8 = s32[8,8,128]{2,1,0:T(8,128)S(1)} copy-done((s32[8,8,128]{2,1,0:T(8,128)S(1)}, s32[8,8,128]{2,1,0:T(8,128)}, u32[]{:S(2)}) %copy-start.8) | copy-done | bytes 32792
  1.8 0.3 shard_map.28
  2.0 3.1 %collective-permute-start = (f32[13,8,128]{2,1,0:T(8,128)S(1)}, f32[13,8,128]{2,1,0:T(8,128)S(1)}, u32[]{:S(2)}, u32[]{:S(2)}) collective-permute-start(f32[13,8,128]{2,1,0:T(8,128)S(1)} %get-tuple-element.19), channel_id=1, source_target_pairs={{0,1},{1,2},{2,3},{3,0},{4,5},{5,6},{6,7},{7,4},{8,9},{9,10},{10,1... | collective-permute-start | bytes 159752 | tf_op jit(solution)/shard_map/ppermute | solution.py:584
  5.1 2.1 %collective-permute-start.1 = (f32[13,8,128]{2,1,0:T(8,128)S(1)}, f32[13,8,128]{2,1,0:T(8,128)S(1)}, u32[]{:S(2)}, u32[]{:S(2)}) collective-permute-start(f32[13,8,128]{2,1,0:T(8,128)S(1)} %get-tuple-element.20), channel_id=1, source_target_pairs={{0,3},{1,0},{2,1},{3,2},{4,7},{5,4},{6,5},{7,6},{8,11},{9,8},{10,9... | collective-permute-start | bytes 159752 | tf_op jit(solution)/shard_map/ppermute | solution.py:584
  7.2 2.1 %collective-permute-done.l_ref = f32[13,8,128]{2,1,0:T(8,128)S(1)} collective-permute-done((f32[13,8,128]{2,1,0:T(8,128)S(1)}, f32[13,8,128]{2,1,0:T(8,128)S(1)}, u32[]{:S(2)}, u32[]{:S(2)}) %collective-permute-start) | collective-permute-done | bytes 53280 | tf_op jit(solution)/shard_map/ppermute | solution.py:584
  9.3 0.5 collective-permute-done.1.r_ref
  9.8 0.0 copy-start.9
  9.8 0.8 %copy-done.9 = s32[8,8,128]{2,1,0:T(8,128)S(1)} copy-done((s32[8,8,128]{2,1,0:T(8,128)S(1)}, s32[8,8,128]{2,1,0:T(8,128)}, u32[]{:S(2)}) %copy-start.9) | copy-done | bytes 32792
  10.6 0.7 %shard_map.29 = (f32[26,8,640]{2,1,0:T(8,128)S(1)}, f32[20,8,640]{2,1,0:T(8,128)S(1)}, f32[20,8,640]{2,1,0:T(8,128)S(1)}) custom-call(f32[768,128]{1,0:T(8,128)S(1)} %bitcast.4, s32[64,128]{1,0:T(8,128)S(1)} %bitcast.6, f32[13,8,128]{2,1,0:T(8,128)S(1)} %collective-permute-done.l_ref, f32[13,8,128]{2,1,0:T(8,128)S(1)} %collective-permute-done.1.r_ref), custom_call_target="tpu_custom_call" | custom-call | tf_op jit(solution)/shard_map/pallas_call | solution.py:572
  11.2 0.1 collective-permute-start.2
  11.3 2.6 %collective-permute-start.3 = (f32[20,8,640]{2,1,0:T(8,128)S(1)}, f32[20,8,640]{2,1,0:T(8,128)S(1)}, u32[]{:S(2)}, u32[]{:S(2)}) collective-permute-start(f32[20,8,640]{2,1,0:T(8,128)S(1)} %get-tuple-element.23), channel_id=1, source_target_pairs={{0,28},{4,0},{8,4},{12,8},{16,12},{20,16},{24,20},{28,24},{1,29},{... | collective-permute-start | bytes 1228808 | tf_op jit(solution)/shard_map/ppermute | solution.py:584
  13.9 8.1 %collective-permute-done.2.l_ref = f32[20,8,640]{2,1,0:T(8,128)S(1)} collective-permute-done((f32[20,8,640]{2,1,0:T(8,128)S(1)}, f32[20,8,640]{2,1,0:T(8,128)S(1)}, u32[]{:S(2)}, u32[]{:S(2)}) %collective-permute-start.2) | collective-permute-done | bytes 409632 | tf_op jit(solution)/shard_map/ppermute | solution.py:584
  22.0 0.0 collective-permute-done.3.r_ref
  22.1 7.2 %shard_map.30 = (f32[32,16,128]{2,1,0:T(8,128)S(1)}, f32[9,8,256]{2,1,0:T(8,128)S(1)}, f32[9,8,256]{2,1,0:T(8,128)S(1)}, f32[3,20,8,640]{3,2,1,0:T(8,128)S(1)}, ...) custom-call(f32[26,8,640]{2,1,0:T(8,128)S(1)} %get-tuple-element.21., ...), custom_call_target="tpu_custom_call" | custom-call | tf_op jit(solution)/shard_map/pallas_call | solution.py:572
  29.3 0.0 copy-start.1
  29.3 1.0 %copy-done.1 = f32[3,20,8,640]{3,2,1,0:T(8,128)} copy-done((f32[3,20,8,640]{3,2,1,0:T(8,128)}, f32[3,20,8,640]{3,2,1,0:T(8,128)S(1)}, u32[]{:S(2)}) %copy-start.1) | copy-done | bytes 1228824
  30.3 0.0 copy-start.3
  30.3 0.8 %copy-done.3 = f32[13,8,8,128]{3,2,1,0:T(8,128)} copy-done((f32[13,8,8,128]{3,2,1,0:T(8,128)}, f32[13,8,8,128]{3,2,1,0:T(8,128)S(1)}, u32[]{:S(2)}) %copy-start.3) | copy-done | bytes 426008
  31.1 0.0 copy-start.5
  31.1 0.7 %copy-done.5 = f32[32,16,128]{2,1,0:T(8,128)} copy-done((f32[32,16,128]{2,1,0:T(8,128)}, f32[32,16,128]{2,1,0:T(8,128)S(1)}, u32[]{:S(2)}) %copy-start.5) | copy-done | bytes 262168
  31.8 0.0 copy-start.6
  31.8 0.7 %copy-done.6 = f32[3,6,8,256]{3,2,1,0:T(8,128)} copy-done((f32[3,6,8,256]{3,2,1,0:T(8,128)}, f32[3,6,8,256]{3,2,1,0:T(8,128)S(1)}, u32[]{:S(2)}) %copy-start.6) | copy-done | bytes 147480
  32.5 0.6 copy-done.14
  33.1 0.0 copy-start.15
  33.1 0.6 copy-done.15
  33.7 6.3 %all-to-all-start = ((f32[32,16,128]{2,1,0:T(8,128)}), f32[32,16,128]{2,1,0:T(8,128)}, u32[]{:S(2)}, u32[]{:S(2)}) async-start(f32[32,16,128]{2,1,0:T(8,128)} %copy-done.5), calls=%async_computation | async-start | bytes 524288 | tf_op jit(solution)/shard_map/all_to_all | solution.py:615
  40.0 0.2 collective-permute-start.4
  40.2 2.5 %collective-permute-start.5 = (f32[9,8,256]{2,1,0:T(8,128)}, f32[9,8,256]{2,1,0:T(8,128)S(1)}, u32[]{:S(2)}, u32[]{:S(2)}) collective-permute-start(f32[9,8,256]{2,1,0:T(8,128)} %copy-done.14), channel_id=1, source_target_pairs={{0,28},{4,0},{8,4},{12,8},{16,12},{20,16},{24,20},{28,24},{1,29},{... | collective-permute-start | bytes 221192 | tf_op jit(solution)/shard_map/ppermute | solution.py:584
  42.7 3.5 %collective-permute-done.4.l_ref = f32[9,8,256]{2,1,0:T(8,128)S(1)} collective-permute-done((f32[9,8,256]{2,1,0:T(8,128)}, f32[9,8,256]{2,1,0:T(8,128)S(1)}, u32[]{:S(2)}, u32[]{:S(2)}) %collective-permute-start.4) | collective-permute-done | bytes 73760 | tf_op jit(solution)/shard_map/ppermute | solution.py:584
  46.2 0.0 copy-start.10
  46.2 0.6 copy-done.10
  46.8 0.0 collective-permute-done.5.r_ref
  46.8 0.0 copy-start.12
  46.8 0.6 copy-done.12
  47.5 2.7 %all-to-all-done.got_ref = f32[32,16,128]{2,1,0:T(8,128)} async-done(((f32[32,16,128]{2,1,0:T(8,128)}), f32[32,16,128]{2,1,0:T(8,128)}, u32[]{:S(2)}, u32[]{:S(2)}) %all-to-all-start) | async-done | bytes 262176 | tf_op jit(solution)/shard_map/all_to_all | solution.py:615
  50.2 0.0 copy-start.2
  50.2 1.3 %copy-done.2 = f32[3,20,8,640]{3,2,1,0:T(8,128)S(1)} copy-done((f32[3,20,8,640]{3,2,1,0:T(8,128)S(1)}, f32[3,20,8,640]{3,2,1,0:T(8,128)}, u32[]{:S(2)}) %copy-start.2) | copy-done | bytes 1228824
  51.4 0.0 copy-start.4
  51.4 1.0 %copy-done.4 = f32[13,8,8,128]{3,2,1,0:T(8,128)S(1)} copy-done((f32[13,8,8,128]{3,2,1,0:T(8,128)S(1)}, f32[13,8,8,128]{3,2,1,0:T(8,128)}, u32[]{:S(2)}) %copy-start.4) | copy-done | bytes 426008
  52.4 0.0 copy-start.7
  52.4 0.9 %copy-done.7 = f32[3,6,8,256]{3,2,1,0:T(8,128)S(1)} copy-done((f32[3,6,8,256]{3,2,1,0:T(8,128)S(1)}, f32[3,6,8,256]{3,2,1,0:T(8,128)}, u32[]{:S(2)}) %copy-start.7) | copy-done | bytes 147480
  53.4 0.0 copy-start.11
  53.4 0.9 %copy-done.11 = f32[9,8,256]{2,1,0:T(8,128)S(1)} copy-done((f32[9,8,256]{2,1,0:T(8,128)S(1)}, f32[9,8,256]{2,1,0:T(8,128)}, u32[]{:S(2)}) %copy-start.11) | copy-done | bytes 73752
  54.2 0.9 %copy-done.13 = f32[9,8,256]{2,1,0:T(8,128)S(1)} copy-done((f32[9,8,256]{2,1,0:T(8,128)S(1)}, f32[9,8,256]{2,1,0:T(8,128)}, u32[]{:S(2)}) %copy-start.13) | copy-done | bytes 73752
  55.1 8.5 %shard_map.31 = f32[768,128]{1,0:T(8,128)} custom-call(f32[32,16,128]{2,1,0:T(8,128)} %all-to-all-done.got_ref, f32[9,8,256]{2,1,0:T(8,128)S(1)} %copy-done.11, f32[9,8,256]{2,1,0:T(8,128)S(1)} %copy-done.13, f32[3,20,8,640]{3,2,1,0:T(8,128)S(1)} %get-tuple-element.27.x1, f32[3,20,8,640]{3,2,1,0:T(8,128)S(1)} %copy-done.2, ...), custom_call_target="tpu_custom_call" | custom-call | tf_op jit(solution)/shard_map/pallas_call | solution.py:572
  (2 shorter events, 0.0 us)
Async XLA Ops:
  0.0 1.0 %copy-start = (f32[4,3,8,8,128]{4,3,2,1,0:T(8,128)S(1)}, f32[4,3,8,8,128]{4,3,2,1,0:T(8,128)}, u32[]{:S(2)}) copy-start(f32[4,3,8,8,128]{4,3,2,1,0:T(8,128)} %param.2) | copy-start | bytes 1179652
  1.0 0.8 %copy-start.8 = (s32[8,8,128]{2,1,0:T(8,128)S(1)}, s32[8,8,128]{2,1,0:T(8,128)}, u32[]{:S(2)}) copy-start(s32[8,8,128]{2,1,0:T(8,128)} %param.3) | copy-start | bytes 98308
  2.0 7.3 %collective-permute-start = (f32[13,8,128]{2,1,0:T(8,128)S(1)}, f32[13,8,128]{2,1,0:T(8,128)S(1)}, u32[]{:S(2)}, u32[]{:S(2)}) collective-permute-start(f32[13,8,128]{2,1,0:T(8,128)S(1)} %get-tuple-element.19), channel_id=1, source_target_pairs={{0,1},{1,2},{2,3},{3,0},{4,5},{5,6},{6,7},{7,4},{8,9},{9,10},{10,1... | collective-permute-start | bytes 159752 | tf_op jit(solution)/shard_map/ppermute | solution.py:584
  5.1 4.7 %collective-permute-start.1 = (f32[13,8,128]{2,1,0:T(8,128)S(1)}, f32[13,8,128]{2,1,0:T(8,128)S(1)}, u32[]{:S(2)}, u32[]{:S(2)}) collective-permute-start(f32[13,8,128]{2,1,0:T(8,128)S(1)} %get-tuple-element.20), channel_id=1, source_target_pairs={{0,3},{1,0},{2,1},{3,2},{4,7},{5,4},{6,5},{7,6},{8,11},{9,8},{10,9... | collective-permute-start | bytes 159752 | tf_op jit(solution)/shard_map/ppermute | solution.py:584
  9.8 0.8 %copy-start.9 = (s32[8,8,128]{2,1,0:T(8,128)S(1)}, s32[8,8,128]{2,1,0:T(8,128)}, u32[]{:S(2)}) copy-start(s32[8,8,128]{2,1,0:T(8,128)} %param.3) | copy-start | bytes 98308
  11.2 10.8 %collective-permute-start.2 = (f32[20,8,640]{2,1,0:T(8,128)S(1)}, f32[20,8,640]{2,1,0:T(8,128)S(1)}, u32[]{:S(2)}, u32[]{:S(2)}) collective-permute-start(f32[20,8,640]{2,1,0:T(8,128)S(1)} %get-tuple-element.22), channel_id=1, source_target_pairs={{0,4},{4,8},{8,12},{12,16},{16,20},{20,24},{24,28},{28,0},{1,5},{5... | collective-permute-start | bytes 1228808 | tf_op jit(solution)/shard_map/ppermute | solution.py:584
  11.3 10.8 %collective-permute-start.3 = (f32[20,8,640]{2,1,0:T(8,128)S(1)}, f32[20,8,640]{2,1,0:T(8,128)S(1)}, u32[]{:S(2)}, u32[]{:S(2)}) collective-permute-start(f32[20,8,640]{2,1,0:T(8,128)S(1)} %get-tuple-element.23), channel_id=1, source_target_pairs={{0,28},{4,0},{8,4},{12,8},{16,12},{20,16},{24,20},{28,24},{1,29},{... | collective-permute-start | bytes 1228808 | tf_op jit(solution)/shard_map/ppermute | solution.py:584
  29.3 1.1 %copy-start.1 = (f32[3,20,8,640]{3,2,1,0:T(8,128)}, f32[3,20,8,640]{3,2,1,0:T(8,128)S(1)}, u32[]{:S(2)}) copy-start(f32[3,20,8,640]{3,2,1,0:T(8,128)S(1)} %get-tuple-element.28.x2) | copy-start | bytes 3686404
  30.3 0.8 %copy-start.3 = (f32[13,8,8,128]{3,2,1,0:T(8,128)}, f32[13,8,8,128]{3,2,1,0:T(8,128)S(1)}, u32[]{:S(2)}) copy-start(f32[13,8,8,128]{3,2,1,0:T(8,128)S(1)} %get-tuple-element.32.k1) | copy-start | bytes 1277956
  31.1 0.7 %copy-start.5 = (f32[32,16,128]{2,1,0:T(8,128)}, f32[32,16,128]{2,1,0:T(8,128)S(1)}, u32[]{:S(2)}) copy-start(f32[32,16,128]{2,1,0:T(8,128)S(1)} %get-tuple-element.24) | copy-start | bytes 786436
  31.8 0.7 %copy-start.6 = (f32[3,6,8,256]{3,2,1,0:T(8,128)}, f32[3,6,8,256]{3,2,1,0:T(8,128)S(1)}, u32[]{:S(2)}) copy-start(f32[3,6,8,256]{3,2,1,0:T(8,128)S(1)} %get-tuple-element.31.y2) | copy-start | bytes 442372
  32.5 0.6 copy-start.14
  33.1 0.6 copy-start.15
  33.7 16.5 %all-to-all-start = ((f32[32,16,128]{2,1,0:T(8,128)}), f32[32,16,128]{2,1,0:T(8,128)}, u32[]{:S(2)}, u32[]{:S(2)}) async-start(f32[32,16,128]{2,1,0:T(8,128)} %copy-done.5), calls=%async_computation | async-start | bytes 524288 | tf_op jit(solution)/shard_map/all_to_all | solution.py:615
  40.0 6.2 %collective-permute-start.4 = (f32[9,8,256]{2,1,0:T(8,128)}, f32[9,8,256]{2,1,0:T(8,128)S(1)}, u32[]{:S(2)}, u32[]{:S(2)}) collective-permute-start(f32[9,8,256]{2,1,0:T(8,128)} %copy-done.15), channel_id=1, source_target_pairs={{0,4},{4,8},{8,12},{12,16},{16,20},{20,24},{24,28},{28,0},{1,5},{5... | collective-permute-start | bytes 221192 | tf_op jit(solution)/shard_map/ppermute | solution.py:584
  40.2 6.6 %collective-permute-start.5 = (f32[9,8,256]{2,1,0:T(8,128)}, f32[9,8,256]{2,1,0:T(8,128)S(1)}, u32[]{:S(2)}, u32[]{:S(2)}) collective-permute-start(f32[9,8,256]{2,1,0:T(8,128)} %copy-done.14), channel_id=1, source_target_pairs={{0,28},{4,0},{8,4},{12,8},{16,12},{20,16},{24,20},{28,24},{1,29},{... | collective-permute-start | bytes 221192 | tf_op jit(solution)/shard_map/ppermute | solution.py:584
  46.2 0.6 copy-start.10
  46.8 0.6 copy-start.12
  50.2 1.3 %copy-start.2 = (f32[3,20,8,640]{3,2,1,0:T(8,128)S(1)}, f32[3,20,8,640]{3,2,1,0:T(8,128)}, u32[]{:S(2)}) copy-start(f32[3,20,8,640]{3,2,1,0:T(8,128)} %copy-done.1) | copy-start | bytes 3686404
  51.4 1.0 %copy-start.4 = (f32[13,8,8,128]{3,2,1,0:T(8,128)S(1)}, f32[13,8,8,128]{3,2,1,0:T(8,128)}, u32[]{:S(2)}) copy-start(f32[13,8,8,128]{3,2,1,0:T(8,128)} %copy-done.3) | copy-start | bytes 1277956
  52.4 0.9 %copy-start.7 = (f32[3,6,8,256]{3,2,1,0:T(8,128)S(1)}, f32[3,6,8,256]{3,2,1,0:T(8,128)}, u32[]{:S(2)}) copy-start(f32[3,6,8,256]{3,2,1,0:T(8,128)} %copy-done.6) | copy-start | bytes 442372
  53.4 0.9 %copy-start.11 = (f32[9,8,256]{2,1,0:T(8,128)S(1)}, f32[9,8,256]{2,1,0:T(8,128)}, u32[]{:S(2)}) copy-start(f32[9,8,256]{2,1,0:T(8,128)} %copy-done.10) | copy-start | bytes 221188
  54.2 0.9 %copy-start.13 = (f32[9,8,256]{2,1,0:T(8,128)S(1)}, f32[9,8,256]{2,1,0:T(8,128)}, u32[]{:S(2)}) copy-start(f32[9,8,256]{2,1,0:T(8,128)} %copy-done.12) | copy-start | bytes 221188

commit v3 on v2

--- a/solution.py
+++ b/solution.py
@@ -12,7 +12,7 @@
 GRAD_DIV = 2.5
 VEC, COMP, NZ, BX, BY = 4, 3, 8, 8, 128
 COARSE = 6
-UNROLL0, UNROLL1, UNROLL2 = 1, 2, 8
+UNROLL0, UNROLL1, UNROLL2 = 4, 4, 16
 RIM = 16
 LEFT = 11
 PIECE = 108
@@ -210,7 +210,12 @@
     return jnp.where(rows_of(m_ref, 0, x) == 1, 1.0, 0.05).astype(F32)
 
 
-def edge_kernel(f_ref, m_ref, left_ref, right_ref):
+def edge_kernel(f_hbm, m_hbm, left_ref, right_ref, f_ref, m_ref, sems):
+    copies = [pltpu.make_async_copy(m_hbm, m_ref, sems.at[0]), pltpu.make_async_copy(f_hbm, f_ref, sems.at[1])]
+    for copy in copies:
+        copy.start()
+    for copy in copies:
+        copy.wait()
     for x in range(BX):
         for v in range(VEC):
             for c in range(COMP):
@@ -263,8 +268,8 @@
 
 def down_kernel(
     gx, own_ref, l_ref, r_ref,
-    pay_ref, send_l, send_r, x1, x2, k0, y1, y2, k1,
-    cx, dr0, t0, p0, rest, stack, cstack, c1, dr1, f1, t1, p1, r1, stack1, pay,
+    pay_ref, send_l, send_r, x1_ref, x2_ref, c0_ref, y1, y2_ref, k1,
+    x1, x2, k0, y2, cx, dr0, t0, p0, rest, stack, cstack, c1, dr1, f1, t1, p1, r1, stack1, pay,
 ):
     place = lax.axis_index("gx")
     from_left = (place > 0).astype(F32)
@@ -324,8 +329,8 @@
     row, col = iota((K0, 128), 0), iota((K0, 128), 1)
     y, y_piece, vec = tile_y(row)
     for v in range(VEC):
-        own_tile = (row < 128) & (y >= -8) & (y < SPLIT) & ((y >> 1) + 32 == col)
-        piece = (row >= 128) & (vec == v) & (y_piece >= SPLIT) & (y_piece < BY + 8) & ((y_piece >> 1) + 32 == col)
+        own_tile = (row < 128) & (y >= -10) & (y < SPLIT) & ((y >> 1) + 32 == col)
+        piece = (row >= 128) & (vec == v) & (y_piece >= SPLIT) & (y_piece < BY + 10) & ((y_piece >> 1) + 32 == col)
         selectors.append(bf16(own_tile | piece, 0.125))
     parts = parts_of(stack[...])
     coarse = [
@@ -391,11 +396,20 @@
         pay_ref[i] = packed
 
     each(0, pay_ref.shape[0], 8, copy)
+    for c in range(COMP):
+        for i in range(10):
+            x1_ref[c, i] = x1[c, i + 5]
+        for i in range(12):
+            x2_ref[c, i] = x2[c, i + 4]
+        for i in range(4):
+            y2_ref[c, i] = y2[c, i + 1]
+    for i in range(12):
+        c0_ref[i] = cx[i + 5]
 
 
 def up_kernel(
-    gx, gy, got_ref, l_ref, r_ref, x1, x2, k0, y1, y2, k1, out_ref,
-    c2, f2, k2, dr2, x1c, ua, ub, rc, t2, p2, s2, c3, k3, x1d, va, vb, t3, p3, s3, sw, w0, w1, t1, p1, sp, u0, u1, t0, p0,
+    gx, gy, got_ref, l_ref, r_ref, x1, x2, c0_ref, y1, y2, k1, out_ref,
+    c2, f2, k2, dr2, x1c, ua, ub, rc, t2, p2, s2, c3, k3, x1d, va, vb, t3, p3, s3, sw, w0, w1, t1, p1, sp, k0, u0, u1, t0, p0,
 ):
     nx2, nx3 = 2 * gx, gx
     yy2, l3 = 32 * gy, c3.shape[-1]
@@ -506,7 +520,7 @@
             if p < 0:
                 val = l_ref[3 * c + p + 3] * from_left
             elif p < 4:
-                val = y2[c, p + 1]
+                val = y2[c, p]
             else:
                 val = r_ref[3 * c + p - 4] * from_right
             at = 16 * (6 * c + (p + 4) // 2)
@@ -539,23 +553,24 @@
             for i in range(6):
                 at = 8 * (6 * c + i)
                 for j in range(2):
-                    u0[c, 2 * i + j, :, pl.ds(128 * v, 128)] = x2[c, 2 * i + j + 4, :, pl.ds(128 * v, 128)] + fine[at : at + 8, :128]
+                    u0[c, 2 * i + j, :, pl.ds(128 * v, 128)] = x2[c, 2 * i + j, :, pl.ds(128 * v, 128)] + fine[at : at + 8, :128]
     for c in range(COMP):
         for i in range(6):
             at = 8 * (6 * c + i)
             for j in range(2):
-                u0[c, 2 * i + j, :, pl.ds(512, 128)] = x2[c, 2 * i + j + 4, :, pl.ds(512, 128)] + piece[at : at + 8]
+                u0[c, 2 * i + j, :, pl.ds(512, 128)] = x2[c, 2 * i + j, :, pl.ds(512, 128)] + piece[at : at + 8]
     a = Level(0, 1, 128, (0, 0, 0, 0, 1))
 
     def write0(c, p, tile, lanes, d):
         u1[c, p + 2, :, lanes] = u0[c, p + 2, :, lanes] + d
 
-    a.apply(u0, 2, t0, p0, k0, FX, x1, FX, -1, 9, UNROLL0, write0)
+    each(-1, 9, 2, lambda p: a.weights(c0_ref, p + 2, k0, p + 1))
+    a.apply(u0, 2, t0, p0, k0, 1, x1, 1, -1, 9, UNROLL0, write0)
 
     def write_last(c, p, tile, lanes, d):
         u0[c, p + 2, :, lanes] = u1[c, p + 2, :, lanes] + d
 
-    a.apply(u1, 2, t0, p0, k0, FX, x1, FX, 0, BX, UNROLL0, write_last)
+    a.apply(u1, 2, t0, p0, k0, 1, x1, 1, 0, BX, UNROLL0, write_last)
     near = iota((8, 128), 1) < SPLIT
     for x in range(BX):
         for c in range(COMP):
@@ -575,7 +590,7 @@
         in_specs=[vmem] * len(args),
         out_specs=[vmem] * len(outs),
         scratch_shapes=[pltpu.VMEM(s, F32) for s in scratch],
-        compiler_params=pltpu.CompilerParams(vmem_limit_bytes=32 * 1024 * 1024),
+        compiler_params=pltpu.CompilerParams(vmem_limit_bytes=48 * 1024 * 1024),
     )(*args)
 
 
@@ -586,7 +601,15 @@
     f = right_side.reshape(VEC * COMP * NZ * BX, BY)
     m = material.reshape(NZ * BX, BY)
     edge = (13, 8, 128)
-    to_left, to_right = call(edge_kernel, [edge, edge], [], f, m)
+    hbm, vmem = pl.BlockSpec(memory_space=pltpu.HBM), pl.BlockSpec(memory_space=pltpu.VMEM)
+    to_left, to_right = pl.pallas_call(
+        edge_kernel,
+        out_shape=[jax.ShapeDtypeStruct(s, F32) for s in (edge, edge)],
+        in_specs=[hbm] * 2,
+        out_specs=[vmem] * 2,
+        scratch_shapes=[pltpu.VMEM(f.shape, F32), pltpu.VMEM(m.shape, jnp.int32), pltpu.SemaphoreType.DMA((2,))],
+        compiler_params=pltpu.CompilerParams(vmem_limit_bytes=8 * 1024 * 1024),
+    )(f, m)
     right = ring(to_left, "gy", gy, -1)
     left = ring(to_right, "gy", gy, 1)
     side = (COMP * FX + 2, 8, L0)
@@ -602,9 +625,10 @@
     pay, to_left, to_right, *kept = call(
         functools.partial(down_kernel, gx),
         [
-            (n, 16, 128), plane1(9), plane1(9), plane(3, nf), plane(3, nf), (13, nf, 8, K0), plane1(3, 8), plane1(3, 6), (13, 8, 8, 128),
+            (n, 16, 128), plane1(9), plane1(9), plane(3, 10), plane(3, 12), (12, 8, K0), plane1(3, 8), plane1(3, 4), (13, 8, 8, 128),
         ],
         [
+            plane(3, nf), plane(3, nf), (13, nf, 8, K0), plane1(3, 6),
             (nc, 8, K0), (nf, 8, K0), plane(nf), plane(nf), plane(3, 16), (192, L0), (80, K0), (10, 8, 128),
             (8, 8, 128), plane1(3, 8), plane1(10), plane1(10), plane1(3, 4), (128, 128), (16, 128),
         ],
@@ -623,7 +647,7 @@
             plane2(nx2 + 2), plane2(3, nx2), plane2(13, nx2), plane2(nx2), plane2(3, nx2), plane2(3, nx2 + 4), plane2(3, nx2 + 4),
             plane2(3, nx2), plane2(nx2 + 2), plane2(nx2 + 2), (32 * nx3, y2),
             plane3(nx3 + 2), plane3(13, nx3), plane3(3, nx3), plane3(3, nx3 + 2), plane3(3, nx3 + 2), plane3(nx3 + 2), plane3(nx3 + 2),
-            (24 * nx3, l3), (288, y2), plane1(3, 10), plane1(3, 10), plane1(10), plane1(10), (4, 144, 128),
+            (24 * nx3, l3), (288, y2), plane1(3, 10), plane1(3, 10), plane1(10), plane1(10), (4, 144, 128), (13, 10, 8, K0),
             plane(3, 12), plane(3, 12), plane(12), plane(12),
         ],
         got, left, right, *kept,

time: 64.2 us -> 50.6 us (0.79)
  local copies, waits for them, and re-layouts: 13.2 us -> 1.76 us
  Pallas kernels: 16.7 us -> 13.6 us
  waiting for transfers between devices: 17 us -> 18.2 us
    unnamed x32 -> x8, local copies, waits for them, and re-layouts: 13.2 us -> 1.76 us
    pallas_call x4 -> x3, Pallas kernels: 16.7 us -> 13.1 us  [call(): pl.pallas_call(kernel, out_shape=shapes, in_specs=[vmem] * len(args), out...]
    all_to_all x1, waiting for transfers between devices: 2.7 us -> 4.19 us  [per_device(): got = lax.all_to_all(pay, ('gx', 'gy'), 0, 0)]
where the time goes in v3:
time: 50.6 us; the launch traced here: 50.3 us
  waiting for transfers between devices  18.2 us (36%)
  starting transfers between devices  16.7 us (33%)
  Pallas kernels  13.6 us (27%)
  local copies, waits for them, and re-layouts  1.76 us (3%)
    ppermute x6, waiting for transfers between devices, ring(): lax.ppermute(value, axis, [(i, (i + step) % size) for i in range(size)])  14.1 us
    pallas_call x3, Pallas kernels, call(): pl.pallas_call(kernel, out_shape=shapes, in_specs=[vmem] * len(args), out...  13.1 us
    ppermute x6, starting transfers between devices, ring(): lax.ppermute(value, axis, [(i, (i + step) % size) for i in range(size)])  10.6 us
    all_to_all x1, starting transfers between devices, per_device(): got = lax.all_to_all(pay, ('gx', 'gy'), 0, 0)  6.14 us
    all_to_all x1, waiting for transfers between devices, per_device(): got = lax.all_to_all(pay, ('gx', 'gy'), 0, 0)  4.19 us
    unnamed x8, local copies, waits for them, and re-layouts  1.76 us
  transfers between devices with their start and end apart: 7, of which 5 were waited for; matrix products, arithmetic and copies ran while one was open for 0% of the time, Pallas kernels for 0%

profile of v3, /device:TPU:0, one launch (start us, length us, event | category | flops | bytes accessed | tf_op | source)
XLA Modules:
  0.0 50.3 jit_solution(18099347002853160687)
XLA Ops:
  0.0 0.0 copy-start
  0.0 1.0 %copy-done = f32[4,3,8,8,128]{4,3,2,1,0:T(8,128)S(1)} copy-done((f32[4,3,8,8,128]{4,3,2,1,0:T(8,128)S(1)}, f32[4,3,8,8,128]{4,3,2,1,0:T(8,128)}, u32[]{:S(2)}) %copy-start) | copy-done | bytes 393240
  1.0 0.0 copy-start.2
  1.0 0.8 %copy-done.2 = s32[8,8,128]{2,1,0:T(8,128)S(1)} copy-done((s32[8,8,128]{2,1,0:T(8,128)S(1)}, s32[8,8,128]{2,1,0:T(8,128)}, u32[]{:S(2)}) %copy-start.2) | copy-done | bytes 32792
  1.8 0.0 copy-start.1
  1.8 0.0 copy-start.3
  1.8 0.5 shard_map.28
  2.3 3.1 %collective-permute-start = (f32[13,8,128]{2,1,0:T(8,128)S(1)}, f32[13,8,128]{2,1,0:T(8,128)S(1)}, u32[]{:S(2)}, u32[]{:S(2)}) collective-permute-start(f32[13,8,128]{2,1,0:T(8,128)S(1)} %get-tuple-element.19), channel_id=1, source_target_pairs={{0,1},{1,2},{2,3},{3,0},{4,5},{5,6},{6,7},{7,4},{8,9},{9,10},{10,1... | collective-permute-start | bytes 159752 | tf_op jit(solution)/shard_map/ppermute | solution.py:599
  5.3 2.1 %collective-permute-start.1 = (f32[13,8,128]{2,1,0:T(8,128)S(1)}, f32[13,8,128]{2,1,0:T(8,128)S(1)}, u32[]{:S(2)}, u32[]{:S(2)}) collective-permute-start(f32[13,8,128]{2,1,0:T(8,128)S(1)} %get-tuple-element.20), channel_id=1, source_target_pairs={{0,3},{1,0},{2,1},{3,2},{4,7},{5,4},{6,5},{7,6},{8,11},{9,8},{10,9... | collective-permute-start | bytes 159752 | tf_op jit(solution)/shard_map/ppermute | solution.py:599
  7.4 2.1 %collective-permute-done.l_ref = f32[13,8,128]{2,1,0:T(8,128)S(1)} collective-permute-done((f32[13,8,128]{2,1,0:T(8,128)S(1)}, f32[13,8,128]{2,1,0:T(8,128)S(1)}, u32[]{:S(2)}, u32[]{:S(2)}) %collective-permute-start) | collective-permute-done | bytes 53280 | tf_op jit(solution)/shard_map/ppermute | solution.py:599
  9.5 0.5 %collective-permute-done.1.r_ref = f32[13,8,128]{2,1,0:T(8,128)S(1)} collective-permute-done((f32[13,8,128]{2,1,0:T(8,128)S(1)}, f32[13,8,128]{2,1,0:T(8,128)S(1)}, u32[]{:S(2)}, u32[]{:S(2)}) %collective-permute-start.1) | collective-permute-done | bytes 53280 | tf_op jit(solution)/shard_map/ppermute | solution.py:599
  10.0 0.0 copy-done.1
  10.0 0.0 copy-done.3
  10.0 0.7 %shard_map.29 = (f32[26,8,640]{2,1,0:T(8,128)S(1)}, f32[20,8,640]{2,1,0:T(8,128)S(1)}, f32[20,8,640]{2,1,0:T(8,128)S(1)}) custom-call(f32[768,128]{1,0:T(8,128)S(1)} %bitcast.4, s32[64,128]{1,0:T(8,128)S(1)} %bitcast.6, f32[13,8,128]{2,1,0:T(8,128)S(1)} %collective-permute-done.l_ref, f32[13,8,128]{2,1,0:T(8,128)S(1)} %collective-permute-done.1.r_ref), custom_call_target="tpu_custom_call" | custom-call | tf_op jit(solution)/shard_map/pallas_call | solution.py:587
  10.7 0.1 collective-permute-start.2
  10.8 2.6 %collective-permute-start.3 = (f32[20,8,640]{2,1,0:T(8,128)S(1)}, f32[20,8,640]{2,1,0:T(8,128)S(1)}, u32[]{:S(2)}, u32[]{:S(2)}) collective-permute-start(f32[20,8,640]{2,1,0:T(8,128)S(1)} %get-tuple-element.23), channel_id=1, source_target_pairs={{0,28},{4,0},{8,4},{12,8},{16,12},{20,16},{24,20},{28,24},{1,29},{... | collective-permute-start | bytes 1228808 | tf_op jit(solution)/shard_map/ppermute | solution.py:599
  13.4 8.1 %collective-permute-done.2.l_ref = f32[20,8,640]{2,1,0:T(8,128)S(1)} collective-permute-done((f32[20,8,640]{2,1,0:T(8,128)S(1)}, f32[20,8,640]{2,1,0:T(8,128)S(1)}, u32[]{:S(2)}, u32[]{:S(2)}) %collective-permute-start.2) | collective-permute-done | bytes 409632 | tf_op jit(solution)/shard_map/ppermute | solution.py:599
  21.5 0.0 collective-permute-done.3.r_ref
  21.5 5.9 %shard_map.30 = (f32[32,16,128]{2,1,0:T(8,128)}, f32[9,8,256]{2,1,0:T(8,128)S(1)}, f32[9,8,256]{2,1,0:T(8,128)S(1)}, f32[3,10,8,640]{3,2,1,0:T(8,128)S(1)}, f32[...) custom-call(f32[26,8,640]{2,1,0:T(8,128)S(1)} %get-tuple-element.21., ...), custom_call_target="tpu_custom_call" | custom-call | tf_op jit(solution)/shard_map/pallas_call | solution.py:587
  27.4 6.1 %all-to-all-start = ((f32[32,16,128]{2,1,0:T(8,128)}), f32[32,16,128]{2,1,0:T(8,128)S(1)}, u32[]{:S(2)}, u32[]{:S(2)}) async-start(f32[32,16,128]{2,1,0:T(8,128)} %get-tuple-element.24), calls=%async_computation | async-start | bytes 524288 | tf_op jit(solution)/shard_map/all_to_all | solution.py:639
  33.6 0.3 collective-permute-start.4
  33.9 2.4 %collective-permute-start.5 = (f32[9,8,256]{2,1,0:T(8,128)S(1)}, f32[9,8,256]{2,1,0:T(8,128)S(1)}, u32[]{:S(2)}, u32[]{:S(2)}) collective-permute-start(f32[9,8,256]{2,1,0:T(8,128)S(1)} %get-tuple-element.26), channel_id=1, source_target_pairs={{0,28},{4,0},{8,4},{12,8},{16,12},{20,16},{24,20},{28,24},{1,29},{... | collective-permute-start | bytes 221192 | tf_op jit(solution)/shard_map/ppermute | solution.py:599
  36.3 3.3 %collective-permute-done.4.l_ref = f32[9,8,256]{2,1,0:T(8,128)S(1)} collective-permute-done((f32[9,8,256]{2,1,0:T(8,128)S(1)}, f32[9,8,256]{2,1,0:T(8,128)S(1)}, u32[]{:S(2)}, u32[]{:S(2)}) %collective-permute-start.4) | collective-permute-done | bytes 73760 | tf_op jit(solution)/shard_map/ppermute | solution.py:599
  39.6 0.0 collective-permute-done.5.r_ref
  39.6 4.2 %all-to-all-done.got_ref = f32[32,16,128]{2,1,0:T(8,128)S(1)} async-done(((f32[32,16,128]{2,1,0:T(8,128)}), f32[32,16,128]{2,1,0:T(8,128)S(1)}, u32[]{:S(2)}, u32[]{:S(2)}) %all-to-all-start) | async-done | bytes 262176 | tf_op jit(solution)/shard_map/all_to_all | solution.py:639
  43.8 6.6 %shard_map.31 = f32[768,128]{1,0:T(8,128)} custom-call(f32[32,16,128]{2,1,0:T(8,128)S(1)} %all-to-all-done.got_ref, f32[9,8,256]{2,1,0:T(8,128)S(1)} %collective-permute-done.4.l_ref, f32[9,8,256]{2,1,0:T(8,128)S(1)} %collective-permute-done.5.r_ref, f32[3,10,8,640]{3,2,1,0:T(8,128)S(1)} %get-tuple-element.27.x1, ...), custom_call_target="tpu_custom_call" | custom-call | tf_op jit(solution)/shard_map/pallas_call | solution.py:587
Async XLA Ops:
  0.0 1.0 %copy-start = (f32[4,3,8,8,128]{4,3,2,1,0:T(8,128)S(1)}, f32[4,3,8,8,128]{4,3,2,1,0:T(8,128)}, u32[]{:S(2)}) copy-start(f32[4,3,8,8,128]{4,3,2,1,0:T(8,128)} %param.2) | copy-start | bytes 1179652
  1.0 0.8 %copy-start.2 = (s32[8,8,128]{2,1,0:T(8,128)S(1)}, s32[8,8,128]{2,1,0:T(8,128)}, u32[]{:S(2)}) copy-start(s32[8,8,128]{2,1,0:T(8,128)} %param.3) | copy-start | bytes 98308
  1.8 8.3 %copy-start.1 = (f32[4,3,8,8,128]{4,3,2,1,0:T(8,128)S(1)}, f32[4,3,8,8,128]{4,3,2,1,0:T(8,128)}, u32[]{:S(2)}) copy-start(f32[4,3,8,8,128]{4,3,2,1,0:T(8,128)} %param.2) | copy-start | bytes 1179652
  1.8 8.3 %copy-start.3 = (s32[8,8,128]{2,1,0:T(8,128)S(1)}, s32[8,8,128]{2,1,0:T(8,128)}, u32[]{:S(2)}) copy-start(s32[8,8,128]{2,1,0:T(8,128)} %param.3) | copy-start | bytes 98308
  2.3 7.3 %collective-permute-start = (f32[13,8,128]{2,1,0:T(8,128)S(1)}, f32[13,8,128]{2,1,0:T(8,128)S(1)}, u32[]{:S(2)}, u32[]{:S(2)}) collective-permute-start(f32[13,8,128]{2,1,0:T(8,128)S(1)} %get-tuple-element.19), channel_id=1, source_target_pairs={{0,1},{1,2},{2,3},{3,0},{4,5},{5,6},{6,7},{7,4},{8,9},{9,10},{10,1... | collective-permute-start | bytes 159752 | tf_op jit(solution)/shard_map/ppermute | solution.py:599
  5.3 4.7 %collective-permute-start.1 = (f32[13,8,128]{2,1,0:T(8,128)S(1)}, f32[13,8,128]{2,1,0:T(8,128)S(1)}, u32[]{:S(2)}, u32[]{:S(2)}) collective-permute-start(f32[13,8,128]{2,1,0:T(8,128)S(1)} %get-tuple-element.20), channel_id=1, source_target_pairs={{0,3},{1,0},{2,1},{3,2},{4,7},{5,4},{6,5},{7,6},{8,11},{9,8},{10,9... | collective-permute-start | bytes 159752 | tf_op jit(solution)/shard_map/ppermute | solution.py:599
  10.7 10.8 %collective-permute-start.2 = (f32[20,8,640]{2,1,0:T(8,128)S(1)}, f32[20,8,640]{2,1,0:T(8,128)S(1)}, u32[]{:S(2)}, u32[]{:S(2)}) collective-permute-start(f32[20,8,640]{2,1,0:T(8,128)S(1)} %get-tuple-element.22), channel_id=1, source_target_pairs={{0,4},{4,8},{8,12},{12,16},{16,20},{20,24},{24,28},{28,0},{1,5},{5... | collective-permute-start | bytes 1228808 | tf_op jit(solution)/shard_map/ppermute | solution.py:599
  10.8 10.8 %collective-permute-start.3 = (f32[20,8,640]{2,1,0:T(8,128)S(1)}, f32[20,8,640]{2,1,0:T(8,128)S(1)}, u32[]{:S(2)}, u32[]{:S(2)}) collective-permute-start(f32[20,8,640]{2,1,0:T(8,128)S(1)} %get-tuple-element.23), channel_id=1, source_target_pairs={{0,28},{4,0},{8,4},{12,8},{16,12},{20,16},{24,20},{28,24},{1,29},{... | collective-permute-start | bytes 1228808 | tf_op jit(solution)/shard_map/ppermute | solution.py:599
  27.4 16.3 %all-to-all-start = ((f32[32,16,128]{2,1,0:T(8,128)}), f32[32,16,128]{2,1,0:T(8,128)S(1)}, u32[]{:S(2)}, u32[]{:S(2)}) async-start(f32[32,16,128]{2,1,0:T(8,128)} %get-tuple-element.24), calls=%async_computation | async-start | bytes 524288 | tf_op jit(solution)/shard_map/all_to_all | solution.py:639
  33.6 6.0 %collective-permute-start.4 = (f32[9,8,256]{2,1,0:T(8,128)S(1)}, f32[9,8,256]{2,1,0:T(8,128)S(1)}, u32[]{:S(2)}, u32[]{:S(2)}) collective-permute-start(f32[9,8,256]{2,1,0:T(8,128)S(1)} %get-tuple-element.25), channel_id=1, source_target_pairs={{0,4},{4,8},{8,12},{12,16},{16,20},{20,24},{24,28},{28,0},{1,5},{5... | collective-permute-start | bytes 221192 | tf_op jit(solution)/shard_map/ppermute | solution.py:599
  33.9 5.7 %collective-permute-start.5 = (f32[9,8,256]{2,1,0:T(8,128)S(1)}, f32[9,8,256]{2,1,0:T(8,128)S(1)}, u32[]{:S(2)}, u32[]{:S(2)}) collective-permute-start(f32[9,8,256]{2,1,0:T(8,128)S(1)} %get-tuple-element.26), channel_id=1, source_target_pairs={{0,28},{4,0},{8,4},{12,8},{16,12},{20,16},{24,20},{28,24},{1,29},{... | collective-permute-start | bytes 221192 | tf_op jit(solution)/shard_map/ppermute | solution.py:599

commit v4 on v3

--- a/solution.py
+++ b/solution.py
@@ -228,17 +228,34 @@
         right_ref[12, :, pl.ds(16 * x, 16)] = val[:, BY - RIM :]
 
 
-def join_kernel(gy, f_ref, m_ref, l_ref, r_ref, own_ref, left_ref, right_ref):
+def at_coeff(base, x):
+    piece = 8 + x // 4
+    return base + x // 5, 128 * (x % 5), base + piece // 5, 128 * (piece % 5) + 32 * (x % 4)
+
+
+def place_kernel(f_ref, m_ref, own_ref):
+    def put(row, lane, piece_row, piece_lane, val):
+        own_ref[row, :, pl.ds(lane + LEFT, 128 - LEFT)] = val[:, : 128 - LEFT]
+        own_ref[piece_row, :, pl.ds(piece_lane, BY - PIECE)] = val[:, PIECE:]
+
+    for x in range(BX):
+        for c in range(COMP):
+            for v in range(VEC):
+                put(BX * c + x, 128 * v, BX * c + x, 512 + 32 * v, rows_of(f_ref, v * COMP + c, x))
+        put(*at_coeff(COMP * BX, x), coeff_rows(m_ref, x))
+
+
+def join_kernel(gy, placed_ref, l_ref, r_ref, own_ref, left_ref, right_ref):
     place = lax.axis_index("gy")
     from_left = (place > 0).astype(F32)
     from_right = (place < gy - 1).astype(F32)
     kept = BY - PIECE
-
-    def put(ref, at, start, piece_at, piece_start, val, left, right):
-        ref[*at, :, pl.ds(start, LEFT)] = left[:, RIM - LEFT :]
-        ref[*at, :, pl.ds(start + LEFT, 128 - LEFT)] = val[:, : 128 - LEFT]
-        ref[*piece_at, :, pl.ds(piece_start, kept)] = val[:, PIECE:]
-        ref[*piece_at, :, pl.ds(piece_start + kept, 32 - kept)] = right[:, : 32 - kept]
+    for i in range(COMP * BX + 2):
+        own_ref[i] = placed_ref[i]
+
+    def put(row, lane, piece_row, piece_lane, left, right):
+        own_ref[row, :, pl.ds(lane, LEFT)] = left[:, RIM - LEFT :]
+        own_ref[piece_row, :, pl.ds(piece_lane + kept, 32 - kept)] = right[:, : 32 - kept]
 
     for x in range(BX):
         for c in range(COMP):
@@ -246,17 +263,10 @@
             right = r_ref[c * 4 + x % 4] * from_right
             for v in range(VEC):
                 at = (x // 4) * 64 + 16 * v
-                val = rows_of(f_ref, v * COMP + c, x)
-                place = (BX * c + x,)
-                put(own_ref, place, 128 * v, place, 512 + 32 * v, val, left[:, at : at + RIM], right[:, at : at + RIM])
+                put(BX * c + x, 128 * v, BX * c + x, 512 + 32 * v, left[:, at : at + RIM], right[:, at : at + RIM])
         left = l_ref[12, :, pl.ds(16 * x, 16)] * from_left
         right = r_ref[12, :, pl.ds(16 * x, 16)] * from_right
-        base = COMP * BX
-        at, piece = x, 8 + x // 4
-        put(
-            own_ref, (base + at // 5,), 128 * (at % 5), (base + piece // 5,), 128 * (piece % 5) + 32 * (x % 4),
-            coeff_rows(m_ref, x), left, right,
-        )
+        put(*at_coeff(COMP * BX, x), left, right)
     for c in range(COMP):
         for x in range(FX):
             left_ref[c * FX + x] = own_ref[BX * c + x]
@@ -277,9 +287,9 @@
     a = Level(0, 1, 128, (0, 0, 0, 0, 1))
 
     def spread(plane, ref, base, x, factor):
-        at, piece = x, 8 + x // 4
-        val = ref[base + at // 5, :, pl.ds(128 * (at % 5), 128)]
-        end = ref[base + piece // 5, :, pl.ds(128 * (piece % 5) + 32 * (x % 4), 32)]
+        row, lane, piece_row, piece_lane = at_coeff(base, x)
+        val = ref[row, :, pl.ds(lane, 128)]
+        end = ref[piece_row, :, pl.ds(piece_lane, 32)]
         if factor is not None:
             val, end = val * factor, end * factor
         cx[plane + CX, :, pl.ds(0, 128)] = val
@@ -302,7 +312,7 @@
                 for tile, kind in enumerate(a.kinds):
                     x1[c, p + FX, :, a.lanes(tile)] = gain[kind] * plane[:, 128 * tile : 128 * tile + 128]
 
-        each(low, high, 2, body)
+        each(low, high, 4, body)
 
     start(-FX, 0, lambda c, p: l_ref[c * FX + p + FX])
     start(0, BX, lambda c, p: own_ref[BX * c + p])
@@ -479,6 +489,7 @@
     for i in range(nx3):
         c3[i + 1] = coarse[8 * (COMP * nx3 + i) : 8 * (COMP * nx3 + i) + 8]
     n = Level(3, 8, l3, (0,), 16 * gy)
+    a = Level(0, 1, 128, (0, 0, 0, 0, 1))
     for p in range(nx3):
         gain, _ = n.weights(c3, p + 1, k3, p)
         for c in range(COMP):
@@ -486,12 +497,14 @@
             x1d[c, p] = val
             va[c, p + 1] = val
     src, dst = va, vb
-    for _ in range(COARSE - 1):
+    for sweep in range(COARSE - 1):
 
         def write3(c, p, tile, lanes, d, src=src, dst=dst):
             dst[c, p + 1] = src[c, p + 1] + d
 
         n.apply(src, 1, t3, p3, k3, 0, x1d, 0, 0, nx3, UNROLL2, write3)
+        for p in (2 * sweep - 1, 2 * sweep):
+            a.weights(c0_ref, p + 2, k0, p + 1)
         src, dst = dst, src
     for c in range(COMP):
         for i in range(nx3):
@@ -559,12 +572,10 @@
             at = 8 * (6 * c + i)
             for j in range(2):
                 u0[c, 2 * i + j, :, pl.ds(512, 128)] = x2[c, 2 * i + j, :, pl.ds(512, 128)] + piece[at : at + 8]
-    a = Level(0, 1, 128, (0, 0, 0, 0, 1))
 
     def write0(c, p, tile, lanes, d):
         u1[c, p + 2, :, lanes] = u0[c, p + 2, :, lanes] + d
 
-    each(-1, 9, 2, lambda p: a.weights(c0_ref, p + 2, k0, p + 1))
     a.apply(u0, 2, t0, p0, k0, 1, x1, 1, -1, 9, UNROLL0, write0)
 
     def write_last(c, p, tile, lanes, d):
@@ -608,14 +619,14 @@
         in_specs=[hbm] * 2,
         out_specs=[vmem] * 2,
         scratch_shapes=[pltpu.VMEM(f.shape, F32), pltpu.VMEM(m.shape, jnp.int32), pltpu.SemaphoreType.DMA((2,))],
-        compiler_params=pltpu.CompilerParams(vmem_limit_bytes=8 * 1024 * 1024),
+        compiler_params=pltpu.CompilerParams(vmem_limit_bytes=61 * 1024 * 1024),
     )(f, m)
     right = ring(to_left, "gy", gy, -1)
     left = ring(to_right, "gy", gy, 1)
     side = (COMP * FX + 2, 8, L0)
-    own, to_left, to_right = call(
-        functools.partial(join_kernel, gy), [(COMP * BX + 2, 8, L0), side, side], [], f, m, left, right
-    )
+    whole = (COMP * BX + 2, 8, L0)
+    (own,) = call(place_kernel, [whole], [], f, m)
+    own, to_left, to_right = call(functools.partial(join_kernel, gy), [whole, side, side], [], own, left, right)
     right = ring(to_left, "gx", gx, -1)
     left = ring(to_right, "gx", gx, 1)
     n = gx * gy

time: 50.6 us -> 49.3 us (0.974)
  local copies, waits for them, and re-layouts: 1.76 us -> 0.01 us
  Pallas kernels: 13.6 us -> 14.2 us
    unnamed x8 -> x4, local copies, waits for them, and re-layouts: 1.76 us -> 0.01 us
    pallas_call x1, Pallas kernels: 0.49 us -> 1.98 us  [per_device(): pl.pallas_call(edge_kernel, out_shape=[jax.ShapeDtypeStruct(s, F32) for s...]
    pallas_call x3 -> x4, Pallas kernels: 13.1 us -> 12.2 us  [call(): pl.pallas_call(kernel, out_shape=shapes, in_specs=[vmem] * len(args), out...]
  transfers between devices with their start and end apart: 7 -> 7, of which waited for: 5 -> 5; matrix products, arithmetic and copies ran while one was open for 0% -> 0% of each run, Pallas kernels for 0% -> 1%
where the time goes in v4:
time: 49.3 us; the launch traced here: 49.1 us
  waiting for transfers between devices  18.2 us (37%)
  starting transfers between devices  16.7 us (34%)
  Pallas kernels  14.2 us (29%)
    ppermute x6, waiting for transfers between devices, ring(): lax.ppermute(value, axis, [(i, (i + step) % size) for i in range(size)])  14 us
    pallas_call x4, Pallas kernels, call(): pl.pallas_call(kernel, out_shape=shapes, in_specs=[vmem] * len(args), out...  12.2 us
    ppermute x6, starting transfers between devices, ring(): lax.ppermute(value, axis, [(i, (i + step) % size) for i in range(size)])  10.6 us
    all_to_all x1, starting transfers between devices, per_device(): got = lax.all_to_all(pay, ('gx', 'gy'), 0, 0)  6.14 us
    all_to_all x1, waiting for transfers between devices, per_device(): got = lax.all_to_all(pay, ('gx', 'gy'), 0, 0)  4.19 us
    pallas_call x1, Pallas kernels, per_device(): pl.pallas_call(edge_kernel, out_shape=[jax.ShapeDtypeStruct(s, F32) for s...  1.98 us
  transfers between devices with their start and end apart: 7, of which 5 were waited for; matrix products, arithmetic and copies ran while one was open for 0% of the time, Pallas kernels for 1%

profile of v4, /device:TPU:0, one launch (start us, length us, event | category | flops | bytes accessed | tf_op | source)
XLA Modules:
  0.0 49.1 jit_solution(15220694894185048156)
XLA Ops:
  0.0 0.0 copy-start
  0.0 0.0 copy-start.1
  0.0 2.0 %shard_map.29 = (f32[13,8,128]{2,1,0:T(8,128)}, f32[13,8,128]{2,1,0:T(8,128)}) custom-call(f32[768,128]{1,0:T(8,128)} %bitcast.3, s32[64,128]{1,0:T(8,128)} %bitcast.5), custom_call_target="tpu_custom_call" | custom-call | tf_op jit(solution)/shard_map/pallas_call | solution.py:616
  2.0 3.1 %collective-permute-start = (f32[13,8,128]{2,1,0:T(8,128)}, f32[13,8,128]{2,1,0:T(8,128)S(1)}, u32[]{:S(2)}, u32[]{:S(2)}) collective-permute-start(f32[13,8,128]{2,1,0:T(8,128)} %get-tuple-element.19), channel_id=1, source_target_pairs={{0,1},{1,2},{2,3},{3,0},{4,5},{5,6},{6,7},{7,4},{8,9},{9,10},{10,1... | collective-permute-start | bytes 159752 | tf_op jit(solution)/shard_map/ppermute | solution.py:610
  5.1 2.1 %collective-permute-start.1 = (f32[13,8,128]{2,1,0:T(8,128)}, f32[13,8,128]{2,1,0:T(8,128)S(1)}, u32[]{:S(2)}, u32[]{:S(2)}) collective-permute-start(f32[13,8,128]{2,1,0:T(8,128)} %get-tuple-element.20), channel_id=1, source_target_pairs={{0,3},{1,0},{2,1},{3,2},{4,7},{5,4},{6,5},{7,6},{8,11},{9,8},{10,9... | collective-permute-start | bytes 159752 | tf_op jit(solution)/shard_map/ppermute | solution.py:610
  7.2 0.0 copy-done
  7.2 0.0 copy-done.1
  7.2 0.3 shard_map.28.placed_ref
  7.5 2.0 %collective-permute-done.l_ref = f32[13,8,128]{2,1,0:T(8,128)S(1)} collective-permute-done((f32[13,8,128]{2,1,0:T(8,128)}, f32[13,8,128]{2,1,0:T(8,128)S(1)}, u32[]{:S(2)}, u32[]{:S(2)}) %collective-permute-start) | collective-permute-done | bytes 53280 | tf_op jit(solution)/shard_map/ppermute | solution.py:610
  9.5 0.5 %collective-permute-done.1.r_ref = f32[13,8,128]{2,1,0:T(8,128)S(1)} collective-permute-done((f32[13,8,128]{2,1,0:T(8,128)}, f32[13,8,128]{2,1,0:T(8,128)S(1)}, u32[]{:S(2)}, u32[]{:S(2)}) %collective-permute-start.1) | collective-permute-done | bytes 53280 | tf_op jit(solution)/shard_map/ppermute | solution.py:610
  10.0 0.4 shard_map.30
  10.4 0.1 collective-permute-start.2
  10.4 2.6 %collective-permute-start.3 = (f32[20,8,640]{2,1,0:T(8,128)S(1)}, f32[20,8,640]{2,1,0:T(8,128)S(1)}, u32[]{:S(2)}, u32[]{:S(2)}) collective-permute-start(f32[20,8,640]{2,1,0:T(8,128)S(1)} %get-tuple-element.23), channel_id=1, source_target_pairs={{0,28},{4,0},{8,4},{12,8},{16,12},{20,16},{24,20},{28,24},{1,29},{... | collective-permute-start | bytes 1228808 | tf_op jit(solution)/shard_map/ppermute | solution.py:610
  13.1 8.1 %collective-permute-done.2.l_ref = f32[20,8,640]{2,1,0:T(8,128)S(1)} collective-permute-done((f32[20,8,640]{2,1,0:T(8,128)S(1)}, f32[20,8,640]{2,1,0:T(8,128)S(1)}, u32[]{:S(2)}, u32[]{:S(2)}) %collective-permute-start.2) | collective-permute-done | bytes 409632 | tf_op jit(solution)/shard_map/ppermute | solution.py:610
  21.2 0.0 collective-permute-done.3.r_ref
  21.2 5.6 %shard_map.31 = (f32[32,16,128]{2,1,0:T(8,128)}, f32[9,8,256]{2,1,0:T(8,128)S(1)}, f32[9,8,256]{2,1,0:T(8,128)S(1)}, f32[3,10,8,640]{3,2,1,0:T(8,128)S(1)}, f32[...) custom-call(f32[26,8,640]{2,1,0:T(8,128)S(1)} %get-tuple-element.21., ...), custom_call_target="tpu_custom_call" | custom-call | tf_op jit(solution)/shard_map/pallas_call | solution.py:598
  26.7 6.1 %all-to-all-start = ((f32[32,16,128]{2,1,0:T(8,128)}), f32[32,16,128]{2,1,0:T(8,128)S(1)}, u32[]{:S(2)}, u32[]{:S(2)}) async-start(f32[32,16,128]{2,1,0:T(8,128)} %get-tuple-element.24), calls=%async_computation | async-start | bytes 524288 | tf_op jit(solution)/shard_map/all_to_all | solution.py:650
  32.9 0.3 collective-permute-start.4
  33.2 2.4 %collective-permute-start.5 = (f32[9,8,256]{2,1,0:T(8,128)S(1)}, f32[9,8,256]{2,1,0:T(8,128)S(1)}, u32[]{:S(2)}, u32[]{:S(2)}) collective-permute-start(f32[9,8,256]{2,1,0:T(8,128)S(1)} %get-tuple-element.26), channel_id=1, source_target_pairs={{0,28},{4,0},{8,4},{12,8},{16,12},{20,16},{24,20},{28,24},{1,29},{... | collective-permute-start | bytes 221192 | tf_op jit(solution)/shard_map/ppermute | solution.py:610
  35.6 3.3 %collective-permute-done.4.l_ref = f32[9,8,256]{2,1,0:T(8,128)S(1)} collective-permute-done((f32[9,8,256]{2,1,0:T(8,128)S(1)}, f32[9,8,256]{2,1,0:T(8,128)S(1)}, u32[]{:S(2)}, u32[]{:S(2)}) %collective-permute-start.4) | collective-permute-done | bytes 73760 | tf_op jit(solution)/shard_map/ppermute | solution.py:610
  38.9 0.0 collective-permute-done.5.r_ref
  38.9 4.2 %all-to-all-done.got_ref = f32[32,16,128]{2,1,0:T(8,128)S(1)} async-done(((f32[32,16,128]{2,1,0:T(8,128)}), f32[32,16,128]{2,1,0:T(8,128)S(1)}, u32[]{:S(2)}, u32[]{:S(2)}) %all-to-all-start) | async-done | bytes 262176 | tf_op jit(solution)/shard_map/all_to_all | solution.py:650
  43.1 6.0 %shard_map.32 = f32[768,128]{1,0:T(8,128)} custom-call(f32[32,16,128]{2,1,0:T(8,128)S(1)} %all-to-all-done.got_ref, f32[9,8,256]{2,1,0:T(8,128)S(1)} %collective-permute-done.4.l_ref, f32[9,8,256]{2,1,0:T(8,128)S(1)} %collective-permute-done.5.r_ref, f32[3,10,8,640]{3,2,1,0:T(8,128)S(1)} %get-tuple-element.27.x1, ...), custom_call_target="tpu_custom_call" | custom-call | tf_op jit(solution)/shard_map/pallas_call | solution.py:598
Async XLA Ops:
  0.0 7.2 %copy-start = (f32[4,3,8,8,128]{4,3,2,1,0:T(8,128)S(1)}, f32[4,3,8,8,128]{4,3,2,1,0:T(8,128)}, u32[]{:S(2)}) copy-start(f32[4,3,8,8,128]{4,3,2,1,0:T(8,128)} %param.2) | copy-start | bytes 1179652
  0.0 7.2 %copy-start.1 = (s32[8,8,128]{2,1,0:T(8,128)S(1)}, s32[8,8,128]{2,1,0:T(8,128)}, u32[]{:S(2)}) copy-start(s32[8,8,128]{2,1,0:T(8,128)} %param.3) | copy-start | bytes 98308
  2.0 7.5 %collective-permute-start = (f32[13,8,128]{2,1,0:T(8,128)}, f32[13,8,128]{2,1,0:T(8,128)S(1)}, u32[]{:S(2)}, u32[]{:S(2)}) collective-permute-start(f32[13,8,128]{2,1,0:T(8,128)} %get-tuple-element.19), channel_id=1, source_target_pairs={{0,1},{1,2},{2,3},{3,0},{4,5},{5,6},{6,7},{7,4},{8,9},{9,10},{10,1... | collective-permute-start | bytes 159752 | tf_op jit(solution)/shard_map/ppermute | solution.py:610
  5.1 4.9 %collective-permute-start.1 = (f32[13,8,128]{2,1,0:T(8,128)}, f32[13,8,128]{2,1,0:T(8,128)S(1)}, u32[]{:S(2)}, u32[]{:S(2)}) collective-permute-start(f32[13,8,128]{2,1,0:T(8,128)} %get-tuple-element.20), channel_id=1, source_target_pairs={{0,3},{1,0},{2,1},{3,2},{4,7},{5,4},{6,5},{7,6},{8,11},{9,8},{10,9... | collective-permute-start | bytes 159752 | tf_op jit(solution)/shard_map/ppermute | solution.py:610
  10.4 10.8 %collective-permute-start.2 = (f32[20,8,640]{2,1,0:T(8,128)S(1)}, f32[20,8,640]{2,1,0:T(8,128)S(1)}, u32[]{:S(2)}, u32[]{:S(2)}) collective-permute-start(f32[20,8,640]{2,1,0:T(8,128)S(1)} %get-tuple-element.22), channel_id=1, source_target_pairs={{0,4},{4,8},{8,12},{12,16},{16,20},{20,24},{24,28},{28,0},{1,5},{5... | collective-permute-start | bytes 1228808 | tf_op jit(solution)/shard_map/ppermute | solution.py:610
  10.4 10.8 %collective-permute-start.3 = (f32[20,8,640]{2,1,0:T(8,128)S(1)}, f32[20,8,640]{2,1,0:T(8,128)S(1)}, u32[]{:S(2)}, u32[]{:S(2)}) collective-permute-start(f32[20,8,640]{2,1,0:T(8,128)S(1)} %get-tuple-element.23), channel_id=1, source_target_pairs={{0,28},{4,0},{8,4},{12,8},{16,12},{20,16},{24,20},{28,24},{1,29},{... | collective-permute-start | bytes 1228808 | tf_op jit(solution)/shard_map/ppermute | solution.py:610
  26.7 16.3 %all-to-all-start = ((f32[32,16,128]{2,1,0:T(8,128)}), f32[32,16,128]{2,1,0:T(8,128)S(1)}, u32[]{:S(2)}, u32[]{:S(2)}) async-start(f32[32,16,128]{2,1,0:T(8,128)} %get-tuple-element.24), calls=%async_computation | async-start | bytes 524288 | tf_op jit(solution)/shard_map/all_to_all | solution.py:650
  32.9 6.0 %collective-permute-start.4 = (f32[9,8,256]{2,1,0:T(8,128)S(1)}, f32[9,8,256]{2,1,0:T(8,128)S(1)}, u32[]{:S(2)}, u32[]{:S(2)}) collective-permute-start(f32[9,8,256]{2,1,0:T(8,128)S(1)} %get-tuple-element.25), channel_id=1, source_target_pairs={{0,4},{4,8},{8,12},{12,16},{16,20},{20,24},{24,28},{28,0},{1,5},{5... | collective-permute-start | bytes 221192 | tf_op jit(solution)/shard_map/ppermute | solution.py:610
  33.2 5.7 %collective-permute-start.5 = (f32[9,8,256]{2,1,0:T(8,128)S(1)}, f32[9,8,256]{2,1,0:T(8,128)S(1)}, u32[]{:S(2)}, u32[]{:S(2)}) collective-permute-start(f32[9,8,256]{2,1,0:T(8,128)S(1)} %get-tuple-element.26), channel_id=1, source_target_pairs={{0,28},{4,0},{8,4},{12,8},{16,12},{20,16},{24,20},{28,24},{1,29},{... | collective-permute-start | bytes 221192 | tf_op jit(solution)/shard_map/ppermute | solution.py:610

commit v5 on v4

--- a/solution.py
+++ b/solution.py
@@ -12,7 +12,7 @@
 GRAD_DIV = 2.5
 VEC, COMP, NZ, BX, BY = 4, 3, 8, 8, 128
 COARSE = 6
-UNROLL0, UNROLL1, UNROLL2 = 4, 4, 16
+UNROLL0, UNROLL1, UNROLL2 = 20, 8, 16
 RIM = 16
 LEFT = 11
 PIECE = 108
@@ -211,18 +211,21 @@
 
 
 def edge_kernel(f_hbm, m_hbm, left_ref, right_ref, f_ref, m_ref, sems):
-    copies = [pltpu.make_async_copy(m_hbm, m_ref, sems.at[0]), pltpu.make_async_copy(f_hbm, f_ref, sems.at[1])]
+    step = f_ref.shape[0] // VEC
+    copies = [pltpu.make_async_copy(f_hbm.at[pl.ds(step * v, step)], f_ref.at[pl.ds(step * v, step)], sems.at[v]) for v in range(VEC)]
+    copies.append(pltpu.make_async_copy(m_hbm, m_ref, sems.at[VEC]))
     for copy in copies:
         copy.start()
-    for copy in copies:
-        copy.wait()
-    for x in range(BX):
-        for v in range(VEC):
+    for v in range(VEC):
+        copies[v].wait()
+        for x in range(BX):
             for c in range(COMP):
                 val = rows_of(f_ref, v * COMP + c, x)
                 lanes = pl.ds((x // 4) * 64 + 16 * v, 16)
                 left_ref[c * 4 + x % 4, :, lanes] = val[:, :RIM]
                 right_ref[c * 4 + x % 4, :, lanes] = val[:, BY - RIM :]
+    copies[VEC].wait()
+    for x in range(BX):
         val = coeff_rows(m_ref, x)
         left_ref[12, :, pl.ds(16 * x, 16)] = val[:, :RIM]
         right_ref[12, :, pl.ds(16 * x, 16)] = val[:, BY - RIM :]
@@ -618,7 +621,7 @@
         out_shape=[jax.ShapeDtypeStruct(s, F32) for s in (edge, edge)],
         in_specs=[hbm] * 2,
         out_specs=[vmem] * 2,
-        scratch_shapes=[pltpu.VMEM(f.shape, F32), pltpu.VMEM(m.shape, jnp.int32), pltpu.SemaphoreType.DMA((2,))],
+        scratch_shapes=[pltpu.VMEM(f.shape, F32), pltpu.VMEM(m.shape, jnp.int32), pltpu.SemaphoreType.DMA((VEC + 1,))],
         compiler_params=pltpu.CompilerParams(vmem_limit_bytes=61 * 1024 * 1024),
     )(f, m)
     right = ring(to_left, "gy", gy, -1)

time: 49.3 us -> 47.9 us (0.972)
  Pallas kernels: 14.2 us -> 12.7 us
    pallas_call x4, Pallas kernels: 12.2 us -> 10.6 us  [call(): pl.pallas_call(kernel, out_shape=shapes, in_specs=[vmem] * len(args), out...]
where the time goes in v5:
time: 47.9 us; the launch traced here: 47.6 us
  waiting for transfers between devices  18.2 us (38%)
  starting transfers between devices  16.7 us (35%)
  Pallas kernels  12.7 us (27%)
    ppermute x6, waiting for transfers between devices, ring(): lax.ppermute(value, axis, [(i, (i + step) % size) for i in range(size)])  14 us
    pallas_call x4, Pallas kernels, call(): pl.pallas_call(kernel, out_shape=shapes, in_specs=[vmem] * len(args), out...  10.6 us
    ppermute x6, starting transfers between devices, ring(): lax.ppermute(value, axis, [(i, (i + step) % size) for i in range(size)])  10.6 us
    all_to_all x1, starting transfers between devices, per_device(): got = lax.all_to_all(pay, ('gx', 'gy'), 0, 0)  6.14 us
    all_to_all x1, waiting for transfers between devices, per_device(): got = lax.all_to_all(pay, ('gx', 'gy'), 0, 0)  4.19 us
    pallas_call x1, Pallas kernels, per_device(): pl.pallas_call(edge_kernel, out_shape=[jax.ShapeDtypeStruct(s, F32) for s...  2.18 us
  transfers between devices with their start and end apart: 7, of which 5 were waited for; matrix products, arithmetic and copies ran while one was open for 0% of the time, Pallas kernels for 1%

profile of v5, /device:TPU:0, one launch (start us, length us, event | category | flops | bytes accessed | tf_op | source)
XLA Modules:
  0.0 47.6 jit_solution(309037678527650941)
XLA Ops:
  0.0 0.0 copy-start
  0.0 0.0 copy-start.1
  0.0 2.2 %shard_map.29 = (f32[13,8,128]{2,1,0:T(8,128)}, f32[13,8,128]{2,1,0:T(8,128)}) custom-call(f32[768,128]{1,0:T(8,128)} %bitcast.3, s32[64,128]{1,0:T(8,128)} %bitcast.5), custom_call_target="tpu_custom_call" | custom-call | tf_op jit(solution)/shard_map/pallas_call | solution.py:619
  2.2 3.1 %collective-permute-start = (f32[13,8,128]{2,1,0:T(8,128)}, f32[13,8,128]{2,1,0:T(8,128)S(1)}, u32[]{:S(2)}, u32[]{:S(2)}) collective-permute-start(f32[13,8,128]{2,1,0:T(8,128)} %get-tuple-element.19), channel_id=1, source_target_pairs={{0,1},{1,2},{2,3},{3,0},{4,5},{5,6},{6,7},{7,4},{8,9},{9,10},{10,1... | collective-permute-start | bytes 159752 | tf_op jit(solution)/shard_map/ppermute | solution.py:613
  5.3 2.1 %collective-permute-start.1 = (f32[13,8,128]{2,1,0:T(8,128)}, f32[13,8,128]{2,1,0:T(8,128)S(1)}, u32[]{:S(2)}, u32[]{:S(2)}) collective-permute-start(f32[13,8,128]{2,1,0:T(8,128)} %get-tuple-element.20), channel_id=1, source_target_pairs={{0,3},{1,0},{2,1},{3,2},{4,7},{5,4},{6,5},{7,6},{8,11},{9,8},{10,9... | collective-permute-start | bytes 159752 | tf_op jit(solution)/shard_map/ppermute | solution.py:613
  7.4 0.0 copy-done
  7.4 0.0 copy-done.1
  7.4 0.3 shard_map.28.placed_ref
  7.7 2.0 %collective-permute-done.l_ref = f32[13,8,128]{2,1,0:T(8,128)S(1)} collective-permute-done((f32[13,8,128]{2,1,0:T(8,128)}, f32[13,8,128]{2,1,0:T(8,128)S(1)}, u32[]{:S(2)}, u32[]{:S(2)}) %collective-permute-start) | collective-permute-done | bytes 53280 | tf_op jit(solution)/shard_map/ppermute | solution.py:613
  9.7 0.5 %collective-permute-done.1.r_ref = f32[13,8,128]{2,1,0:T(8,128)S(1)} collective-permute-done((f32[13,8,128]{2,1,0:T(8,128)}, f32[13,8,128]{2,1,0:T(8,128)S(1)}, u32[]{:S(2)}, u32[]{:S(2)}) %collective-permute-start.1) | collective-permute-done | bytes 53280 | tf_op jit(solution)/shard_map/ppermute | solution.py:613
  10.2 0.4 shard_map.30
  10.6 0.1 collective-permute-start.2
  10.6 2.6 %collective-permute-start.3 = (f32[20,8,640]{2,1,0:T(8,128)S(1)}, f32[20,8,640]{2,1,0:T(8,128)S(1)}, u32[]{:S(2)}, u32[]{:S(2)}) collective-permute-start(f32[20,8,640]{2,1,0:T(8,128)S(1)} %get-tuple-element.23), channel_id=1, source_target_pairs={{0,28},{4,0},{8,4},{12,8},{16,12},{20,16},{24,20},{28,24},{1,29},{... | collective-permute-start | bytes 1228808 | tf_op jit(solution)/shard_map/ppermute | solution.py:613
  13.3 8.1 %collective-permute-done.2.l_ref = f32[20,8,640]{2,1,0:T(8,128)S(1)} collective-permute-done((f32[20,8,640]{2,1,0:T(8,128)S(1)}, f32[20,8,640]{2,1,0:T(8,128)S(1)}, u32[]{:S(2)}, u32[]{:S(2)}) %collective-permute-start.2) | collective-permute-done | bytes 409632 | tf_op jit(solution)/shard_map/ppermute | solution.py:613
  21.4 0.0 collective-permute-done.3.r_ref
  21.4 4.8 %shard_map.31 = (f32[32,16,128]{2,1,0:T(8,128)}, f32[9,8,256]{2,1,0:T(8,128)S(1)}, f32[9,8,256]{2,1,0:T(8,128)S(1)}, f32[3,10,8,640]{3,2,1,0:T(8,128)S(1)}, f32[...) custom-call(f32[26,8,640]{2,1,0:T(8,128)S(1)} %get-tuple-element.21., ...), custom_call_target="tpu_custom_call" | custom-call | tf_op jit(solution)/shard_map/pallas_call | solution.py:601
  26.2 6.1 %all-to-all-start = ((f32[32,16,128]{2,1,0:T(8,128)}), f32[32,16,128]{2,1,0:T(8,128)S(1)}, u32[]{:S(2)}, u32[]{:S(2)}) async-start(f32[32,16,128]{2,1,0:T(8,128)} %get-tuple-element.24), calls=%async_computation | async-start | bytes 524288 | tf_op jit(solution)/shard_map/all_to_all | solution.py:653
  32.4 0.3 collective-permute-start.4
  32.7 2.4 %collective-permute-start.5 = (f32[9,8,256]{2,1,0:T(8,128)S(1)}, f32[9,8,256]{2,1,0:T(8,128)S(1)}, u32[]{:S(2)}, u32[]{:S(2)}) collective-permute-start(f32[9,8,256]{2,1,0:T(8,128)S(1)} %get-tuple-element.26), channel_id=1, source_target_pairs={{0,28},{4,0},{8,4},{12,8},{16,12},{20,16},{24,20},{28,24},{1,29},{... | collective-permute-start | bytes 221192 | tf_op jit(solution)/shard_map/ppermute | solution.py:613
  35.1 3.3 %collective-permute-done.4.l_ref = f32[9,8,256]{2,1,0:T(8,128)S(1)} collective-permute-done((f32[9,8,256]{2,1,0:T(8,128)S(1)}, f32[9,8,256]{2,1,0:T(8,128)S(1)}, u32[]{:S(2)}, u32[]{:S(2)}) %collective-permute-start.4) | collective-permute-done | bytes 73760 | tf_op jit(solution)/shard_map/ppermute | solution.py:613
  38.4 0.0 collective-permute-done.5.r_ref
  38.4 4.2 %all-to-all-done.got_ref = f32[32,16,128]{2,1,0:T(8,128)S(1)} async-done(((f32[32,16,128]{2,1,0:T(8,128)}), f32[32,16,128]{2,1,0:T(8,128)S(1)}, u32[]{:S(2)}, u32[]{:S(2)}) %all-to-all-start) | async-done | bytes 262176 | tf_op jit(solution)/shard_map/all_to_all | solution.py:653
  42.6 5.1 %shard_map.32 = f32[768,128]{1,0:T(8,128)} custom-call(f32[32,16,128]{2,1,0:T(8,128)S(1)} %all-to-all-done.got_ref, f32[9,8,256]{2,1,0:T(8,128)S(1)} %collective-permute-done.4.l_ref, f32[9,8,256]{2,1,0:T(8,128)S(1)} %collective-permute-done.5.r_ref, f32[3,10,8,640]{3,2,1,0:T(8,128)S(1)} %get-tuple-element.27.x1, ...), custom_call_target="tpu_custom_call" | custom-call | tf_op jit(solution)/shard_map/pallas_call | solution.py:601
Async XLA Ops:
  0.0 7.4 %copy-start = (f32[4,3,8,8,128]{4,3,2,1,0:T(8,128)S(1)}, f32[4,3,8,8,128]{4,3,2,1,0:T(8,128)}, u32[]{:S(2)}) copy-start(f32[4,3,8,8,128]{4,3,2,1,0:T(8,128)} %param.2) | copy-start | bytes 1179652
  0.0 7.4 %copy-start.1 = (s32[8,8,128]{2,1,0:T(8,128)S(1)}, s32[8,8,128]{2,1,0:T(8,128)}, u32[]{:S(2)}) copy-start(s32[8,8,128]{2,1,0:T(8,128)} %param.3) | copy-start | bytes 98308
  2.2 7.5 %collective-permute-start = (f32[13,8,128]{2,1,0:T(8,128)}, f32[13,8,128]{2,1,0:T(8,128)S(1)}, u32[]{:S(2)}, u32[]{:S(2)}) collective-permute-start(f32[13,8,128]{2,1,0:T(8,128)} %get-tuple-element.19), channel_id=1, source_target_pairs={{0,1},{1,2},{2,3},{3,0},{4,5},{5,6},{6,7},{7,4},{8,9},{9,10},{10,1... | collective-permute-start | bytes 159752 | tf_op jit(solution)/shard_map/ppermute | solution.py:613
  5.3 4.9 %collective-permute-start.1 = (f32[13,8,128]{2,1,0:T(8,128)}, f32[13,8,128]{2,1,0:T(8,128)S(1)}, u32[]{:S(2)}, u32[]{:S(2)}) collective-permute-start(f32[13,8,128]{2,1,0:T(8,128)} %get-tuple-element.20), channel_id=1, source_target_pairs={{0,3},{1,0},{2,1},{3,2},{4,7},{5,4},{6,5},{7,6},{8,11},{9,8},{10,9... | collective-permute-start | bytes 159752 | tf_op jit(solution)/shard_map/ppermute | solution.py:613
  10.6 10.8 %collective-permute-start.2 = (f32[20,8,640]{2,1,0:T(8,128)S(1)}, f32[20,8,640]{2,1,0:T(8,128)S(1)}, u32[]{:S(2)}, u32[]{:S(2)}) collective-permute-start(f32[20,8,640]{2,1,0:T(8,128)S(1)} %get-tuple-element.22), channel_id=1, source_target_pairs={{0,4},{4,8},{8,12},{12,16},{16,20},{20,24},{24,28},{28,0},{1,5},{5... | collective-permute-start | bytes 1228808 | tf_op jit(solution)/shard_map/ppermute | solution.py:613
  10.6 10.8 %collective-permute-start.3 = (f32[20,8,640]{2,1,0:T(8,128)S(1)}, f32[20,8,640]{2,1,0:T(8,128)S(1)}, u32[]{:S(2)}, u32[]{:S(2)}) collective-permute-start(f32[20,8,640]{2,1,0:T(8,128)S(1)} %get-tuple-element.23), channel_id=1, source_target_pairs={{0,28},{4,0},{8,4},{12,8},{16,12},{20,16},{24,20},{28,24},{1,29},{... | collective-permute-start | bytes 1228808 | tf_op jit(solution)/shard_map/ppermute | solution.py:613
  26.2 16.3 %all-to-all-start = ((f32[32,16,128]{2,1,0:T(8,128)}), f32[32,16,128]{2,1,0:T(8,128)S(1)}, u32[]{:S(2)}, u32[]{:S(2)}) async-start(f32[32,16,128]{2,1,0:T(8,128)} %get-tuple-element.24), calls=%async_computation | async-start | bytes 524288 | tf_op jit(solution)/shard_map/all_to_all | solution.py:653
  32.4 6.0 %collective-permute-start.4 = (f32[9,8,256]{2,1,0:T(8,128)S(1)}, f32[9,8,256]{2,1,0:T(8,128)S(1)}, u32[]{:S(2)}, u32[]{:S(2)}) collective-permute-start(f32[9,8,256]{2,1,0:T(8,128)S(1)} %get-tuple-element.25), channel_id=1, source_target_pairs={{0,4},{4,8},{8,12},{12,16},{16,20},{20,24},{24,28},{28,0},{1,5},{5... | collective-permute-start | bytes 221192 | tf_op jit(solution)/shard_map/ppermute | solution.py:613
  32.7 5.7 %collective-permute-start.5 = (f32[9,8,256]{2,1,0:T(8,128)S(1)}, f32[9,8,256]{2,1,0:T(8,128)S(1)}, u32[]{:S(2)}, u32[]{:S(2)}) collective-permute-start(f32[9,8,256]{2,1,0:T(8,128)S(1)} %get-tuple-element.26), channel_id=1, source_target_pairs={{0,28},{4,0},{8,4},{12,8},{16,12},{20,16},{24,20},{28,24},{1,29},{... | collective-permute-start | bytes 221192 | tf_op jit(solution)/shard_map/ppermute | solution.py:613

commit v6 on v5

--- a/solution.py
+++ b/solution.py
@@ -282,7 +282,7 @@
 def down_kernel(
     gx, own_ref, l_ref, r_ref,
     pay_ref, send_l, send_r, x1_ref, x2_ref, c0_ref, y1, y2_ref, k1,
-    x1, x2, k0, y2, cx, dr0, t0, p0, rest, stack, cstack, c1, dr1, f1, t1, p1, r1, stack1, pay,
+    x1, x2, k0, y2, cx, dr0, t0, p0, rest, stack, cstack, c1, dr1, f1, t1, p1, r1, stack1, pay, many, sems,
 ):
     place = lax.axis_index("gx")
     from_left = (place > 0).astype(F32)
@@ -404,11 +404,13 @@
         high = pltpu.roll(coarse1[64 + 8 * g : 72 + 8 * g], 2, 0)
         pay[pl.ds(8 * (g // 4), 8), pl.ds(32 * (g % 4), 32)] = jnp.where(first, low[:, :32], high[:, :32])
     packed = pay[...]
-
-    def copy(i):
-        pay_ref[i] = packed
-
-    each(0, pay_ref.shape[0], 8, copy)
+    batch = many.shape[0]
+    for i in range(batch):
+        many[i] = packed
+    copies = []
+    for i in range(pay_ref.shape[0] // batch):
+        copies.append(pltpu.make_async_copy(many, pay_ref.at[pl.ds(batch * i, batch)], sems.at[i]))
+        copies[-1].start()
     for c in range(COMP):
         for i in range(10):
             x1_ref[c, i] = x1[c, i + 5]
@@ -418,11 +420,13 @@
             y2_ref[c, i] = y2[c, i + 1]
     for i in range(12):
         c0_ref[i] = cx[i + 5]
+    for copy in copies:
+        copy.wait()
 
 
 def up_kernel(
-    gx, gy, got_ref, l_ref, r_ref, x1, x2, c0_ref, y1, y2, k1, out_ref,
-    c2, f2, k2, dr2, x1c, ua, ub, rc, t2, p2, s2, c3, k3, x1d, va, vb, t3, p3, s3, sw, w0, w1, t1, p1, sp, k0, u0, u1, t0, p0,
+    gx, gy, got_ref, l_ref, r_ref, x1, x2, c0_ref, y1, y2, k1, out_hbm,
+    c2, f2, k2, dr2, x1c, ua, ub, rc, t2, p2, s2, c3, k3, x1d, va, vb, t3, p3, s3, sw, w0, w1, t1, p1, sp, k0, u0, u1, t0, p0, out_ref, sems,
 ):
     nx2, nx3 = 2 * gx, gx
     yy2, l3 = 32 * gy, c3.shape[-1]
@@ -586,24 +590,30 @@
 
     a.apply(u1, 2, t0, p0, k0, 1, x1, 1, 0, BX, UNROLL0, write_last)
     near = iota((8, 128), 1) < SPLIT
-    for x in range(BX):
-        for c in range(COMP):
-            last = u0[c, x + 2, :, pl.ds(512, 128)]
-            for v in range(VEC):
+    copies = []
+    for v in range(VEC):
+        for c in range(COMP):
+            group = v * COMP + c
+            for x in range(BX):
                 main = pltpu.roll(u0[c, x + 2, :, pl.ds(128 * v, 128)], 128 - LEFT, 1)
-                ends = pltpu.roll(last, (PIECE - 32 * v) % 128, 1)
-                out_ref[pl.ds((v * COMP + c) * 64 + x, 8, stride=8), :] = jnp.where(near, main, ends)
-
-
-def call(kernel, outs, scratch, *args):
+                ends = pltpu.roll(u0[c, x + 2, :, pl.ds(512, 128)], (PIECE - 32 * v) % 128, 1)
+                out_ref[pl.ds(group * 64 + x, 8, stride=8), :] = jnp.where(near, main, ends)
+            rows = pl.ds(group * 64, 64)
+            copies.append(pltpu.make_async_copy(out_ref.at[rows], out_hbm.at[rows], sems.at[group]))
+            copies[-1].start()
+    for copy in copies:
+        copy.wait()
+
+
+def call(kernel, outs, scratch, *args, far=False):
     vmem = pl.BlockSpec(memory_space=pltpu.VMEM)
     shapes = [jax.ShapeDtypeStruct(s, F32) for s in outs]
     return pl.pallas_call(
         kernel,
         out_shape=shapes,
         in_specs=[vmem] * len(args),
-        out_specs=[vmem] * len(outs),
-        scratch_shapes=[pltpu.VMEM(s, F32) for s in scratch],
+        out_specs=[pl.BlockSpec(memory_space=pltpu.HBM) if far and i == 0 else vmem for i in range(len(outs))],
+        scratch_shapes=[pltpu.VMEM(s, F32) if isinstance(s, tuple) else s for s in scratch],
         compiler_params=pltpu.CompilerParams(vmem_limit_bytes=48 * 1024 * 1024),
     )(*args)
 
@@ -622,7 +632,7 @@
         in_specs=[hbm] * 2,
         out_specs=[vmem] * 2,
         scratch_shapes=[pltpu.VMEM(f.shape, F32), pltpu.VMEM(m.shape, jnp.int32), pltpu.SemaphoreType.DMA((VEC + 1,))],
-        compiler_params=pltpu.CompilerParams(vmem_limit_bytes=61 * 1024 * 1024),
+        compiler_params=pltpu.CompilerParams(vmem_limit_bytes=65126 * 1024),
     )(f, m)
     right = ring(to_left, "gy", gy, -1)
     left = ring(to_right, "gy", gy, 1)
@@ -644,9 +654,9 @@
         [
             plane(3, nf), plane(3, nf), (13, nf, 8, K0), plane1(3, 6),
             (nc, 8, K0), (nf, 8, K0), plane(nf), plane(nf), plane(3, 16), (192, L0), (80, K0), (10, 8, 128),
-            (8, 8, 128), plane1(3, 8), plane1(10), plane1(10), plane1(3, 4), (128, 128), (16, 128),
+            (8, 8, 128), plane1(3, 8), plane1(10), plane1(10), plane1(3, 4), (128, 128), (16, 128), (8, 16, 128), pltpu.SemaphoreType.DMA((n // 8,)),
         ],
-        own, left, right,
+        own, left, right, far=True,
     )
     right = ring(to_left, "gx", gx, -1)
     left = ring(to_right, "gx", gx, 1)
@@ -662,9 +672,9 @@
             plane2(3, nx2), plane2(nx2 + 2), plane2(nx2 + 2), (32 * nx3, y2),
             plane3(nx3 + 2), plane3(13, nx3), plane3(3, nx3), plane3(3, nx3 + 2), plane3(3, nx3 + 2), plane3(nx3 + 2), plane3(nx3 + 2),
             (24 * nx3, l3), (288, y2), plane1(3, 10), plane1(3, 10), plane1(10), plane1(10), (4, 144, 128), (13, 10, 8, K0),
-            plane(3, 12), plane(3, 12), plane(12), plane(12),
+            plane(3, 12), plane(3, 12), plane(12), plane(12), f.shape, pltpu.SemaphoreType.DMA((VEC * COMP,)),
         ],
-        got, left, right, *kept,
+        got, left, right, *kept, far=True,
     )
     return out.reshape(right_side.shape)
 

time: 47.9 us -> 47.7 us (level)
  waiting for transfers between devices: 18.2 us -> 17.2 us
  local copies, waits for them, and re-layouts: 0.01 us -> 1 us
    ppermute x6, waiting for transfers between devices: 14 us -> 13 us  [ring(): lax.ppermute(value, axis, [(i, (i + step) % size) for i in range(size)])]
    unnamed x4, local copies, waits for them, and re-layouts: 0.01 us -> 1 us
where the time goes in v6:
time: 47.7 us; the launch traced here: 47.5 us
  waiting for transfers between devices  17.2 us (36%)
  starting transfers between devices  16.7 us (35%)
  Pallas kernels  12.6 us (26%)
  local copies, waits for them, and re-layouts  1 us (2%)
    ppermute x6, waiting for transfers between devices, ring(): lax.ppermute(value, axis, [(i, (i + step) % size) for i in range(size)])  13 us
    ppermute x6, starting transfers between devices, ring(): lax.ppermute(value, axis, [(i, (i + step) % size) for i in range(size)])  10.6 us
    pallas_call x4, Pallas kernels, call(): pl.pallas_call(kernel, out_shape=shapes, in_specs=[vmem] * len(args), out...  10.4 us
    all_to_all x1, starting transfers between devices, per_device(): got = lax.all_to_all(pay, ('gx', 'gy'), 0, 0)  6.15 us
    all_to_all x1, waiting for transfers between devices, per_device(): got = lax.all_to_all(pay, ('gx', 'gy'), 0, 0)  4.19 us
    pallas_call x1, Pallas kernels, per_device(): pl.pallas_call(edge_kernel, out_shape=[jax.ShapeDtypeStruct(s, F32) for s...  2.12 us
    unnamed x4, local copies, waits for them, and re-layouts  1 us
  transfers between devices with their start and end apart: 7, of which 5 were waited for; matrix products, arithmetic and copies ran while one was open for 0% of the time, Pallas kernels for 1%

profile of v6, /device:TPU:0, one launch (start us, length us, event | category | flops | bytes accessed | tf_op | source)
XLA Modules:
  0.0 47.5 jit_solution(14974092696119463770)
XLA Ops:
  0.0 0.0 copy-start.1
  0.0 2.1 %shard_map.29 = (f32[13,8,128]{2,1,0:T(8,128)}, f32[13,8,128]{2,1,0:T(8,128)}) custom-call(f32[768,128]{1,0:T(8,128)} %bitcast.3, s32[64,128]{1,0:T(8,128)} %bitcast.5), custom_call_target="tpu_custom_call" | custom-call | tf_op jit(solution)/shard_map/pallas_call | solution.py:629
  2.1 3.1 %collective-permute-start = (f32[13,8,128]{2,1,0:T(8,128)}, f32[13,8,128]{2,1,0:T(8,128)S(1)}, u32[]{:S(2)}, u32[]{:S(2)}) collective-permute-start(f32[13,8,128]{2,1,0:T(8,128)} %get-tuple-element.19), channel_id=1, source_target_pairs={{0,1},{1,2},{2,3},{3,0},{4,5},{5,6},{6,7},{7,4},{8,9},{9,10},{10,1... | collective-permute-start | bytes 159752 | tf_op jit(solution)/shard_map/ppermute | solution.py:623
  5.2 2.1 %collective-permute-start.1 = (f32[13,8,128]{2,1,0:T(8,128)}, f32[13,8,128]{2,1,0:T(8,128)S(1)}, u32[]{:S(2)}, u32[]{:S(2)}) collective-permute-start(f32[13,8,128]{2,1,0:T(8,128)} %get-tuple-element.20), channel_id=1, source_target_pairs={{0,3},{1,0},{2,1},{3,2},{4,7},{5,4},{6,5},{7,6},{8,11},{9,8},{10,9... | collective-permute-start | bytes 159752 | tf_op jit(solution)/shard_map/ppermute | solution.py:623
  7.3 0.0 copy-done.1
  7.3 0.0 copy-start
  7.3 1.0 %copy-done = f32[4,3,8,8,128]{4,3,2,1,0:T(8,128)S(1)} copy-done((f32[4,3,8,8,128]{4,3,2,1,0:T(8,128)S(1)}, f32[4,3,8,8,128]{4,3,2,1,0:T(8,128)}, u32[]{:S(2)}) %copy-start) | copy-done | bytes 393240
  8.3 0.3 shard_map.28.placed_ref
  8.6 1.0 %collective-permute-done.l_ref = f32[13,8,128]{2,1,0:T(8,128)S(1)} collective-permute-done((f32[13,8,128]{2,1,0:T(8,128)}, f32[13,8,128]{2,1,0:T(8,128)S(1)}, u32[]{:S(2)}, u32[]{:S(2)}) %collective-permute-start) | collective-permute-done | bytes 53280 | tf_op jit(solution)/shard_map/ppermute | solution.py:623
  9.6 0.5 %collective-permute-done.1.r_ref = f32[13,8,128]{2,1,0:T(8,128)S(1)} collective-permute-done((f32[13,8,128]{2,1,0:T(8,128)}, f32[13,8,128]{2,1,0:T(8,128)S(1)}, u32[]{:S(2)}, u32[]{:S(2)}) %collective-permute-start.1) | collective-permute-done | bytes 53280 | tf_op jit(solution)/shard_map/ppermute | solution.py:623
  10.1 0.4 shard_map.30
  10.5 0.1 collective-permute-start.2
  10.6 2.6 %collective-permute-start.3 = (f32[20,8,640]{2,1,0:T(8,128)S(1)}, f32[20,8,640]{2,1,0:T(8,128)S(1)}, u32[]{:S(2)}, u32[]{:S(2)}) collective-permute-start(f32[20,8,640]{2,1,0:T(8,128)S(1)} %get-tuple-element.23), channel_id=1, source_target_pairs={{0,28},{4,0},{8,4},{12,8},{16,12},{20,16},{24,20},{28,24},{1,29},{... | collective-permute-start | bytes 1228808 | tf_op jit(solution)/shard_map/ppermute | solution.py:623
  13.2 8.1 %collective-permute-done.2.l_ref = f32[20,8,640]{2,1,0:T(8,128)S(1)} collective-permute-done((f32[20,8,640]{2,1,0:T(8,128)S(1)}, f32[20,8,640]{2,1,0:T(8,128)S(1)}, u32[]{:S(2)}, u32[]{:S(2)}) %collective-permute-start.2) | collective-permute-done | bytes 409632 | tf_op jit(solution)/shard_map/ppermute | solution.py:623
  21.3 0.0 collective-permute-done.3.r_ref
  21.3 4.7 %shard_map.31 = (f32[32,16,128]{2,1,0:T(8,128)}, f32[9,8,256]{2,1,0:T(8,128)S(1)}, f32[9,8,256]{2,1,0:T(8,128)S(1)}, f32[3,10,8,640]{3,2,1,0:T(8,128)S(1)}, f32[...) custom-call(f32[26,8,640]{2,1,0:T(8,128)S(1)} %get-tuple-element.21., ...), custom_call_target="tpu_custom_call" | custom-call | tf_op jit(solution)/shard_map/pallas_call | solution.py:611
  26.0 6.1 %all-to-all-start = ((f32[32,16,128]{2,1,0:T(8,128)}), f32[32,16,128]{2,1,0:T(8,128)S(1)}, u32[]{:S(2)}, u32[]{:S(2)}) async-start(f32[32,16,128]{2,1,0:T(8,128)} %get-tuple-element.24), calls=%async_computation | async-start | bytes 524288 | tf_op jit(solution)/shard_map/all_to_all | solution.py:663
  32.2 0.3 collective-permute-start.4
  32.5 2.4 %collective-permute-start.5 = (f32[9,8,256]{2,1,0:T(8,128)S(1)}, f32[9,8,256]{2,1,0:T(8,128)S(1)}, u32[]{:S(2)}, u32[]{:S(2)}) collective-permute-start(f32[9,8,256]{2,1,0:T(8,128)S(1)} %get-tuple-element.26), channel_id=1, source_target_pairs={{0,28},{4,0},{8,4},{12,8},{16,12},{20,16},{24,20},{28,24},{1,29},{... | collective-permute-start | bytes 221192 | tf_op jit(solution)/shard_map/ppermute | solution.py:623
  34.9 3.3 %collective-permute-done.4.l_ref = f32[9,8,256]{2,1,0:T(8,128)S(1)} collective-permute-done((f32[9,8,256]{2,1,0:T(8,128)S(1)}, f32[9,8,256]{2,1,0:T(8,128)S(1)}, u32[]{:S(2)}, u32[]{:S(2)}) %collective-permute-start.4) | collective-permute-done | bytes 73760 | tf_op jit(solution)/shard_map/ppermute | solution.py:623
  38.2 0.0 collective-permute-done.5.r_ref
  38.2 4.2 %all-to-all-done.got_ref = f32[32,16,128]{2,1,0:T(8,128)S(1)} async-done(((f32[32,16,128]{2,1,0:T(8,128)}), f32[32,16,128]{2,1,0:T(8,128)S(1)}, u32[]{:S(2)}, u32[]{:S(2)}) %all-to-all-start) | async-done | bytes 262176 | tf_op jit(solution)/shard_map/all_to_all | solution.py:663
  42.4 5.1 %shard_map.32 = f32[768,128]{1,0:T(8,128)} custom-call(f32[32,16,128]{2,1,0:T(8,128)S(1)} %all-to-all-done.got_ref, f32[9,8,256]{2,1,0:T(8,128)S(1)} %collective-permute-done.4.l_ref, f32[9,8,256]{2,1,0:T(8,128)S(1)} %collective-permute-done.5.r_ref, f32[3,10,8,640]{3,2,1,0:T(8,128)S(1)} %get-tuple-element.27.x1, ...), custom_call_target="tpu_custom_call" | custom-call | tf_op jit(solution)/shard_map/pallas_call | solution.py:611
Async XLA Ops:
  0.0 7.3 %copy-start.1 = (s32[8,8,128]{2,1,0:T(8,128)S(1)}, s32[8,8,128]{2,1,0:T(8,128)}, u32[]{:S(2)}) copy-start(s32[8,8,128]{2,1,0:T(8,128)} %param.3) | copy-start | bytes 98308
  2.1 7.5 %collective-permute-start = (f32[13,8,128]{2,1,0:T(8,128)}, f32[13,8,128]{2,1,0:T(8,128)S(1)}, u32[]{:S(2)}, u32[]{:S(2)}) collective-permute-start(f32[13,8,128]{2,1,0:T(8,128)} %get-tuple-element.19), channel_id=1, source_target_pairs={{0,1},{1,2},{2,3},{3,0},{4,5},{5,6},{6,7},{7,4},{8,9},{9,10},{10,1... | collective-permute-start | bytes 159752 | tf_op jit(solution)/shard_map/ppermute | solution.py:623
  5.2 4.9 %collective-permute-start.1 = (f32[13,8,128]{2,1,0:T(8,128)}, f32[13,8,128]{2,1,0:T(8,128)S(1)}, u32[]{:S(2)}, u32[]{:S(2)}) collective-permute-start(f32[13,8,128]{2,1,0:T(8,128)} %get-tuple-element.20), channel_id=1, source_target_pairs={{0,3},{1,0},{2,1},{3,2},{4,7},{5,4},{6,5},{7,6},{8,11},{9,8},{10,9... | collective-permute-start | bytes 159752 | tf_op jit(solution)/shard_map/ppermute | solution.py:623
  7.3 1.0 %copy-start = (f32[4,3,8,8,128]{4,3,2,1,0:T(8,128)S(1)}, f32[4,3,8,8,128]{4,3,2,1,0:T(8,128)}, u32[]{:S(2)}) copy-start(f32[4,3,8,8,128]{4,3,2,1,0:T(8,128)} %param.2) | copy-start | bytes 1179652
  10.5 10.8 %collective-permute-start.2 = (f32[20,8,640]{2,1,0:T(8,128)S(1)}, f32[20,8,640]{2,1,0:T(8,128)S(1)}, u32[]{:S(2)}, u32[]{:S(2)}) collective-permute-start(f32[20,8,640]{2,1,0:T(8,128)S(1)} %get-tuple-element.22), channel_id=1, source_target_pairs={{0,4},{4,8},{8,12},{12,16},{16,20},{20,24},{24,28},{28,0},{1,5},{5... | collective-permute-start | bytes 1228808 | tf_op jit(solution)/shard_map/ppermute | solution.py:623
  10.6 10.8 %collective-permute-start.3 = (f32[20,8,640]{2,1,0:T(8,128)S(1)}, f32[20,8,640]{2,1,0:T(8,128)S(1)}, u32[]{:S(2)}, u32[]{:S(2)}) collective-permute-start(f32[20,8,640]{2,1,0:T(8,128)S(1)} %get-tuple-element.23), channel_id=1, source_target_pairs={{0,28},{4,0},{8,4},{12,8},{16,12},{20,16},{24,20},{28,24},{1,29},{... | collective-permute-start | bytes 1228808 | tf_op jit(solution)/shard_map/ppermute | solution.py:623
  26.0 16.4 %all-to-all-start = ((f32[32,16,128]{2,1,0:T(8,128)}), f32[32,16,128]{2,1,0:T(8,128)S(1)}, u32[]{:S(2)}, u32[]{:S(2)}) async-start(f32[32,16,128]{2,1,0:T(8,128)} %get-tuple-element.24), calls=%async_computation | async-start | bytes 524288 | tf_op jit(solution)/shard_map/all_to_all | solution.py:663
  32.2 6.0 %collective-permute-start.4 = (f32[9,8,256]{2,1,0:T(8,128)S(1)}, f32[9,8,256]{2,1,0:T(8,128)S(1)}, u32[]{:S(2)}, u32[]{:S(2)}) collective-permute-start(f32[9,8,256]{2,1,0:T(8,128)S(1)} %get-tuple-element.25), channel_id=1, source_target_pairs={{0,4},{4,8},{8,12},{12,16},{16,20},{20,24},{24,28},{28,0},{1,5},{5... | collective-permute-start | bytes 221192 | tf_op jit(solution)/shard_map/ppermute | solution.py:623
  32.5 5.7 %collective-permute-start.5 = (f32[9,8,256]{2,1,0:T(8,128)S(1)}, f32[9,8,256]{2,1,0:T(8,128)S(1)}, u32[]{:S(2)}, u32[]{:S(2)}) collective-permute-start(f32[9,8,256]{2,1,0:T(8,128)S(1)} %get-tuple-element.26), channel_id=1, source_target_pairs={{0,28},{4,0},{8,4},{12,8},{16,12},{20,16},{24,20},{28,24},{1,29},{... | collective-permute-start | bytes 221192 | tf_op jit(solution)/shard_map/ppermute | solution.py:623

commit v7 on v6

--- a/solution.py
+++ b/solution.py
@@ -19,6 +19,7 @@
 SPLIT = 112
 L0 = 5 * 128
 K0 = 2 * 128
+PAY = 13
 L1 = 2 * 128
 FX = 6
 CX = 7
@@ -399,14 +400,23 @@
     selector1 = bf16((lane >> 1 == iota((128, 128), 1)) & (lane >= 0) & (lane < 64), 0.125)
     coarse1 = exact_dot(parts_of(stack1[...]), selector1)
     first = (iota((8, 32), 0) & 2) == 0
+    blocks = []
     for g in range(8):
         low = coarse1[8 * g : 8 * g + 8]
         high = pltpu.roll(coarse1[64 + 8 * g : 72 + 8 * g], 2, 0)
-        pay[pl.ds(8 * (g // 4), 8), pl.ds(32 * (g % 4), 32)] = jnp.where(first, low[:, :32], high[:, :32])
-    packed = pay[...]
+        blocks.append(jnp.where(first, low[:, :32], high[:, :32]))
+    for g in range(4):
+        pay[pl.ds(0, 8), pl.ds(32 * g, 32)] = blocks[g]
+    for g in range(2):
+        pay[pl.ds(8, 4), pl.ds(32 * g, 32)] = blocks[4 + g][:4]
+        pay[pl.ds(8, 4), pl.ds(64 + 32 * g, 32)] = blocks[4 + g][4:]
+        pay[pl.ds(12, 1), pl.ds(64 * g, 32)] = blocks[6 + g][:1]
+        pay[pl.ds(12, 1), pl.ds(64 * g + 32, 32)] = blocks[6 + g][4:5]
     batch = many.shape[0]
-    for i in range(batch):
-        many[i] = packed
+    for r in range(PAY):
+        row = pay[pl.ds(r, 1), :]
+        for i in range(batch):
+            many[i, :, pl.ds(128 * r, 128)] = row
     copies = []
     for i in range(pay_ref.shape[0] // batch):
         copies.append(pltpu.make_async_copy(many, pay_ref.at[pl.ds(batch * i, batch)], sems.at[i]))
@@ -425,8 +435,8 @@
 
 
 def up_kernel(
-    gx, gy, got_ref, l_ref, r_ref, x1, x2, c0_ref, y1, y2, k1, out_hbm,
-    c2, f2, k2, dr2, x1c, ua, ub, rc, t2, p2, s2, c3, k3, x1d, va, vb, t3, p3, s3, sw, w0, w1, t1, p1, sp, k0, u0, u1, t0, p0, out_ref, sems,
+    gx, gy, got_ref, l_ref, r_ref, x1, x2, c0_ref, y1, y2, k1, out_ref,
+    c2, f2, k2, dr2, x1c, ua, ub, rc, t2, p2, s2, c3, k3, x1d, va, vb, t3, p3, s3, sw, w0, w1, t1, p1, sp, k0, u0, u1, t0, p0, gs,
 ):
     nx2, nx3 = 2 * gx, gx
     yy2, l3 = 32 * gy, c3.shape[-1]
@@ -445,12 +455,16 @@
 
     def unpack(i):
         for j in range(gy):
-            for g in range(8):
-                block = got_ref[i * gy + j, pl.ds(8 * (g // 4), 8), pl.ds(32 * (g % 4), 32)]
-                if g < 6:
-                    f2[g // 2, 2 * i + g % 2, :, pl.ds(32 * j, 32)] = block
-                else:
-                    c2[2 * i + g - 5, :, pl.ds(32 * j, 32)] = block
+            at, lanes = i * gy + j, pl.ds(32 * j, 32)
+            for r in range(PAY - 1):
+                gs[at, pl.ds(r, 1), :] = got_ref[at, :, pl.ds(128 * r, 128)]
+            for g in range(4):
+                f2[g // 2, 2 * i + g % 2, :, lanes] = gs[at, pl.ds(0, 8), pl.ds(32 * g, 32)]
+            for g in range(2):
+                for half in range(2):
+                    f2[2, 2 * i + g, pl.ds(4 * half, 4), lanes] = gs[at, pl.ds(8, 4), pl.ds(64 * half + 32 * g, 32)]
+                    row = got_ref[at, :, pl.ds(128 * (PAY - 1) + 64 * g + 32 * half, 32)]
+                    c2[2 * i + g + 1, pl.ds(4 * half, 4), lanes] = jnp.broadcast_to(row, (4, 32))
 
     each(0, gx, 8, unpack)
     m = Level(2, 4, yy2, (0,), yy2)
@@ -590,19 +604,13 @@
 
     a.apply(u1, 2, t0, p0, k0, 1, x1, 1, 0, BX, UNROLL0, write_last)
     near = iota((8, 128), 1) < SPLIT
-    copies = []
-    for v in range(VEC):
-        for c in range(COMP):
-            group = v * COMP + c
-            for x in range(BX):
+    for x in range(BX):
+        for c in range(COMP):
+            last = u0[c, x + 2, :, pl.ds(512, 128)]
+            for v in range(VEC):
                 main = pltpu.roll(u0[c, x + 2, :, pl.ds(128 * v, 128)], 128 - LEFT, 1)
-                ends = pltpu.roll(u0[c, x + 2, :, pl.ds(512, 128)], (PIECE - 32 * v) % 128, 1)
-                out_ref[pl.ds(group * 64 + x, 8, stride=8), :] = jnp.where(near, main, ends)
-            rows = pl.ds(group * 64, 64)
-            copies.append(pltpu.make_async_copy(out_ref.at[rows], out_hbm.at[rows], sems.at[group]))
-            copies[-1].start()
-    for copy in copies:
-        copy.wait()
+                ends = pltpu.roll(last, (PIECE - 32 * v) % 128, 1)
+                out_ref[pl.ds((v * COMP + c) * 64 + x, 8, stride=8), :] = jnp.where(near, main, ends)
 
 
 def call(kernel, outs, scratch, *args, far=False):
@@ -649,12 +657,12 @@
     pay, to_left, to_right, *kept = call(
         functools.partial(down_kernel, gx),
         [
-            (n, 16, 128), plane1(9), plane1(9), plane(3, 10), plane(3, 12), (12, 8, K0), plane1(3, 8), plane1(3, 4), (13, 8, 8, 128),
+            (n, 1, 128 * PAY), plane1(9), plane1(9), plane(3, 10), plane(3, 12), (12, 8, K0), plane1(3, 8), plane1(3, 4), (13, 8, 8, 128),
         ],
         [
             plane(3, nf), plane(3, nf), (13, nf, 8, K0), plane1(3, 6),
             (nc, 8, K0), (nf, 8, K0), plane(nf), plane(nf), plane(3, 16), (192, L0), (80, K0), (10, 8, 128),
-            (8, 8, 128), plane1(3, 8), plane1(10), plane1(10), plane1(3, 4), (128, 128), (16, 128), (8, 16, 128), pltpu.SemaphoreType.DMA((n // 8,)),
+            (8, 8, 128), plane1(3, 8), plane1(10), plane1(10), plane1(3, 4), (128, 128), (16, 128), (8, 1, 128 * PAY), pltpu.SemaphoreType.DMA((n // 8,)),
         ],
         own, left, right, far=True,
     )
@@ -672,9 +680,9 @@
             plane2(3, nx2), plane2(nx2 + 2), plane2(nx2 + 2), (32 * nx3, y2),
             plane3(nx3 + 2), plane3(13, nx3), plane3(3, nx3), plane3(3, nx3 + 2), plane3(3, nx3 + 2), plane3(nx3 + 2), plane3(nx3 + 2),
             (24 * nx3, l3), (288, y2), plane1(3, 10), plane1(3, 10), plane1(10), plane1(10), (4, 144, 128), (13, 10, 8, K0),
-            plane(3, 12), plane(3, 12), plane(12), plane(12), f.shape, pltpu.SemaphoreType.DMA((VEC * COMP,)),
+            plane(3, 12), plane(3, 12), plane(12), plane(12), (n, 16, 128),
         ],
-        got, left, right, *kept, far=True,
+        got, left, right, *kept,
     )
     return out.reshape(right_side.shape)
 

time: 47.7 us -> 47.2 us (0.990)
  waiting for transfers between devices: 17.2 us -> 16.5 us
where the time goes in v7:
time: 47.2 us; the launch traced here: 46.9 us
  starting transfers between devices  16.7 us (35%)
  waiting for transfers between devices  16.5 us (35%)
  Pallas kernels  12.7 us (27%)
  local copies, waits for them, and re-layouts  1 us (2%)
    ppermute x6, waiting for transfers between devices, ring(): lax.ppermute(value, axis, [(i, (i + step) % size) for i in range(size)])  12.7 us
    ppermute x6, starting transfers between devices, ring(): lax.ppermute(value, axis, [(i, (i + step) % size) for i in range(size)])  10.6 us
    pallas_call x4, Pallas kernels, call(): pl.pallas_call(kernel, out_shape=shapes, in_specs=[vmem] * len(args), out...  10.5 us
    all_to_all x1, starting transfers between devices, per_device(): got = lax.all_to_all(pay, ('gx', 'gy'), 0, 0)  6.15 us
    all_to_all x1, waiting for transfers between devices, per_device(): got = lax.all_to_all(pay, ('gx', 'gy'), 0, 0)  3.82 us
    pallas_call x1, Pallas kernels, per_device(): pl.pallas_call(edge_kernel, out_shape=[jax.ShapeDtypeStruct(s, F32) for s...  2.12 us
    unnamed x4, local copies, waits for them, and re-layouts  1 us
  transfers between devices with their start and end apart: 7, of which 5 were waited for; matrix products, arithmetic and copies ran while one was open for 0% of the time, Pallas kernels for 1%

profile of v7, /device:TPU:0, one launch (start us, length us, event | category | flops | bytes accessed | tf_op | source)
XLA Modules:
  0.0 46.9 jit_solution(7522251883490650489)
XLA Ops:
  0.0 0.0 copy-start.1
  0.0 2.1 %shard_map.29 = (f32[13,8,128]{2,1,0:T(8,128)}, f32[13,8,128]{2,1,0:T(8,128)}) custom-call(f32[768,128]{1,0:T(8,128)} %bitcast.3, s32[64,128]{1,0:T(8,128)} %bitcast.5), custom_call_target="tpu_custom_call" | custom-call | tf_op jit(solution)/shard_map/pallas_call | solution.py:637
  2.1 3.1 %collective-permute-start = (f32[13,8,128]{2,1,0:T(8,128)}, f32[13,8,128]{2,1,0:T(8,128)S(1)}, u32[]{:S(2)}, u32[]{:S(2)}) collective-permute-start(f32[13,8,128]{2,1,0:T(8,128)} %get-tuple-element.19), channel_id=1, source_target_pairs={{0,1},{1,2},{2,3},{3,0},{4,5},{5,6},{6,7},{7,4},{8,9},{9,10},{10,1... | collective-permute-start | bytes 159752 | tf_op jit(solution)/shard_map/ppermute | solution.py:631
  5.2 2.1 %collective-permute-start.1 = (f32[13,8,128]{2,1,0:T(8,128)}, f32[13,8,128]{2,1,0:T(8,128)S(1)}, u32[]{:S(2)}, u32[]{:S(2)}) collective-permute-start(f32[13,8,128]{2,1,0:T(8,128)} %get-tuple-element.20), channel_id=1, source_target_pairs={{0,3},{1,0},{2,1},{3,2},{4,7},{5,4},{6,5},{7,6},{8,11},{9,8},{10,9... | collective-permute-start | bytes 159752 | tf_op jit(solution)/shard_map/ppermute | solution.py:631
  7.3 0.0 copy-done.1
  7.3 0.0 copy-start
  7.3 1.0 %copy-done = f32[4,3,8,8,128]{4,3,2,1,0:T(8,128)S(1)} copy-done((f32[4,3,8,8,128]{4,3,2,1,0:T(8,128)S(1)}, f32[4,3,8,8,128]{4,3,2,1,0:T(8,128)}, u32[]{:S(2)}) %copy-start) | copy-done | bytes 393240
  8.3 0.3 shard_map.28.placed_ref
  8.6 1.0 %collective-permute-done.l_ref = f32[13,8,128]{2,1,0:T(8,128)S(1)} collective-permute-done((f32[13,8,128]{2,1,0:T(8,128)}, f32[13,8,128]{2,1,0:T(8,128)S(1)}, u32[]{:S(2)}, u32[]{:S(2)}) %collective-permute-start) | collective-permute-done | bytes 53280 | tf_op jit(solution)/shard_map/ppermute | solution.py:631
  9.6 0.5 %collective-permute-done.1.r_ref = f32[13,8,128]{2,1,0:T(8,128)S(1)} collective-permute-done((f32[13,8,128]{2,1,0:T(8,128)}, f32[13,8,128]{2,1,0:T(8,128)S(1)}, u32[]{:S(2)}, u32[]{:S(2)}) %collective-permute-start.1) | collective-permute-done | bytes 53280 | tf_op jit(solution)/shard_map/ppermute | solution.py:631
  10.1 0.4 shard_map.30
  10.5 0.1 collective-permute-start.2
  10.6 2.6 %collective-permute-start.3 = (f32[20,8,640]{2,1,0:T(8,128)S(1)}, f32[20,8,640]{2,1,0:T(8,128)S(1)}, u32[]{:S(2)}, u32[]{:S(2)}) collective-permute-start(f32[20,8,640]{2,1,0:T(8,128)S(1)} %get-tuple-element.23), channel_id=1, source_target_pairs={{0,28},{4,0},{8,4},{12,8},{16,12},{20,16},{24,20},{28,24},{1,29},{... | collective-permute-start | bytes 1228808 | tf_op jit(solution)/shard_map/ppermute | solution.py:631
  13.2 8.1 %collective-permute-done.2.l_ref = f32[20,8,640]{2,1,0:T(8,128)S(1)} collective-permute-done((f32[20,8,640]{2,1,0:T(8,128)S(1)}, f32[20,8,640]{2,1,0:T(8,128)S(1)}, u32[]{:S(2)}, u32[]{:S(2)}) %collective-permute-start.2) | collective-permute-done | bytes 409632 | tf_op jit(solution)/shard_map/ppermute | solution.py:631
  21.3 0.0 collective-permute-done.3.r_ref
  21.3 4.7 %shard_map.31 = (f32[32,1,1664]{2,1,0:T(1,128)}, f32[9,8,256]{2,1,0:T(8,128)S(1)}, f32[9,8,256]{2,1,0:T(8,128)S(1)}, f32[3,10,8,640]{3,2,1,0:T(8,128)S(1)}, f32[...) custom-call(f32[26,8,640]{2,1,0:T(8,128)S(1)} %get-tuple-element.21., ...), custom_call_target="tpu_custom_call" | custom-call | tf_op jit(solution)/shard_map/pallas_call | solution.py:619
  26.0 6.1 %all-to-all-start = ((f32[32,1,1664]{2,1,0:T(1,128)}), f32[32,1,1664]{2,1,0:T(1,128)S(1)}, u32[]{:S(2)}, u32[]{:S(2)}) async-start(f32[32,1,1664]{2,1,0:T(1,128)} %get-tuple-element.24), calls=%async_computation | async-start | bytes 425984 | tf_op jit(solution)/shard_map/all_to_all | solution.py:671
  32.2 0.3 collective-permute-start.4
  32.5 2.4 %collective-permute-start.5 = (f32[9,8,256]{2,1,0:T(8,128)S(1)}, f32[9,8,256]{2,1,0:T(8,128)S(1)}, u32[]{:S(2)}, u32[]{:S(2)}) collective-permute-start(f32[9,8,256]{2,1,0:T(8,128)S(1)} %get-tuple-element.26), channel_id=1, source_target_pairs={{0,28},{4,0},{8,4},{12,8},{16,12},{20,16},{24,20},{28,24},{1,29},{... | collective-permute-start | bytes 221192 | tf_op jit(solution)/shard_map/ppermute | solution.py:631
  34.9 3.0 %collective-permute-done.4.l_ref = f32[9,8,256]{2,1,0:T(8,128)S(1)} collective-permute-done((f32[9,8,256]{2,1,0:T(8,128)S(1)}, f32[9,8,256]{2,1,0:T(8,128)S(1)}, u32[]{:S(2)}, u32[]{:S(2)}) %collective-permute-start.4) | collective-permute-done | bytes 73760 | tf_op jit(solution)/shard_map/ppermute | solution.py:631
  37.9 0.0 collective-permute-done.5.r_ref
  37.9 3.8 %all-to-all-done.got_ref = f32[32,1,1664]{2,1,0:T(1,128)S(1)} async-done(((f32[32,1,1664]{2,1,0:T(1,128)}), f32[32,1,1664]{2,1,0:T(1,128)S(1)}, u32[]{:S(2)}, u32[]{:S(2)}) %all-to-all-start) | async-done | bytes 213024 | tf_op jit(solution)/shard_map/all_to_all | solution.py:671
  41.8 5.2 %shard_map.32 = f32[768,128]{1,0:T(8,128)} custom-call(f32[32,1,1664]{2,1,0:T(1,128)S(1)} %all-to-all-done.got_ref, f32[9,8,256]{2,1,0:T(8,128)S(1)} %collective-permute-done.4.l_ref, f32[9,8,256]{2,1,0:T(8,128)S(1)} %collective-permute-done.5.r_ref, f32[3,10,8,640]{3,2,1,0:T(8,128)S(1)} %get-tuple-element.27.x1, ...), custom_call_target="tpu_custom_call" | custom-call | tf_op jit(solution)/shard_map/pallas_call | solution.py:619
Async XLA Ops:
  0.0 7.3 %copy-start.1 = (s32[8,8,128]{2,1,0:T(8,128)S(1)}, s32[8,8,128]{2,1,0:T(8,128)}, u32[]{:S(2)}) copy-start(s32[8,8,128]{2,1,0:T(8,128)} %param.3) | copy-start | bytes 98308
  2.1 7.5 %collective-permute-start = (f32[13,8,128]{2,1,0:T(8,128)}, f32[13,8,128]{2,1,0:T(8,128)S(1)}, u32[]{:S(2)}, u32[]{:S(2)}) collective-permute-start(f32[13,8,128]{2,1,0:T(8,128)} %get-tuple-element.19), channel_id=1, source_target_pairs={{0,1},{1,2},{2,3},{3,0},{4,5},{5,6},{6,7},{7,4},{8,9},{9,10},{10,1... | collective-permute-start | bytes 159752 | tf_op jit(solution)/shard_map/ppermute | solution.py:631
  5.2 4.9 %collective-permute-start.1 = (f32[13,8,128]{2,1,0:T(8,128)}, f32[13,8,128]{2,1,0:T(8,128)S(1)}, u32[]{:S(2)}, u32[]{:S(2)}) collective-permute-start(f32[13,8,128]{2,1,0:T(8,128)} %get-tuple-element.20), channel_id=1, source_target_pairs={{0,3},{1,0},{2,1},{3,2},{4,7},{5,4},{6,5},{7,6},{8,11},{9,8},{10,9... | collective-permute-start | bytes 159752 | tf_op jit(solution)/shard_map/ppermute | solution.py:631
  7.3 1.0 %copy-start = (f32[4,3,8,8,128]{4,3,2,1,0:T(8,128)S(1)}, f32[4,3,8,8,128]{4,3,2,1,0:T(8,128)}, u32[]{:S(2)}) copy-start(f32[4,3,8,8,128]{4,3,2,1,0:T(8,128)} %param.2) | copy-start | bytes 1179652
  10.5 10.8 %collective-permute-start.2 = (f32[20,8,640]{2,1,0:T(8,128)S(1)}, f32[20,8,640]{2,1,0:T(8,128)S(1)}, u32[]{:S(2)}, u32[]{:S(2)}) collective-permute-start(f32[20,8,640]{2,1,0:T(8,128)S(1)} %get-tuple-element.22), channel_id=1, source_target_pairs={{0,4},{4,8},{8,12},{12,16},{16,20},{20,24},{24,28},{28,0},{1,5},{5... | collective-permute-start | bytes 1228808 | tf_op jit(solution)/shard_map/ppermute | solution.py:631
  10.6 10.8 %collective-permute-start.3 = (f32[20,8,640]{2,1,0:T(8,128)S(1)}, f32[20,8,640]{2,1,0:T(8,128)S(1)}, u32[]{:S(2)}, u32[]{:S(2)}) collective-permute-start(f32[20,8,640]{2,1,0:T(8,128)S(1)} %get-tuple-element.23), channel_id=1, source_target_pairs={{0,28},{4,0},{8,4},{12,8},{16,12},{20,16},{24,20},{28,24},{1,29},{... | collective-permute-start | bytes 1228808 | tf_op jit(solution)/shard_map/ppermute | solution.py:631
  26.0 15.7 %all-to-all-start = ((f32[32,1,1664]{2,1,0:T(1,128)}), f32[32,1,1664]{2,1,0:T(1,128)S(1)}, u32[]{:S(2)}, u32[]{:S(2)}) async-start(f32[32,1,1664]{2,1,0:T(1,128)} %get-tuple-element.24), calls=%async_computation | async-start | bytes 425984 | tf_op jit(solution)/shard_map/all_to_all | solution.py:671
  32.2 5.7 %collective-permute-start.4 = (f32[9,8,256]{2,1,0:T(8,128)S(1)}, f32[9,8,256]{2,1,0:T(8,128)S(1)}, u32[]{:S(2)}, u32[]{:S(2)}) collective-permute-start(f32[9,8,256]{2,1,0:T(8,128)S(1)} %get-tuple-element.25), channel_id=1, source_target_pairs={{0,4},{4,8},{8,12},{12,16},{16,20},{20,24},{24,28},{28,0},{1,5},{5... | collective-permute-start | bytes 221192 | tf_op jit(solution)/shard_map/ppermute | solution.py:631
  32.5 5.4 %collective-permute-start.5 = (f32[9,8,256]{2,1,0:T(8,128)S(1)}, f32[9,8,256]{2,1,0:T(8,128)S(1)}, u32[]{:S(2)}, u32[]{:S(2)}) collective-permute-start(f32[9,8,256]{2,1,0:T(8,128)S(1)} %get-tuple-element.26), channel_id=1, source_target_pairs={{0,28},{4,0},{8,4},{12,8},{16,12},{20,16},{24,20},{28,24},{1,29},{... | collective-permute-start | bytes 221192 | tf_op jit(solution)/shard_map/ppermute | solution.py:631

commit v8 on v7

--- a/solution.py
+++ b/solution.py
@@ -207,27 +207,15 @@
     return ref[pl.ds(group * 64 + x, 8, stride=8), :]
 
 
-def coeff_rows(m_ref, x):
-    return jnp.where(rows_of(m_ref, 0, x) == 1, 1.0, 0.05).astype(F32)
-
-
-def edge_kernel(f_hbm, m_hbm, left_ref, right_ref, f_ref, m_ref, sems):
-    step = f_ref.shape[0] // VEC
-    copies = [pltpu.make_async_copy(f_hbm.at[pl.ds(step * v, step)], f_ref.at[pl.ds(step * v, step)], sems.at[v]) for v in range(VEC)]
-    copies.append(pltpu.make_async_copy(m_hbm, m_ref, sems.at[VEC]))
-    for copy in copies:
-        copy.start()
-    for v in range(VEC):
-        copies[v].wait()
-        for x in range(BX):
+def edge_kernel(f_ref, left_ref, right_ref):
+    for x in range(BX):
+        for v in range(VEC):
             for c in range(COMP):
                 val = rows_of(f_ref, v * COMP + c, x)
                 lanes = pl.ds((x // 4) * 64 + 16 * v, 16)
                 left_ref[c * 4 + x % 4, :, lanes] = val[:, :RIM]
                 right_ref[c * 4 + x % 4, :, lanes] = val[:, BY - RIM :]
-    copies[VEC].wait()
-    for x in range(BX):
-        val = coeff_rows(m_ref, x)
+        val = rows_of(f_ref, VEC * COMP, x)
         left_ref[12, :, pl.ds(16 * x, 16)] = val[:, :RIM]
         right_ref[12, :, pl.ds(16 * x, 16)] = val[:, BY - RIM :]
 
@@ -237,7 +225,7 @@
     return base + x // 5, 128 * (x % 5), base + piece // 5, 128 * (piece % 5) + 32 * (x % 4)
 
 
-def place_kernel(f_ref, m_ref, own_ref):
+def place_kernel(f_ref, own_ref):
     def put(row, lane, piece_row, piece_lane, val):
         own_ref[row, :, pl.ds(lane + LEFT, 128 - LEFT)] = val[:, : 128 - LEFT]
         own_ref[piece_row, :, pl.ds(piece_lane, BY - PIECE)] = val[:, PIECE:]
@@ -246,7 +234,7 @@
         for c in range(COMP):
             for v in range(VEC):
                 put(BX * c + x, 128 * v, BX * c + x, 512 + 32 * v, rows_of(f_ref, v * COMP + c, x))
-        put(*at_coeff(COMP * BX, x), coeff_rows(m_ref, x))
+        put(*at_coeff(COMP * BX, x), rows_of(f_ref, VEC * COMP, x))
 
 
 def join_kernel(gy, placed_ref, l_ref, r_ref, own_ref, left_ref, right_ref):
@@ -631,22 +619,17 @@
         return lax.ppermute(value, axis, [(i, (i + step) % size) for i in range(size)])
 
     f = right_side.reshape(VEC * COMP * NZ * BX, BY)
-    m = material.reshape(NZ * BX, BY)
+    rows = f.shape[0]
+    m = jnp.pad(material.reshape(NZ * BX, BY), ((rows, 0), (0, 0)))
+    coeff = jnp.where(m == 1, 1.0, 0.05).astype(F32)
+    f = jnp.where(iota((rows + NZ * BX, BY), 0) < rows, jnp.pad(f, ((0, NZ * BX), (0, 0))), coeff)
     edge = (13, 8, 128)
-    hbm, vmem = pl.BlockSpec(memory_space=pltpu.HBM), pl.BlockSpec(memory_space=pltpu.VMEM)
-    to_left, to_right = pl.pallas_call(
-        edge_kernel,
-        out_shape=[jax.ShapeDtypeStruct(s, F32) for s in (edge, edge)],
-        in_specs=[hbm] * 2,
-        out_specs=[vmem] * 2,
-        scratch_shapes=[pltpu.VMEM(f.shape, F32), pltpu.VMEM(m.shape, jnp.int32), pltpu.SemaphoreType.DMA((VEC + 1,))],
-        compiler_params=pltpu.CompilerParams(vmem_limit_bytes=65126 * 1024),
-    )(f, m)
+    to_left, to_right = call(edge_kernel, [edge, edge], [], f)
     right = ring(to_left, "gy", gy, -1)
     left = ring(to_right, "gy", gy, 1)
     side = (COMP * FX + 2, 8, L0)
     whole = (COMP * BX + 2, 8, L0)
-    (own,) = call(place_kernel, [whole], [], f, m)
+    (own,) = call(place_kernel, [whole], [], f)
     own, to_left, to_right = call(functools.partial(join_kernel, gy), [whole, side, side], [], own, left, right)
     right = ring(to_left, "gx", gx, -1)
     left = ring(to_right, "gx", gx, 1)

time: 47.2 us -> 46.3 us (0.981)
  Pallas kernels: 12.7 us -> 10.8 us
  other arithmetic: 0 us -> 1.18 us
  local copies, waits for them, and re-layouts: 1 us -> 0 us
  waiting for transfers between devices: 16.5 us -> 17.3 us
    pallas_call x1 -> x0, Pallas kernels: 2.12 us -> none  [per_device(): pl.pallas_call(edge_kernel, out_shape=[jax.ShapeDtypeStruct(s, F32) for s...]
    select_n x0 -> x1, other arithmetic: none -> 1.17 us  [per_device(): jnp.where(iota((rows + NZ * BX, BY), 0) < rows, jnp.pad(f, ((0, NZ * BX),...]
    unnamed x4 -> x0, local copies, waits for them, and re-layouts: 1 us -> none
    ppermute x6, waiting for transfers between devices: 12.7 us -> 13.5 us  [ring(): lax.ppermute(value, axis, [(i, (i + step) % size) for i in range(size)])]
    pallas_call x4 -> x5, Pallas kernels: 10.5 us -> 10.8 us  [call(): pl.pallas_call(kernel, out_shape=shapes, in_specs=[vmem] * len(args), out...]
where the time goes in v8:
time: 46.3 us; the launch traced here: 46 us
  waiting for transfers between devices  17.3 us (37%)
  starting transfers between devices  16.7 us (36%)
  Pallas kernels  10.8 us (23%)
  other arithmetic  1.18 us (3%)
    ppermute x6, waiting for transfers between devices, ring(): lax.ppermute(value, axis, [(i, (i + step) % size) for i in range(size)])  13.5 us
    pallas_call x5, Pallas kernels, call(): pl.pallas_call(kernel, out_shape=shapes, in_specs=[vmem] * len(args), out...  10.8 us
    ppermute x6, starting transfers between devices, ring(): lax.ppermute(value, axis, [(i, (i + step) % size) for i in range(size)])  10.6 us
    all_to_all x1, starting transfers between devices, per_device(): got = lax.all_to_all(pay, ('gx', 'gy'), 0, 0)  6.14 us
    all_to_all x1, waiting for transfers between devices, per_device(): got = lax.all_to_all(pay, ('gx', 'gy'), 0, 0)  3.82 us
    select_n x1, other arithmetic, per_device(): jnp.where(iota((rows + NZ * BX, BY), 0) < rows, jnp.pad(f, ((0, NZ * BX),...  1.17 us
  transfers between devices with their start and end apart: 7, of which 5 were waited for; matrix products, arithmetic and copies ran while one was open for 0% of the time, Pallas kernels for 1%

profile of v8, /device:TPU:0, one launch (start us, length us, event | category | flops | bytes accessed | tf_op | source)
XLA Modules:
  0.0 46.0 jit_solution(8475596201264365582)
XLA Ops:
  0.0 1.2 %select_select_fusion.f_ref = f32[832,128]{1,0:T(8,128)S(1)} fusion(f32[768,128]{1,0:T(8,128)} %bitcast.3, s32[64,128]{1,0:T(8,128)} %bitcast.4, pred[832]{0:T(1024)(128)(4,1)S(1)} %iota_compare_fusion), kind=kLoop, calls=%fused_computation | loop fusion | flops 319488 | bytes 852800 | tf_op jit(solution)/shard_map/jit(_where)/select_n | solution.py:625
  1.2 0.3 shard_map.29
  1.5 3.1 %collective-permute-start = (f32[13,8,128]{2,1,0:T(8,128)S(1)}, f32[13,8,128]{2,1,0:T(8,128)S(1)}, u32[]{:S(2)}, u32[]{:S(2)}) collective-permute-start(f32[13,8,128]{2,1,0:T(8,128)S(1)} %get-tuple-element.19), channel_id=1, source_target_pairs={{0,1},{1,2},{2,3},{3,0},{4,5},{5,6},{6,7},{7,4},{8,9},{9,10},{10,1... | collective-permute-start | bytes 159752 | tf_op jit(solution)/shard_map/ppermute | solution.py:619
  4.5 2.1 %collective-permute-start.1 = (f32[13,8,128]{2,1,0:T(8,128)S(1)}, f32[13,8,128]{2,1,0:T(8,128)S(1)}, u32[]{:S(2)}, u32[]{:S(2)}) collective-permute-start(f32[13,8,128]{2,1,0:T(8,128)S(1)} %get-tuple-element.20), channel_id=1, source_target_pairs={{0,3},{1,0},{2,1},{3,2},{4,7},{5,4},{6,5},{7,6},{8,11},{9,8},{10,9... | collective-permute-start | bytes 159752 | tf_op jit(solution)/shard_map/ppermute | solution.py:619
  6.6 0.3 shard_map.28.placed_ref
  6.9 1.8 %collective-permute-done.l_ref = f32[13,8,128]{2,1,0:T(8,128)S(1)} collective-permute-done((f32[13,8,128]{2,1,0:T(8,128)S(1)}, f32[13,8,128]{2,1,0:T(8,128)S(1)}, u32[]{:S(2)}, u32[]{:S(2)}) %collective-permute-start) | collective-permute-done | bytes 53280 | tf_op jit(solution)/shard_map/ppermute | solution.py:619
  8.7 0.5 %collective-permute-done.1.r_ref = f32[13,8,128]{2,1,0:T(8,128)S(1)} collective-permute-done((f32[13,8,128]{2,1,0:T(8,128)S(1)}, f32[13,8,128]{2,1,0:T(8,128)S(1)}, u32[]{:S(2)}, u32[]{:S(2)}) %collective-permute-start.1) | collective-permute-done | bytes 53280 | tf_op jit(solution)/shard_map/ppermute | solution.py:619
  9.2 0.4 shard_map.30
  9.6 0.1 collective-permute-start.2
  9.7 2.6 %collective-permute-start.3 = (f32[20,8,640]{2,1,0:T(8,128)S(1)}, f32[20,8,640]{2,1,0:T(8,128)S(1)}, u32[]{:S(2)}, u32[]{:S(2)}) collective-permute-start(f32[20,8,640]{2,1,0:T(8,128)S(1)} %get-tuple-element.23), channel_id=1, source_target_pairs={{0,28},{4,0},{8,4},{12,8},{16,12},{20,16},{24,20},{28,24},{1,29},{... | collective-permute-start | bytes 1228808 | tf_op jit(solution)/shard_map/ppermute | solution.py:619
  12.3 8.1 %collective-permute-done.2.l_ref = f32[20,8,640]{2,1,0:T(8,128)S(1)} collective-permute-done((f32[20,8,640]{2,1,0:T(8,128)S(1)}, f32[20,8,640]{2,1,0:T(8,128)S(1)}, u32[]{:S(2)}, u32[]{:S(2)}) %collective-permute-start.2) | collective-permute-done | bytes 409632 | tf_op jit(solution)/shard_map/ppermute | solution.py:619
  20.4 0.0 collective-permute-done.3.r_ref
  20.4 4.7 %shard_map.31 = (f32[32,1,1664]{2,1,0:T(1,128)}, f32[9,8,256]{2,1,0:T(8,128)S(1)}, f32[9,8,256]{2,1,0:T(8,128)S(1)}, f32[3,10,8,640]{3,2,1,0:T(8,128)S(1)}, f32[...) custom-call(f32[26,8,640]{2,1,0:T(8,128)S(1)} %get-tuple-element.21., ...), custom_call_target="tpu_custom_call" | custom-call | tf_op jit(solution)/shard_map/pallas_call | solution.py:607
  25.1 6.1 %all-to-all-start = ((f32[32,1,1664]{2,1,0:T(1,128)}), f32[32,1,1664]{2,1,0:T(1,128)S(1)}, u32[]{:S(2)}, u32[]{:S(2)}) async-start(f32[32,1,1664]{2,1,0:T(1,128)} %get-tuple-element.24), calls=%async_computation | async-start | bytes 425984 | tf_op jit(solution)/shard_map/all_to_all | solution.py:654
  31.3 0.3 collective-permute-start.4
  31.6 2.4 %collective-permute-start.5 = (f32[9,8,256]{2,1,0:T(8,128)S(1)}, f32[9,8,256]{2,1,0:T(8,128)S(1)}, u32[]{:S(2)}, u32[]{:S(2)}) collective-permute-start(f32[9,8,256]{2,1,0:T(8,128)S(1)} %get-tuple-element.26), channel_id=1, source_target_pairs={{0,28},{4,0},{8,4},{12,8},{16,12},{20,16},{24,20},{28,24},{1,29},{... | collective-permute-start | bytes 221192 | tf_op jit(solution)/shard_map/ppermute | solution.py:619
  34.0 3.0 %collective-permute-done.4.l_ref = f32[9,8,256]{2,1,0:T(8,128)S(1)} collective-permute-done((f32[9,8,256]{2,1,0:T(8,128)S(1)}, f32[9,8,256]{2,1,0:T(8,128)S(1)}, u32[]{:S(2)}, u32[]{:S(2)}) %collective-permute-start.4) | collective-permute-done | bytes 73760 | tf_op jit(solution)/shard_map/ppermute | solution.py:619
  37.0 0.0 collective-permute-done.5.r_ref
  37.0 3.8 %all-to-all-done.got_ref = f32[32,1,1664]{2,1,0:T(1,128)S(1)} async-done(((f32[32,1,1664]{2,1,0:T(1,128)}), f32[32,1,1664]{2,1,0:T(1,128)S(1)}, u32[]{:S(2)}, u32[]{:S(2)}) %all-to-all-start) | async-done | bytes 213024 | tf_op jit(solution)/shard_map/all_to_all | solution.py:654
  40.9 5.2 %shard_map.32 = f32[768,128]{1,0:T(8,128)} custom-call(f32[32,1,1664]{2,1,0:T(1,128)S(1)} %all-to-all-done.got_ref, f32[9,8,256]{2,1,0:T(8,128)S(1)} %collective-permute-done.4.l_ref, f32[9,8,256]{2,1,0:T(8,128)S(1)} %collective-permute-done.5.r_ref, f32[3,10,8,640]{3,2,1,0:T(8,128)S(1)} %get-tuple-element.27.x1, ...), custom_call_target="tpu_custom_call" | custom-call | tf_op jit(solution)/shard_map/pallas_call | solution.py:607
  (1 shorter events, 0.0 us)
Async XLA Ops:
  1.5 7.3 %collective-permute-start = (f32[13,8,128]{2,1,0:T(8,128)S(1)}, f32[13,8,128]{2,1,0:T(8,128)S(1)}, u32[]{:S(2)}, u32[]{:S(2)}) collective-permute-start(f32[13,8,128]{2,1,0:T(8,128)S(1)} %get-tuple-element.19), channel_id=1, source_target_pairs={{0,1},{1,2},{2,3},{3,0},{4,5},{5,6},{6,7},{7,4},{8,9},{9,10},{10,1... | collective-permute-start | bytes 159752 | tf_op jit(solution)/shard_map/ppermute | solution.py:619
  4.5 4.7 %collective-permute-start.1 = (f32[13,8,128]{2,1,0:T(8,128)S(1)}, f32[13,8,128]{2,1,0:T(8,128)S(1)}, u32[]{:S(2)}, u32[]{:S(2)}) collective-permute-start(f32[13,8,128]{2,1,0:T(8,128)S(1)} %get-tuple-element.20), channel_id=1, source_target_pairs={{0,3},{1,0},{2,1},{3,2},{4,7},{5,4},{6,5},{7,6},{8,11},{9,8},{10,9... | collective-permute-start | bytes 159752 | tf_op jit(solution)/shard_map/ppermute | solution.py:619
  9.6 10.8 %collective-permute-start.2 = (f32[20,8,640]{2,1,0:T(8,128)S(1)}, f32[20,8,640]{2,1,0:T(8,128)S(1)}, u32[]{:S(2)}, u32[]{:S(2)}) collective-permute-start(f32[20,8,640]{2,1,0:T(8,128)S(1)} %get-tuple-element.22), channel_id=1, source_target_pairs={{0,4},{4,8},{8,12},{12,16},{16,20},{20,24},{24,28},{28,0},{1,5},{5... | collective-permute-start | bytes 1228808 | tf_op jit(solution)/shard_map/ppermute | solution.py:619
  9.7 10.8 %collective-permute-start.3 = (f32[20,8,640]{2,1,0:T(8,128)S(1)}, f32[20,8,640]{2,1,0:T(8,128)S(1)}, u32[]{:S(2)}, u32[]{:S(2)}) collective-permute-start(f32[20,8,640]{2,1,0:T(8,128)S(1)} %get-tuple-element.23), channel_id=1, source_target_pairs={{0,28},{4,0},{8,4},{12,8},{16,12},{20,16},{24,20},{28,24},{1,29},{... | collective-permute-start | bytes 1228808 | tf_op jit(solution)/shard_map/ppermute | solution.py:619
  25.1 15.7 %all-to-all-start = ((f32[32,1,1664]{2,1,0:T(1,128)}), f32[32,1,1664]{2,1,0:T(1,128)S(1)}, u32[]{:S(2)}, u32[]{:S(2)}) async-start(f32[32,1,1664]{2,1,0:T(1,128)} %get-tuple-element.24), calls=%async_computation | async-start | bytes 425984 | tf_op jit(solution)/shard_map/all_to_all | solution.py:654
  31.3 5.7 %collective-permute-start.4 = (f32[9,8,256]{2,1,0:T(8,128)S(1)}, f32[9,8,256]{2,1,0:T(8,128)S(1)}, u32[]{:S(2)}, u32[]{:S(2)}) collective-permute-start(f32[9,8,256]{2,1,0:T(8,128)S(1)} %get-tuple-element.25), channel_id=1, source_target_pairs={{0,4},{4,8},{8,12},{12,16},{16,20},{20,24},{24,28},{28,0},{1,5},{5... | collective-permute-start | bytes 221192 | tf_op jit(solution)/shard_map/ppermute | solution.py:619
  31.6 5.4 %collective-permute-start.5 = (f32[9,8,256]{2,1,0:T(8,128)S(1)}, f32[9,8,256]{2,1,0:T(8,128)S(1)}, u32[]{:S(2)}, u32[]{:S(2)}) collective-permute-start(f32[9,8,256]{2,1,0:T(8,128)S(1)} %get-tuple-element.26), channel_id=1, source_target_pairs={{0,28},{4,0},{8,4},{12,8},{16,12},{20,16},{24,20},{28,24},{1,29},{... | collective-permute-start | bytes 221192 | tf_op jit(solution)/shard_map/ppermute | solution.py:619

commit v9 on v8

--- a/solution.py
+++ b/solution.py
@@ -304,7 +304,7 @@
                 for tile, kind in enumerate(a.kinds):
                     x1[c, p + FX, :, a.lanes(tile)] = gain[kind] * plane[:, 128 * tile : 128 * tile + 128]
 
-        each(low, high, 4, body)
+        each(low, high, 8, body)
 
     start(-FX, 0, lambda c, p: l_ref[c * FX + p + FX])
     start(0, BX, lambda c, p: own_ref[BX * c + p])
@@ -465,7 +465,7 @@
             x1c[c, p] = val
             ua[c, p + 2] = val
 
-    each(0, nx2, 8, start2)
+    each(0, nx2, 16, start2)
 
     def sweep2(src, dst):
         def write(c, p, tile, lanes, d):

time: 46.3 us -> 45.5 us (0.983)
  Pallas kernels: 10.8 us -> 10.1 us
    pallas_call x5, Pallas kernels: 10.8 us -> 10.1 us  [call(): pl.pallas_call(kernel, out_shape=shapes, in_specs=[vmem] * len(args), out...]
where the time goes in v9:
time: 45.5 us; the launch traced here: 45.3 us
  waiting for transfers between devices  17.3 us (38%)
  starting transfers between devices  16.7 us (37%)
  Pallas kernels  10.1 us (22%)
  other arithmetic  1.18 us (3%)
    ppermute x6, waiting for transfers between devices, ring(): lax.ppermute(value, axis, [(i, (i + step) % size) for i in range(size)])  13.5 us
    ppermute x6, starting transfers between devices, ring(): lax.ppermute(value, axis, [(i, (i + step) % size) for i in range(size)])  10.6 us
    pallas_call x5, Pallas kernels, call(): pl.pallas_call(kernel, out_shape=shapes, in_specs=[vmem] * len(args), out...  10.1 us
    all_to_all x1, starting transfers between devices, per_device(): got = lax.all_to_all(pay, ('gx', 'gy'), 0, 0)  6.15 us
    all_to_all x1, waiting for transfers between devices, per_device(): got = lax.all_to_all(pay, ('gx', 'gy'), 0, 0)  3.82 us
    select_n x1, other arithmetic, per_device(): jnp.where(iota((rows + NZ * BX, BY), 0) < rows, jnp.pad(f, ((0, NZ * BX),...  1.17 us
  transfers between devices with their start and end apart: 7, of which 5 were waited for; matrix products, arithmetic and copies ran while one was open for 0% of the time, Pallas kernels for 1%

profile of v9, /device:TPU:0, one launch (start us, length us, event | category | flops | bytes accessed | tf_op | source)
XLA Modules:
  0.0 45.3 jit_solution(17366405120959189801)
XLA Ops:
  0.0 1.2 %select_select_fusion.f_ref = f32[832,128]{1,0:T(8,128)S(1)} fusion(f32[768,128]{1,0:T(8,128)} %bitcast.3, s32[64,128]{1,0:T(8,128)} %bitcast.4, pred[832]{0:T(1024)(128)(4,1)S(1)} %iota_compare_fusion), kind=kLoop, calls=%fused_computation | loop fusion | flops 319488 | bytes 852800 | tf_op jit(solution)/shard_map/jit(_where)/select_n | solution.py:625
  1.2 0.3 shard_map.29
  1.5 3.1 %collective-permute-start = (f32[13,8,128]{2,1,0:T(8,128)S(1)}, f32[13,8,128]{2,1,0:T(8,128)S(1)}, u32[]{:S(2)}, u32[]{:S(2)}) collective-permute-start(f32[13,8,128]{2,1,0:T(8,128)S(1)} %get-tuple-element.19), channel_id=1, source_target_pairs={{0,1},{1,2},{2,3},{3,0},{4,5},{5,6},{6,7},{7,4},{8,9},{9,10},{10,1... | collective-permute-start | bytes 159752 | tf_op jit(solution)/shard_map/ppermute | solution.py:619
  4.5 2.1 %collective-permute-start.1 = (f32[13,8,128]{2,1,0:T(8,128)S(1)}, f32[13,8,128]{2,1,0:T(8,128)S(1)}, u32[]{:S(2)}, u32[]{:S(2)}) collective-permute-start(f32[13,8,128]{2,1,0:T(8,128)S(1)} %get-tuple-element.20), channel_id=1, source_target_pairs={{0,3},{1,0},{2,1},{3,2},{4,7},{5,4},{6,5},{7,6},{8,11},{9,8},{10,9... | collective-permute-start | bytes 159752 | tf_op jit(solution)/shard_map/ppermute | solution.py:619
  6.6 0.3 shard_map.28.placed_ref
  6.9 1.8 %collective-permute-done.l_ref = f32[13,8,128]{2,1,0:T(8,128)S(1)} collective-permute-done((f32[13,8,128]{2,1,0:T(8,128)S(1)}, f32[13,8,128]{2,1,0:T(8,128)S(1)}, u32[]{:S(2)}, u32[]{:S(2)}) %collective-permute-start) | collective-permute-done | bytes 53280 | tf_op jit(solution)/shard_map/ppermute | solution.py:619
  8.7 0.5 %collective-permute-done.1.r_ref = f32[13,8,128]{2,1,0:T(8,128)S(1)} collective-permute-done((f32[13,8,128]{2,1,0:T(8,128)S(1)}, f32[13,8,128]{2,1,0:T(8,128)S(1)}, u32[]{:S(2)}, u32[]{:S(2)}) %collective-permute-start.1) | collective-permute-done | bytes 53280 | tf_op jit(solution)/shard_map/ppermute | solution.py:619
  9.2 0.4 shard_map.30
  9.6 0.1 collective-permute-start.2
  9.7 2.6 %collective-permute-start.3 = (f32[20,8,640]{2,1,0:T(8,128)S(1)}, f32[20,8,640]{2,1,0:T(8,128)S(1)}, u32[]{:S(2)}, u32[]{:S(2)}) collective-permute-start(f32[20,8,640]{2,1,0:T(8,128)S(1)} %get-tuple-element.23), channel_id=1, source_target_pairs={{0,28},{4,0},{8,4},{12,8},{16,12},{20,16},{24,20},{28,24},{1,29},{... | collective-permute-start | bytes 1228808 | tf_op jit(solution)/shard_map/ppermute | solution.py:619
  12.3 8.1 %collective-permute-done.2.l_ref = f32[20,8,640]{2,1,0:T(8,128)S(1)} collective-permute-done((f32[20,8,640]{2,1,0:T(8,128)S(1)}, f32[20,8,640]{2,1,0:T(8,128)S(1)}, u32[]{:S(2)}, u32[]{:S(2)}) %collective-permute-start.2) | collective-permute-done | bytes 409632 | tf_op jit(solution)/shard_map/ppermute | solution.py:619
  20.4 0.0 collective-permute-done.3.r_ref
  20.4 4.2 %shard_map.31 = (f32[32,1,1664]{2,1,0:T(1,128)}, f32[9,8,256]{2,1,0:T(8,128)S(1)}, f32[9,8,256]{2,1,0:T(8,128)S(1)}, f32[3,10,8,640]{3,2,1,0:T(8,128)S(1)}, f32[...) custom-call(f32[26,8,640]{2,1,0:T(8,128)S(1)} %get-tuple-element.21., ...), custom_call_target="tpu_custom_call" | custom-call | tf_op jit(solution)/shard_map/pallas_call | solution.py:607
  24.6 6.1 %all-to-all-start = ((f32[32,1,1664]{2,1,0:T(1,128)}), f32[32,1,1664]{2,1,0:T(1,128)S(1)}, u32[]{:S(2)}, u32[]{:S(2)}) async-start(f32[32,1,1664]{2,1,0:T(1,128)} %get-tuple-element.24), calls=%async_computation | async-start | bytes 425984 | tf_op jit(solution)/shard_map/all_to_all | solution.py:654
  30.8 0.3 collective-permute-start.4
  31.1 2.4 %collective-permute-start.5 = (f32[9,8,256]{2,1,0:T(8,128)S(1)}, f32[9,8,256]{2,1,0:T(8,128)S(1)}, u32[]{:S(2)}, u32[]{:S(2)}) collective-permute-start(f32[9,8,256]{2,1,0:T(8,128)S(1)} %get-tuple-element.26), channel_id=1, source_target_pairs={{0,28},{4,0},{8,4},{12,8},{16,12},{20,16},{24,20},{28,24},{1,29},{... | collective-permute-start | bytes 221192 | tf_op jit(solution)/shard_map/ppermute | solution.py:619
  33.5 3.0 %collective-permute-done.4.l_ref = f32[9,8,256]{2,1,0:T(8,128)S(1)} collective-permute-done((f32[9,8,256]{2,1,0:T(8,128)S(1)}, f32[9,8,256]{2,1,0:T(8,128)S(1)}, u32[]{:S(2)}, u32[]{:S(2)}) %collective-permute-start.4) | collective-permute-done | bytes 73760 | tf_op jit(solution)/shard_map/ppermute | solution.py:619
  36.5 0.0 collective-permute-done.5.r_ref
  36.5 3.8 %all-to-all-done.got_ref = f32[32,1,1664]{2,1,0:T(1,128)S(1)} async-done(((f32[32,1,1664]{2,1,0:T(1,128)}), f32[32,1,1664]{2,1,0:T(1,128)S(1)}, u32[]{:S(2)}, u32[]{:S(2)}) %all-to-all-start) | async-done | bytes 213024 | tf_op jit(solution)/shard_map/all_to_all | solution.py:654
  40.3 5.0 %shard_map.32 = f32[768,128]{1,0:T(8,128)} custom-call(f32[32,1,1664]{2,1,0:T(1,128)S(1)} %all-to-all-done.got_ref, f32[9,8,256]{2,1,0:T(8,128)S(1)} %collective-permute-done.4.l_ref, f32[9,8,256]{2,1,0:T(8,128)S(1)} %collective-permute-done.5.r_ref, f32[3,10,8,640]{3,2,1,0:T(8,128)S(1)} %get-tuple-element.27.x1, ...), custom_call_target="tpu_custom_call" | custom-call | tf_op jit(solution)/shard_map/pallas_call | solution.py:607
  (1 shorter events, 0.0 us)
Async XLA Ops:
  1.5 7.3 %collective-permute-start = (f32[13,8,128]{2,1,0:T(8,128)S(1)}, f32[13,8,128]{2,1,0:T(8,128)S(1)}, u32[]{:S(2)}, u32[]{:S(2)}) collective-permute-start(f32[13,8,128]{2,1,0:T(8,128)S(1)} %get-tuple-element.19), channel_id=1, source_target_pairs={{0,1},{1,2},{2,3},{3,0},{4,5},{5,6},{6,7},{7,4},{8,9},{9,10},{10,1... | collective-permute-start | bytes 159752 | tf_op jit(solution)/shard_map/ppermute | solution.py:619
  4.5 4.7 %collective-permute-start.1 = (f32[13,8,128]{2,1,0:T(8,128)S(1)}, f32[13,8,128]{2,1,0:T(8,128)S(1)}, u32[]{:S(2)}, u32[]{:S(2)}) collective-permute-start(f32[13,8,128]{2,1,0:T(8,128)S(1)} %get-tuple-element.20), channel_id=1, source_target_pairs={{0,3},{1,0},{2,1},{3,2},{4,7},{5,4},{6,5},{7,6},{8,11},{9,8},{10,9... | collective-permute-start | bytes 159752 | tf_op jit(solution)/shard_map/ppermute | solution.py:619
  9.6 10.8 %collective-permute-start.2 = (f32[20,8,640]{2,1,0:T(8,128)S(1)}, f32[20,8,640]{2,1,0:T(8,128)S(1)}, u32[]{:S(2)}, u32[]{:S(2)}) collective-permute-start(f32[20,8,640]{2,1,0:T(8,128)S(1)} %get-tuple-element.22), channel_id=1, source_target_pairs={{0,4},{4,8},{8,12},{12,16},{16,20},{20,24},{24,28},{28,0},{1,5},{5... | collective-permute-start | bytes 1228808 | tf_op jit(solution)/shard_map/ppermute | solution.py:619
  9.7 10.8 %collective-permute-start.3 = (f32[20,8,640]{2,1,0:T(8,128)S(1)}, f32[20,8,640]{2,1,0:T(8,128)S(1)}, u32[]{:S(2)}, u32[]{:S(2)}) collective-permute-start(f32[20,8,640]{2,1,0:T(8,128)S(1)} %get-tuple-element.23), channel_id=1, source_target_pairs={{0,28},{4,0},{8,4},{12,8},{16,12},{20,16},{24,20},{28,24},{1,29},{... | collective-permute-start | bytes 1228808 | tf_op jit(solution)/shard_map/ppermute | solution.py:619
  24.6 15.7 %all-to-all-start = ((f32[32,1,1664]{2,1,0:T(1,128)}), f32[32,1,1664]{2,1,0:T(1,128)S(1)}, u32[]{:S(2)}, u32[]{:S(2)}) async-start(f32[32,1,1664]{2,1,0:T(1,128)} %get-tuple-element.24), calls=%async_computation | async-start | bytes 425984 | tf_op jit(solution)/shard_map/all_to_all | solution.py:654
  30.8 5.7 %collective-permute-start.4 = (f32[9,8,256]{2,1,0:T(8,128)S(1)}, f32[9,8,256]{2,1,0:T(8,128)S(1)}, u32[]{:S(2)}, u32[]{:S(2)}) collective-permute-start(f32[9,8,256]{2,1,0:T(8,128)S(1)} %get-tuple-element.25), channel_id=1, source_target_pairs={{0,4},{4,8},{8,12},{12,16},{16,20},{20,24},{24,28},{28,0},{1,5},{5... | collective-permute-start | bytes 221192 | tf_op jit(solution)/shard_map/ppermute | solution.py:619
  31.1 5.4 %collective-permute-start.5 = (f32[9,8,256]{2,1,0:T(8,128)S(1)}, f32[9,8,256]{2,1,0:T(8,128)S(1)}, u32[]{:S(2)}, u32[]{:S(2)}) collective-permute-start(f32[9,8,256]{2,1,0:T(8,128)S(1)} %get-tuple-element.26), channel_id=1, source_target_pairs={{0,28},{4,0},{8,4},{12,8},{16,12},{20,16},{24,20},{28,24},{1,29},{... | collective-permute-start | bytes 221192 | tf_op jit(solution)/shard_map/ppermute | solution.py:619
